TPU v7x, 32 devices: a whole 2x2x4 slice. The times are simulated.
32 devices in a mesh: dp: 2 (over x), tile: 16 (over z, y, core).
Axes of the slice: x: 2, y: 2, z: 4, core: 2. Of those that a mesh axis runs over, the one named last changes fastest.
Arguments:
- inputs: bfloat16 [2, 256, 8, 8, 128], P('dp', 'tile'), may hold values from -6 to 6
- cotangent: bfloat16 [2, 256, 4, 4, 128], P('dp', 'tile'), may hold values from -6 to 6
- w_first: bfloat16 [1152, 128], replicated, may hold values from -0.1875 to 0.1875
- w_second: bfloat16 [1152, 128], replicated, may hold values from -0.1875 to 0.1875
- w_down: bfloat16 [512, 128], replicated, may hold values from -0.25 to 0.25
- edge_owner: int32 [256, 4], replicated, may hold values from 0 to 15, all different within a row; in each aligned block of 16 rows (0 to 15, 16 to 31, ...) at most 5 rows name the same one
- corner_owner: int32 [256, 4], replicated, may hold values from 0 to 15, all different within a row; in each aligned block of 16 rows (0 to 15, 16 to 31, ...) at most 5 rows name the same one
- neighbour_tile: int32 [256, 8], replicated, may hold values from 0 to 15
- seam_rotation: int32 [256, 8], replicated, may hold values from 0 to 3
Outputs:
- features: bfloat16 [2, 256, 4, 4, 128], P('dp', 'tile')
- input_grad: float32 [2, 256, 8, 8, 128], P('dp', 'tile')
- grad_first: float32 [1152, 128], P('dp')
- grad_second: float32 [1152, 128], P('dp')
- grad_down: float32 [512, 128], P('dp')
Inputs may be any that keep to these rules, and one draw needn't show every extreme that they name: `edge_owner`: the four devices of a row differ. Among the rows of the 16 tiles of one device no device is named more than 5 times, and some device exactly 5 times. `corner_owner`: as for edge_owner.
All inputs are finite; a program needn't handle non-finite values.
Results may differ from a plain program's by a relative error of at most 0.0085.
Values may be sent and summed in bfloat16 or wider, within the bound.
No kernel may reach another device: no remote copies, remote signals or barrier semaphores. Data moves between devices by JAX's collectives and lax.ppermute only.
A program may use at most 64 MiB of HBM per device.

v0:
```python
import functools
import jax
import jax.numpy as jnp
from jax import lax
from jax.experimental import pallas as pl
from jax.experimental.pallas import tpu as pltpu
from jax.sharding import PartitionSpec as P

F32, BF16, I32 = jnp.float32, jnp.bfloat16, jnp.int32
LANES = 128


class Sizes:
    def __init__(self, tiles, side, chan, devices, samples):
        self.tiles, self.side, self.chan = tiles, side, chan
        self.devices, self.samples = devices, samples
        self.slots = max(2, 4 * tiles // devices + 1)
        self.pair = -(-self.slots * (side + 1) // 16) * 16
        self.sent = devices * self.pair
        self.line = tiles * side
        self.pixels = side * self.line
        self.column = (side + 2) * tiles
        self.cells = 2 * self.line + 2 * self.column
        self.cells_up = -(-self.cells // LANES) * LANES
        self.tap_rows = 9 * chan // samples
        self.down_rows = 4 * chan // samples
        self.late = self.tap_rows
        self.early = self.tap_rows + self.down_rows
        self.chunk = -(-(self.early + self.late) // (16 * devices)) * 16


def iota(shape, dim):
    return lax.broadcasted_iota(I32, shape, dim)


def mm(a, b):
    return jnp.dot(a.astype(BF16), b.astype(BF16), preferred_element_type=F32)


def mm_t(a, b):
    return lax.dot_general(a, b, (((0,), (0,)), ((), ())), preferred_element_type=F32)


def flag(cond):
    return jnp.where(cond, 1.0, 0.0).astype(BF16)


def pick_rows(index, width):
    rows = index.shape[0]
    lane = iota((rows, LANES), 1)
    return jnp.concatenate([flag(index == lane + at) for at in range(0, width, LANES)], axis=1)


def pick_columns(index, height):
    shape = (height, index.shape[1])
    return flag(jnp.broadcast_to(index, shape) == iota(shape, 0))


def row_first(x):
    tiles, side, _, chan = x.shape
    x = x.astype(F32)
    return jnp.stack([x[:, r].reshape(tiles * side, chan) for r in range(side)], axis=0)


def sender_index(me, owners, local_ids, turns, z):
    requests = z.devices * z.tiles
    lane8 = iota((requests, 8), 1)
    matched = owners == me
    code = jnp.where(matched, local_ids * 16 + turns * 4 + (lane8 & 3) + 1, 0).astype(F32)
    found = jnp.where(matched, 1.0, 0.0)
    edge = lane8 < 4
    has_e = jnp.sum(jnp.where(edge, found, 0.0), axis=1, keepdims=True)
    has_c = jnp.sum(jnp.where(edge, 0.0, found), axis=1, keepdims=True)
    code_e = jnp.sum(jnp.where(edge, code, 0.0), axis=1, keepdims=True)
    code_c = jnp.sum(jnp.where(edge, 0.0, code), axis=1, keepdims=True)
    lane = iota((requests, LANES), 1)
    half = LANES // 2
    first = lane < half
    has = jnp.where(first, has_e, has_c)
    code = jnp.where(first, code_e, code_c)
    block = (z.devices, z.tiles, requests)
    own_block = (iota(block, 2) >= iota(block, 0) * z.tiles) & (
        iota(block, 2) < iota(block, 0) * z.tiles + iota(block, 1)
    )
    rank = mm(flag(own_block).reshape(requests, requests), has)
    placed = jnp.where((lane & (half - 1)).astype(F32) == rank, code, 0.0)
    group = (z.devices, requests)
    low = iota(group, 0) * z.tiles
    per_device = mm(flag((iota(group, 1) >= low) & (iota(group, 1) < low + z.tiles)), placed)
    spread = (z.devices, z.pair, z.devices)
    rows = mm(flag(iota(spread, 0) == iota(spread, 2)).reshape(z.sent, z.devices), per_device)
    cube = (z.devices, z.pair, LANES)
    at = iota(cube, 1).reshape(z.sent, LANES)
    lane = iota((z.sent, LANES), 1)
    edges = z.slots * z.side
    is_edge = at < edges
    slot = jnp.where(is_edge, lax.div(at, z.side), at - edges + half)
    wanted = (slot == lane) & (at < edges + z.slots)
    code = mm(jnp.where(wanted, rows, 0.0), jnp.ones((LANES, LANES), BF16)).astype(I32) - 1
    along = lax.rem(at, z.side)
    source, turn, towards = code >> 4, (code >> 2) & 3, code & 3
    end = z.side - 1
    i_edge = jnp.where(towards == 0, end, jnp.where(towards == 2, 0, along))
    j_edge = jnp.where(towards == 1, 0, jnp.where(towards == 3, end, along))
    i_corner = jnp.where((towards == 0) | (towards == 3), end, 0)
    j_corner = jnp.where(towards >= 2, end, 0)
    i = jnp.where(is_edge, i_edge, i_corner)
    j = jnp.where(is_edge, j_edge, j_corner)
    row = jnp.where(turn == 0, i, jnp.where(turn == 1, j, jnp.where(turn == 2, end - i, end - j)))
    col = jnp.where(turn == 0, j, jnp.where(turn == 1, end - i, jnp.where(turn == 2, end - j, i)))
    return jnp.where(code >= 0, row * z.line + source * z.side + col, -1)


def receiver_index(own_e, own_c, z):
    lane = iota((z.tiles, LANES), 1)
    lower = flag(iota((z.tiles, z.tiles), 1) < iota((z.tiles, z.tiles), 0))
    values = jnp.zeros((z.tiles, LANES), F32)
    for base, own in ((0, own_e), (8, own_c)):
        hits = [jnp.broadcast_to(own[:, k : k + 1], (z.tiles, LANES)) == lane for k in range(4)]
        named = sum(jnp.where(hit, 1.0, 0.0) for hit in hits)
        before = mm(lower, named)
        for k in range(4):
            rank = jnp.sum(jnp.where(hits[k], before, 0.0), axis=1, keepdims=True)
            values = jnp.where(lane == base + k, own[:, k : k + 1].astype(F32), values)
            values = jnp.where(lane == base + 4 + k, rank, values)
    ones = jnp.ones((LANES, LANES), BF16)

    def spread(tile, own_lane, is_edge, along):
        rows = tile.shape[0]
        lane = iota((rows, LANES), 1)
        here = mm(flag(tile[:, : z.tiles] == iota((rows, z.tiles), 1)), values)
        own = mm(jnp.where(lane == own_lane, here, 0.0), ones).astype(I32)
        rank = mm(jnp.where(lane == own_lane + 4, here, 0.0), ones).astype(I32)
        return own * z.pair + jnp.where(is_edge, rank * z.side + along, z.slots * z.side + rank)

    line = (z.tiles, z.side, LANES)
    tile = iota(line, 0).reshape(z.line, LANES)
    along = iota(line, 1).reshape(z.line, LANES)
    parts = [spread(tile, k, jnp.full(tile.shape, True), along) for k in (0, 2)]
    column = (z.side + 2, z.tiles, LANES)
    row = iota(column, 0).reshape(z.column, LANES)
    tile = iota(column, 1).reshape(z.column, LANES)
    is_edge = (row > 0) & (row <= z.side)
    for edge, top, bottom in ((3, 3, 2), (1, 0, 1)):
        own_lane = jnp.where(is_edge, edge, jnp.where(row == 0, 8 + top, 8 + bottom))
        parts.append(spread(tile, own_lane, is_edge, row - 1))
    parts.append(jnp.full((z.cells_up - z.cells, LANES), -1, I32))
    return jnp.concatenate(parts, axis=0)


def as_row(index):
    return jnp.transpose(index.astype(F32))[0:8].astype(I32)


def pack_kernel(z, me_ref, eo_ref, co_ref, ids_ref, turn_ref, x_ref, send_ref, col_ref, row_ref):
    owners = jnp.concatenate([eo_ref[...], co_ref[...]], axis=1)
    index = sender_index(me_ref[0], owners, ids_ref[...], turn_ref[...], z)
    pixels = row_first(x_ref[...]).reshape(z.pixels, z.chan)
    sent = mm(pick_rows(index, z.pixels), pixels)
    send_ref[...] = sent.astype(BF16).reshape(send_ref.shape)
    col_ref[...] = index
    row_ref[...] = as_row(index)


def side_kernel(
    z, me_ref, eo_ref, co_ref, cot_ref, wd_ref, w1_ref, w2_ref, col_ref, row_ref, back_ref, cot_out, t1_ref, t2_ref
):
    mine = pl.ds(me_ref[0] * z.tiles, z.tiles)
    index = receiver_index(eo_ref[mine, :], co_ref[mine, :], z)
    col_ref[...] = index
    row_ref[...] = as_row(index)
    chan, half = z.chan, z.side // 2
    for taps, out in ((w1_ref, t1_ref), (w2_ref, t2_ref)):
        for tap in range(9):
            rows = slice(tap * chan, (tap + 1) * chan)
            out[rows, :] = jnp.transpose(taps[rows, :].astype(F32)).astype(BF16)
    cot = cot_ref[...]
    cot_out[...] = cot
    part = half * z.tiles
    for p in range(2):
        for q in range(2):
            tap = wd_ref[(2 * p + q) * chan : (2 * p + q + 1) * chan, :]
            back = lax.dot_general(cot, tap, (((1,), (1,)), ((), ())), preferred_element_type=F32)
            for i in range(half):
                back_ref[pl.ds((2 * i + p) * z.line + q, part, stride=2), :] = back[i * part : (i + 1) * part]


def padded_columns(z, center, arrived, index, west_ref, east_ref, out_ref):
    rims = mm(pick_rows(index, z.sent), arrived)
    north, south = rims[: z.line], rims[z.line : 2 * z.line]
    at = 2 * z.line
    west_ref[pl.ds(0, z.column, stride=z.side), :] = rims[at : at + z.column]
    east_ref[pl.ds(z.side - 1, z.column, stride=z.side), :] = rims[at + z.column : at + 2 * z.column]
    shape = (z.column, z.side, z.chan)
    middle = jnp.concatenate([north, center, south], axis=0).reshape(shape)
    place = iota(shape, 1)
    flat = (z.column * z.side, z.chan)
    left = jnp.where(place == 0, west_ref[...].reshape(shape), pltpu.roll(middle, 1, 1))
    right = jnp.where(place == z.side - 1, east_ref[...].reshape(shape), pltpu.roll(middle, z.side - 1, 1))
    out_ref[:, : z.chan] = left.reshape(flat).astype(BF16)
    out_ref[:, z.chan : 2 * z.chan] = middle.reshape(flat).astype(BF16)
    out_ref[:, 2 * z.chan :] = right.reshape(flat).astype(BF16)


def conv(z, columns_ref, w_ref):
    total = None
    for p in range(3):
        part = jnp.dot(
            columns_ref[p * z.line : p * z.line + z.pixels, :],
            w_ref[3 * p * z.chan : 3 * (p + 1) * z.chan, :],
            preferred_element_type=F32,
        )
        total = part if total is None else total + part
    return total


def silu_and_slope(v):
    s = 1.0 / (1.0 + jnp.exp(-v))
    return v * s, s * (1.0 + v * (1.0 - s))


def first_kernel(
    z, got_ref, cell_ref, x_ref, w_ref, pix_ref, send_ref, hidden_ref, slope_ref, columns_ref, west_ref, east_ref
):
    center = row_first(x_ref[...]).reshape(z.pixels, z.chan)
    padded_columns(z, center, got_ref[...].reshape(z.sent, z.chan), cell_ref[...], west_ref, east_ref, columns_ref)
    hidden, slope = silu_and_slope(conv(z, columns_ref, w_ref))
    hidden = hidden.astype(BF16)
    send_ref[...] = mm(pick_rows(pix_ref[...], z.pixels), hidden).astype(BF16).reshape(send_ref.shape)
    hidden_ref[...] = hidden
    slope_ref[...] = slope


def adjoint(z, slope, turned_ref, slope_ref, wide_ref):
    chan = z.chan
    shape = (z.pixels // z.side, z.side, chan)
    cube = slope.reshape(shape)
    place = iota(shape, 1)
    zero = jnp.zeros((2 * z.line, 3 * chan), BF16)
    wide_ref[: 2 * z.line, :] = zero
    wide_ref[2 * z.line + z.pixels :, :] = zero
    inner = slice(2 * z.line, 2 * z.line + z.pixels)
    after = jnp.where(place == z.side - 1, 0.0, pltpu.roll(cube, z.side - 1, 1))
    before = jnp.where(place == 0, 0.0, pltpu.roll(cube, 1, 1))
    wide_ref[inner, :chan] = after.reshape(z.pixels, chan).astype(BF16)
    wide_ref[inner, chan : 2 * chan] = slope.astype(BF16)
    wide_ref[inner, 2 * chan :] = before.reshape(z.pixels, chan).astype(BF16)
    rows = (z.side + 2) * z.line
    total = None
    for p in range(3):
        part = jnp.dot(
            wide_ref[(2 - p) * z.line : (2 - p) * z.line + rows, :],
            turned_ref[3 * p * chan : 3 * (p + 1) * chan, :],
            preferred_element_type=F32,
        )
        total = part if total is None else total + part
    slope_ref[...] = slope
    blank = jnp.zeros((2 * z.tiles, chan), F32)
    sides = []
    for start, q in ((0, 0), (z.side - 1, 2)):
        line = slope_ref[pl.ds(start, z.side * z.tiles, stride=z.side), :]
        line = jnp.concatenate([blank, line, blank], axis=0).astype(BF16)
        side = None
        for p in range(3):
            part = jnp.dot(
                line[(2 - p) * z.tiles : (2 - p) * z.tiles + z.column],
                turned_ref[(3 * p + q) * chan : (3 * p + q + 1) * chan, :],
                preferred_element_type=F32,
            )
            side = part if side is None else side + part
        sides.append(side)
    spare = jnp.zeros((z.cells_up - z.cells, chan), F32)
    rims = jnp.concatenate([total[: z.line], total[rows - z.line :]] + sides + [spare], axis=0)
    return total[z.line : z.line + z.pixels], rims.astype(BF16)


def second_kernel(
    z, got_ref, cell_ref, cell_row_ref, hidden_ref, w_ref, turned_ref, back_ref,
    send_ref, inner_ref, slope_ref, out_ref, columns_ref, west_ref, east_ref, scratch_ref, wide_ref,
):
    center = hidden_ref[...].astype(F32)
    padded_columns(z, center, got_ref[...].reshape(z.sent, z.chan), cell_ref[...], west_ref, east_ref, columns_ref)
    hidden, slope = silu_and_slope(conv(z, columns_ref, w_ref))
    out_ref[...] = hidden.astype(BF16).astype(F32)
    slope = (back_ref[...] * slope).astype(BF16)
    slope_ref[...] = slope
    inner, rims = adjoint(z, slope.astype(F32), turned_ref, scratch_ref, wide_ref)
    inner_ref[...] = inner
    send_ref[...] = mm(pick_columns(cell_row_ref[0:1, :], z.sent), rims).astype(BF16).reshape(send_ref.shape)


def tap_products(z, columns_ref, slope, scale, total_ref):
    for p in range(3):
        part = mm_t(columns_ref[p * z.line : p * z.line + z.pixels, :], slope)
        total_ref[3 * p * z.chan : 3 * (p + 1) * z.chan, :] = part * scale


def early_kernel(
    z, scale, at_ref, columns_ref, slope_ref, hidden_ref, cot_ref, wd_ref,
    feature_ref, own_ref, other_ref, total_ref, down_ref, block_ref,
):
    chan, half = z.chan, z.side // 2
    part = half * z.tiles
    tap_products(z, columns_ref, slope_ref[...], scale, total_ref)
    for i in range(half):
        for p in range(2):
            for q in range(2):
                block_ref[i * part : (i + 1) * part, (2 * p + q) * chan : (2 * p + q + 1) * chan] = hidden_ref[
                    pl.ds((2 * i + p) * z.line + q, part, stride=2), :
                ].astype(BF16)
    block = block_ref[...]
    feature_ref[...] = jnp.dot(block, wd_ref[...], preferred_element_type=F32).astype(BF16)
    down_ref[...] = mm_t(block, cot_ref[...]) * scale
    sample = at_ref[0]
    for shift in range(z.samples):
        whose = lax.rem(sample + shift, z.samples)
        taps = total_ref[pl.ds(whose * z.tap_rows, z.tap_rows), :]
        down = down_ref[pl.ds(whose * z.down_rows, z.down_rows), :]
        if shift == 0:
            own_ref[: z.tap_rows, :] = taps
            own_ref[z.tap_rows :, :] = down
        else:
            other_ref[shift - 1, : z.tap_rows, :] = taps.astype(BF16)
            other_ref[shift - 1, z.tap_rows :, :] = down.astype(BF16)


def slope_kernel(
    z, scale, at_ref, got_ref, pix_row_ref, inner_ref, slope_in_ref, columns_ref, slope_ref, own_ref, other_ref, total_ref
):
    back = inner_ref[...] + mm(pick_columns(pix_row_ref[0:1, :], z.pixels), got_ref[...].reshape(z.sent, z.chan))
    slope = (back * slope_in_ref[...]).astype(BF16)
    slope_ref[...] = slope
    tap_products(z, columns_ref, slope, scale, total_ref)
    sample = at_ref[0]
    for shift in range(z.samples):
        whose = lax.rem(sample + shift, z.samples)
        taps = total_ref[pl.ds(whose * z.tap_rows, z.tap_rows), :]
        if shift == 0:
            own_ref[...] = taps
        else:
            other_ref[shift - 1] = taps.astype(BF16)


def last_kernel(z, slope_ref, turned_ref, cell_row_ref, send_ref, inner_ref, scratch_ref, wide_ref):
    inner, rims = adjoint(z, slope_ref[...].astype(F32), turned_ref, scratch_ref, wide_ref)
    inner_ref[...] = inner
    send_ref[...] = mm(pick_columns(cell_row_ref[0:1, :], z.sent), rims).astype(BF16).reshape(send_ref.shape)


def join_kernel(z, rim_ref, early_ref, early_got_ref, late_ref, late_got_ref, send_ref, total_ref):
    early, late = early_ref[...], late_ref[...]
    for k in range(z.samples - 1):
        early = early + early_got_ref[k].astype(F32)
        late = late + late_got_ref[k].astype(F32)
    total_ref[: z.early, :] = early
    total_ref[z.early : z.early + z.late, :] = late
    spare = z.devices * z.chunk - z.early - z.late
    if spare:
        total_ref[z.early + z.late :, :] = jnp.zeros((spare, z.chan), F32)
    send_ref[:, : z.pair, :] = rim_ref[...]
    send_ref[:, z.pair :, :] = total_ref[...].astype(BF16).reshape(z.devices, z.chunk, z.chan)


def sum_kernel(z, got_ref, out_ref):
    total = got_ref[0, z.pair :, :].astype(F32)
    for k in range(1, z.devices):
        total = total + got_ref[k, z.pair :, :].astype(F32)
    total = total.astype(BF16)
    for k in range(z.devices):
        out_ref[k] = total


def input_kernel(z, got_ref, pix_row_ref, inner_ref, out_ref):
    arrived = got_ref[:, : z.pair, :].reshape(z.sent, z.chan)
    total = inner_ref[...] + mm(pick_columns(pix_row_ref[0:1, :], z.pixels), arrived)
    for r in range(z.side):
        out_ref[:, r] = total[r * z.line : (r + 1) * z.line].reshape(z.tiles, z.side, z.chan)


def spread_kernel(z, got_ref, one_ref, two_ref, low_ref):
    total = got_ref[...].astype(F32).reshape(z.devices * z.chunk, z.chan)
    two_ref[...] = total[: z.tap_rows]
    low_ref[...] = total[z.tap_rows : z.early]
    one_ref[...] = total[z.early : z.early + z.late]


def vmem(*shape, dtype=F32):
    return pltpu.VMEM(shape, dtype)


def call(body, outs, scratch=(), scalars=0, name=None):
    def run(*operands):
        spec = pl.BlockSpec(memory_space=pltpu.VMEM)
        small = pl.BlockSpec(memory_space=pltpu.SMEM)
        return pl.pallas_call(
            body,
            out_shape=[jax.ShapeDtypeStruct(shape, dtype) for shape, dtype in outs],
            in_specs=[small] * scalars + [spec] * (len(operands) - scalars),
            out_specs=[spec] * len(outs),
            scratch_shapes=list(scratch),
            compiler_params=pltpu.CompilerParams(vmem_limit_bytes=40 * 1024 * 1024),
            name=name,
        )(*operands)

    return run


def exchange(x):
    return lax.all_to_all(x, "tile", split_axis=0, concat_axis=0, tiled=True)


def to_samples(others, samples):
    got = []
    for k in range(samples - 1):
        got.append(lax.ppermute(others[k], "dp", [(s, (s + k + 1) % samples) for s in range(samples)]))
    return jnp.stack(got) if samples > 2 else got[0][None]


def local(inputs, cotangent, w_first, w_second, w_down, edge_owner, corner_owner, neighbour_tile, seam_rotation):
    tiles_in, cot = inputs[0], cotangent[0]
    tiles, side, _, chan = tiles_in.shape
    z = Sizes(tiles, side, chan, lax.axis_size("tile"), lax.axis_size("dp"))
    scale = float(z.samples * z.devices * z.pixels) ** -0.5
    me = lax.axis_index("tile").astype(I32).reshape(1)
    sample = lax.axis_index("dp").astype(I32).reshape(1)
    half = side // 2
    down_pixels = half * half * tiles
    field = ((z.pixels, chan), F32)
    field16 = ((z.pixels, chan), BF16)
    columns = ((z.column * side, 3 * chan), BF16)
    sent = ((z.devices, z.pair, chan), BF16)
    wide = vmem((side + 4) * z.line, 3 * chan, dtype=BF16)
    side_columns = (vmem(z.column * side, chan), vmem(z.column * side, chan))
    flat = vmem(z.pixels, chan)
    taps = vmem(9 * chan, chan)
    bind = functools.partial

    send, pix_col, pix_row = call(
        bind(pack_kernel, z), [sent, ((z.sent, LANES), I32), ((8, z.sent), I32)], scalars=1, name="pack"
    )(me, edge_owner, corner_owner, neighbour_tile, seam_rotation, tiles_in)
    got = exchange(send)
    cot_rows = cot.transpose(1, 0, 2, 3).reshape(down_pixels, chan)
    cell_col, cell_row, back_second, cot_rows, turned_first, turned_second = call(
        bind(side_kernel, z),
        [
            ((z.cells_up, LANES), I32),
            ((8, z.cells_up), I32),
            field,
            ((down_pixels, chan), BF16),
            ((9 * chan, chan), BF16),
            ((9 * chan, chan), BF16),
        ],
        scalars=1,
        name="aside",
    )(me, edge_owner, corner_owner, cot_rows, w_down, w_first, w_second)
    send, hidden, slope_in, columns_first = call(
        bind(first_kernel, z), [sent, field16, field, columns], side_columns, name="first"
    )(got, cell_col, tiles_in, w_first, pix_col)
    got = exchange(send)
    send, inner, slope_second, hidden_second, columns_second = call(
        bind(second_kernel, z), [sent, field, field16, field, columns], side_columns + (flat, wide), name="second"
    )(got, cell_col, cell_row, hidden, w_second, turned_second, back_second)
    got = exchange(send)
    features, early_own, early_other = call(
        bind(early_kernel, z, scale),
        [((down_pixels, chan), BF16), ((z.early, chan), F32), ((z.samples - 1, z.early, chan), BF16)],
        (taps, vmem(4 * chan, chan), vmem(down_pixels, 4 * chan, dtype=BF16)),
        scalars=1,
        name="early",
    )(sample, columns_second, slope_second, hidden_second, cot_rows, w_down)
    features = features.reshape(half, tiles, half, chan).transpose(1, 0, 2, 3)
    early_got = to_samples(early_other, z.samples)
    slope_first, late_own, late_other = call(
        bind(slope_kernel, z, scale),
        [field16, ((z.late, chan), F32), ((z.samples - 1, z.late, chan), BF16)],
        (taps,),
        scalars=1,
        name="slope",
    )(sample, got, pix_row, inner, slope_in, columns_first)
    late_got = to_samples(late_other, z.samples)
    send, inner = call(bind(last_kernel, z), [sent, field], (flat, wide), name="last")(
        slope_first, turned_first, cell_row
    )
    (send,) = call(
        bind(join_kernel, z),
        [((z.devices, z.pair + z.chunk, chan), BF16)],
        (vmem(z.devices * z.chunk, chan),),
        name="join",
    )(send, early_own, early_got, late_own, late_got)
    got = exchange(send)
    (chunk,) = call(bind(sum_kernel, z), [((z.devices, z.chunk, chan), BF16)], name="sum")(got)
    whole = exchange(chunk)
    (input_grad,) = call(bind(input_kernel, z), [((tiles, side, side, chan), F32)], name="input")(got, pix_row, inner)
    grad_first, grad_second, grad_down = call(
        bind(spread_kernel, z),
        [((z.tap_rows, chan), F32), ((z.tap_rows, chan), F32), ((z.down_rows, chan), F32)],
        name="spread",
    )(whole)
    return features[None], input_grad[None], grad_first, grad_second, grad_down


def solution(mesh):
    split = P("dp", "tile", None, None, None)
    return jax.shard_map(
        local,
        mesh=mesh,
        in_specs=(split, split, P(), P(), P(), P(), P(), P(), P()),
        out_specs=(split, split, P("dp", None), P("dp", None), P("dp", None)),
        check_vma=False,
    )
```

profile of v0, /device:TPU:1, one launch (start us, length us, event | category | flops | bytes accessed | tf_op | source)
XLA Modules:
  0.0 103.4 jit_solution(15093193370149687339)
XLA Ops:
  0.6 0.0 copy-start.33
  0.6 0.7 copy-done.33
  1.3 0.1 copy.14.eo_ref
  1.5 0.0 copy-start.31
  1.5 0.8 copy.15.co_ref
  2.3 0.0 copy-done.31
  2.3 0.0 copy-start.32
  2.3 0.1 copy.16.ids_ref
  2.5 0.6 copy-done.32
  3.0 0.1 copy.17.turn_ref
  3.1 0.0 copy-done.2
  3.2 0.0 copy-start.1
  3.2 2.4 %pack.1 = (bf16[16,48,128]{2,1,0:T(8,128)(2,1)}, s32[768,128]{1,0:T(8,128)S(1)}, s32[8,768]{1,0:T(8,128)S(1)}) custom-call(s32[1]{0:T(128)} %bitcast.1.me_ref, s32[256,4]{1,0:T(8,128)S(1)} %copy.14.eo_ref, s32[256,4]{1,0:T(8,128)S(1)} %copy.15.co_ref, s32[256,8]{1,0:T(8,128)S(1)} %copy.16.ids_ref, s32[256,8]{1,0:T(8,128)S(1)} %copy.17.turn_ref, ...), custom_call_target="tpu_custom_call" | custom-call | tf_op jit(solution)/shard_map/pack/pallas_call | solution.py:395
  5.6 0.6 copy-done.20
  6.2 7.4 %all-to-all-start = ((bf16[16,48,128]{2,1,0:T(8,128)(2,1)}), bf16[16,48,128]{2,1,0:T(8,128)(2,1)S(1)}, u32[]{:S(2)}, u32[]{:S(2)}) async-start(bf16[16,48,128]{2,1,0:T(8,128)(2,1)} %get-tuple-element.34), calls=%async_computation | async-start | bytes 393216 | tf_op jit(solution)/shard_map/all_to_all | solution.py:409
  13.6 0.0 copy-done.30
  13.6 0.0 copy-done.1
  13.6 0.0 copy-done
  13.6 0.8 copy-done.11
  14.5 0.9 aside.1
  15.4 0.0 copy-start.9
  15.4 0.8 copy-done.9
  16.2 0.7 copy-done.14
  16.9 0.6 copy-done.26
  17.5 4.4 %all-to-all-done.got_ref = bf16[16,48,128]{2,1,0:T(8,128)(2,1)S(1)} async-done(((bf16[16,48,128]{2,1,0:T(8,128)(2,1)}), bf16[16,48,128]{2,1,0:T(8,128)(2,1)S(1)}, u32[]{:S(2)}, u32[]{:S(2)}) %all-to-all-start) | async-done | bytes 196640 | tf_op jit(solution)/shard_map/all_to_all | solution.py:409
  21.9 2.3 %first.1 = (bf16[16,48,128]{2,1,0:T(8,128)(2,1)S(1)}, bf16[1024,128]{1,0:T(8,128)(2,1)S(1)}, f32[1024,128]{1,0:T(8,128)S(1)}, bf16[1280,384]{1,0:T(8,128)(2,1)S(1)}) custom-call(bf16[16,48,128]{2,1,0:T(8,128)(2,1)S(1)} %all-to-all-done.got_ref, s32[640,128]{1,0:T(8,128)S(1)} %get-tuple-element.35.cell_ref, bf16[16,8,8,128]{3,2,1,0:T(8,128)(2,1)S(1)} %bitcast.19, ...), custom_call_target="tpu_custom_call" | custom-call | tf_op jit(solution)/shard_map/first/pallas_call | solution.py:395
  24.2 0.0 copy-done.16
  24.2 0.0 copy-done.23
  24.2 0.8 copy-done.3
  25.0 11.3 %all_to_all.25.got_ref = bf16[16,48,128]{2,1,0:T(8,128)(2,1)S(1)} all-to-all(bf16[16,48,128]{2,1,0:T(8,128)(2,1)S(1)} %get-tuple-element.37), channel_id=1, replica_groups=mesh['dp'=2,'tile'=16] {'tile'}, dimensions={0} | all-to-all | bytes 393216 | tf_op jit(solution)/shard_map/all_to_all | solution.py:409
  36.3 0.0 copy-done.24
  36.3 3.8 %second.1 = (bf16[16,48,128]{2,1,0:T(8,128)(2,1)}, f32[1024,128]{1,0:T(8,128)S(1)}, bf16[1024,128]{1,0:T(8,128)(2,1)S(1)}, f32[1024,128]{1,0:T(8,128)S(1)}, bf16[1280,384]{1,0:T(8,128)(2,1)S(1)}) custom-call(bf16[16,48,128]{2,1,0:T(8,128)(2,1)S(1)} %all_to_all.25.got_ref, s32[640,128]{1,0:T(8,128)S(1)} %get-tuple-element.35.cell_ref, ...), custom_call_target="tpu_custom_call" | custom-call | tf_op jit(solution)/shard_map/second/pallas_call | solution.py:395
  40.1 0.8 copy-done.5
  40.9 0.8 copy-done.7
  41.7 0.7 copy-done.18
  42.4 4.6 %all-to-all-start.2 = ((bf16[16,48,128]{2,1,0:T(8,128)(2,1)}), bf16[16,48,128]{2,1,0:T(8,128)(2,1)S(1)}, u32[]{:S(2)}, u32[]{:S(2)}) async-start(bf16[16,48,128]{2,1,0:T(8,128)(2,1)} %get-tuple-element.47), calls=%async_computation.2 | async-start | bytes 393216 | tf_op jit(solution)/shard_map/all_to_all | solution.py:409
  47.0 0.0 copy-start.8
  47.1 1.0 copy-done.8
  48.1 0.9 copy-done.19
  49.0 1.8 %early.1 = (bf16[256,128]{1,0:T(8,128)(2,1)S(1)}, f32[832,128]{1,0:T(8,128)S(1)}, bf16[1,832,128]{2,1,0:T(8,128)(2,1)}) custom-call(s32[1]{0:T(128)} %bitcast.at_ref, bf16[1280,384]{1,0:T(8,128)(2,1)S(1)} %get-tuple-element.42.columns_ref, bf16[1024,128]{1,0:T(8,128)(2,1)S(1)} %copy-done.19, f32[1024,128]{1,0:T(8,128)S(1)} %copy-done.8, ...), custom_call_target="tpu_custom_call" | custom-call | tf_op jit(solution)/shard_map/early/pallas_call | solution.py:395
  50.8 0.8 copy-done.12
  51.6 0.6 copy-done.28
  52.2 1.2 %collective-permute-start = (bf16[832,128]{1,0:T(8,128)(2,1)}, bf16[832,128]{1,0:T(8,128)(2,1)S(1)}, u32[]{:S(2)}, u32[]{:S(2)}) collective-permute-start(bf16[832,128]{1,0:T(8,128)(2,1)} %bitcast.9), channel_id=1, source_target_pairs={{0,16},{16,0},{1,17},{17,1},{2,18},{18,2},{3,19},{19,3},{4,20},{20... | collective-permute-start | bytes 638984 | tf_op jit(solution)/shard_map/ppermute | solution.py:415
  53.4 1.6 %all-to-all-done.2.got_ref = bf16[16,48,128]{2,1,0:T(8,128)(2,1)S(1)} async-done(((bf16[16,48,128]{2,1,0:T(8,128)(2,1)}), bf16[16,48,128]{2,1,0:T(8,128)(2,1)S(1)}, u32[]{:S(2)}, u32[]{:S(2)}) %all-to-all-start.2) | async-done | bytes 196640 | tf_op jit(solution)/shard_map/all_to_all | solution.py:409
  55.1 0.0 copy-done.6
  55.1 0.0 copy-start.15
  55.1 0.0 copy-start.25
  55.1 1.6 %slope.1 = (bf16[1024,128]{1,0:T(8,128)(2,1)S(1)}, f32[576,128]{1,0:T(8,128)S(1)}, bf16[1,576,128]{2,1,0:T(8,128)(2,1)S(1)}) custom-call(s32[1]{0:T(128)} %bitcast.at_ref, bf16[16,48,128]{2,1,0:T(8,128)(2,1)S(1)} %all-to-all-done.2.got_ref, s32[8,768]{1,0:T(8,128)S(1)} %copy-done.21, f32[1024,128]{1,0:T(8,128)S(1)} %copy-done.6, f32[1024,128]{1,0:T(8,128)S(1)} %copy-done.4, ...), custom_call_target="tpu_custom_call" | custom-call | tf_op jit(solution)/shard_map/slope/pallas_call | solution.py:395
  56.7 0.0 copy-start.13
  56.7 1.3 %collective-permute-start.1 = (bf16[576,128]{1,0:T(8,128)(2,1)S(1)}, bf16[576,128]{1,0:T(8,128)(2,1)S(1)}, u32[]{:S(2)}, u32[]{:S(2)}) collective-permute-start(bf16[576,128]{1,0:T(8,128)(2,1)S(1)} %bitcast.24), channel_id=1, source_target_pairs={{0,16},{16,0},{1,17},{17,1},{2,18},{18,2},{3,19},{19,3},{4,20},{20... | collective-permute-start | bytes 442376 | tf_op jit(solution)/shard_map/ppermute | solution.py:415
  58.0 1.7 %last.1 = (bf16[16,48,128]{2,1,0:T(8,128)(2,1)S(1)}, f32[1024,128]{1,0:T(8,128)S(1)}) custom-call(bf16[1024,128]{1,0:T(8,128)(2,1)S(1)} %get-tuple-element.52.slope_ref, bf16[1152,128]{1,0:T(8,128)(2,1)S(1)} %copy-done.15, s32[8,640]{1,0:T(8,128)S(1)} %copy-done.25), custom_call_target="tpu_custom_call" | custom-call | tf_op jit(solution)/shard_map/last/pallas_call | solution.py:395
  59.7 0.0 collective-permute-done
  59.7 1.7 %collective-permute-done.1 = bf16[576,128]{1,0:T(8,128)(2,1)S(1)} collective-permute-done((bf16[576,128]{1,0:T(8,128)(2,1)S(1)}, bf16[576,128]{1,0:T(8,128)(2,1)S(1)}, u32[]{:S(2)}, u32[]{:S(2)}) %collective-permute-start.1) | collective-permute-done | bytes 147488 | tf_op jit(solution)/shard_map/ppermute | solution.py:415
  61.4 0.0 copy-done.13
  61.4 0.1 join.1
  61.5 24.4 %all_to_all.26.got_ref = bf16[16,144,128]{2,1,0:T(8,128)(2,1)S(1)} all-to-all(bf16[16,144,128]{2,1,0:T(8,128)(2,1)S(1)} %join.1), channel_id=1, replica_groups=mesh['dp'=2,'tile'=16] {'tile'}, dimensions={0} | all-to-all | bytes 1179648 | tf_op jit(solution)/shard_map/all_to_all | solution.py:409
  85.8 0.8 sum.1
  86.6 3.9 %all-to-all-start.4 = ((bf16[16,96,128]{2,1,0:T(8,128)(2,1)}), bf16[16,96,128]{2,1,0:T(8,128)(2,1)S(1)}, u32[]{:S(2)}, u32[]{:S(2)}) async-start(bf16[16,96,128]{2,1,0:T(8,128)(2,1)} %sum.1), calls=%async_computation.4 | async-start | bytes 786432 | tf_op jit(solution)/shard_map/all_to_all | solution.py:409
  90.5 0.0 copy-start.22
  90.5 0.7 copy.23
  91.2 0.1 copy-done.22
  91.3 1.4 %input.1 = f32[16,8,8,128]{3,2,1,0:T(8,128)} custom-call(bf16[16,144,128]{2,1,0:T(8,128)(2,1)S(1)} %all_to_all.26.got_ref, s32[8,768]{1,0:T(8,128)S(1)} %copy-done.22, f32[1024,128]{1,0:T(8,128)S(1)} %get-tuple-element.59.inner_ref), custom_call_target="tpu_custom_call" | custom-call | tf_op jit(solution)/shard_map/input/pallas_call | solution.py:395
  92.6 9.9 %all-to-all-done.4.got_ref = bf16[16,96,128]{2,1,0:T(8,128)(2,1)S(1)} async-done(((bf16[16,96,128]{2,1,0:T(8,128)(2,1)}), bf16[16,96,128]{2,1,0:T(8,128)(2,1)S(1)}, u32[]{:S(2)}, u32[]{:S(2)}) %all-to-all-start.4) | async-done | bytes 393248 | tf_op jit(solution)/shard_map/all_to_all | solution.py:409
  102.5 0.9 spread.1
  (33 shorter events, 0.1 us)
Async XLA Ops:
  0.6 0.7 copy-start.33
  1.3 1.8 %copy-start.2 = (bf16[1,16,8,8,128]{4,3,2,1,0:T(8,128)(2,1)S(1)}, bf16[1,16,8,8,128]{4,3,2,1,0:T(8,128)(2,1)}, u32[]{:S(2)}) copy-start(bf16[1,16,8,8,128]{4,3,2,1,0:T(8,128)(2,1)} %param.9) | copy-start | bytes 786436
  1.5 0.8 copy-start.31
  2.3 0.7 copy-start.32
  3.2 10.5 %copy-start.1 = (bf16[1152,128]{1,0:T(8,128)(2,1)S(1)}, bf16[1152,128]{1,0:T(8,128)(2,1)}, u32[]{:S(2)}) copy-start(bf16[1152,128]{1,0:T(8,128)(2,1)} %w_ref.3) | copy-start | bytes 884740
  5.6 0.6 copy-start.20
  5.6 8.0 %copy-start = (bf16[1152,128]{1,0:T(8,128)(2,1)S(1)}, bf16[1152,128]{1,0:T(8,128)(2,1)}, u32[]{:S(2)}) copy-start(bf16[1152,128]{1,0:T(8,128)(2,1)} %w_ref.2) | copy-start | bytes 884740
  5.6 8.0 %copy-start.30 = (bf16[1,16,4,4,128]{4,3,2,1,0:T(4,128)(2,1)S(1)}, bf16[1,16,4,4,128]{4,3,2,1,0:T(4,128)(2,1)}, u32[]{:S(2)}) copy-start(bf16[1,16,4,4,128]{4,3,2,1,0:T(4,128)(2,1)} %param.10) | copy-start | bytes 196612
  6.2 15.7 %all-to-all-start = ((bf16[16,48,128]{2,1,0:T(8,128)(2,1)}), bf16[16,48,128]{2,1,0:T(8,128)(2,1)S(1)}, u32[]{:S(2)}, u32[]{:S(2)}) async-start(bf16[16,48,128]{2,1,0:T(8,128)(2,1)} %get-tuple-element.34), calls=%async_computation | async-start | bytes 393216 | tf_op jit(solution)/shard_map/all_to_all | solution.py:409
  13.6 0.9 copy-start.11
  15.4 0.8 copy-start.9
  16.2 0.7 copy-start.14
  16.9 0.6 copy-start.26
  17.5 6.7 %copy-start.16 = (bf16[1152,128]{1,0:T(8,128)(2,1)}, bf16[1152,128]{1,0:T(8,128)(2,1)S(1)}, u32[]{:S(2)}) copy-start(bf16[1152,128]{1,0:T(8,128)(2,1)S(1)} %get-tuple-element.40.turned_ref) | copy-start | bytes 884740
  17.5 6.7 %copy-start.23 = (s32[8,640]{1,0:T(8,128)}, s32[8,640]{1,0:T(8,128)S(1)}, u32[]{:S(2)}) copy-start(s32[8,640]{1,0:T(8,128)S(1)} %get-tuple-element.38.cell_row_ref) | copy-start | bytes 61444
  21.9 14.4 %copy-start.10 = (f32[1024,128]{1,0:T(8,128)S(1)}, f32[1024,128]{1,0:T(8,128)}, u32[]{:S(2)}) copy-start(f32[1024,128]{1,0:T(8,128)} %copy-done.9) | copy-start | bytes 1572868
  24.2 0.8 copy-start.3
  25.0 11.3 %copy-start.17 = (bf16[1152,128]{1,0:T(8,128)(2,1)S(1)}, bf16[1152,128]{1,0:T(8,128)(2,1)}, u32[]{:S(2)}) copy-start(bf16[1152,128]{1,0:T(8,128)(2,1)} %copy-done.16) | copy-start | bytes 884740
  25.0 11.3 %copy-start.24 = (s32[8,640]{1,0:T(8,128)S(1)}, s32[8,640]{1,0:T(8,128)}, u32[]{:S(2)}) copy-start(s32[8,640]{1,0:T(8,128)} %copy-done.23) | copy-start | bytes 61444
  40.1 0.8 copy-start.5
  40.9 0.8 copy-start.7
  41.7 0.7 copy-start.18
  42.4 4.6 %copy-start.27 = (bf16[256,128]{1,0:T(8,128)(2,1)S(1)}, bf16[256,128]{1,0:T(8,128)(2,1)}, u32[]{:S(2)}) copy-start(bf16[256,128]{1,0:T(8,128)(2,1)} %copy-done.26) | copy-start | bytes 196612
  42.4 12.6 %all-to-all-start.2 = ((bf16[16,48,128]{2,1,0:T(8,128)(2,1)}), bf16[16,48,128]{2,1,0:T(8,128)(2,1)S(1)}, u32[]{:S(2)}, u32[]{:S(2)}) async-start(bf16[16,48,128]{2,1,0:T(8,128)(2,1)} %get-tuple-element.47), calls=%async_computation.2 | async-start | bytes 393216 | tf_op jit(solution)/shard_map/all_to_all | solution.py:409
  47.0 1.0 %copy-start.8 = (f32[1024,128]{1,0:T(8,128)S(1)}, f32[1024,128]{1,0:T(8,128)}, u32[]{:S(2)}) copy-start(f32[1024,128]{1,0:T(8,128)} %copy-done.7) | copy-start | bytes 1572868
  48.1 0.9 copy-start.19
  49.0 6.0 %copy-start.4 = (f32[1024,128]{1,0:T(8,128)S(1)}, f32[1024,128]{1,0:T(8,128)}, u32[]{:S(2)}) copy-start(f32[1024,128]{1,0:T(8,128)} %copy-done.3) | copy-start | bytes 1572868
  49.0 6.0 %copy-start.6 = (f32[1024,128]{1,0:T(8,128)S(1)}, f32[1024,128]{1,0:T(8,128)}, u32[]{:S(2)}) copy-start(f32[1024,128]{1,0:T(8,128)} %copy-done.5) | copy-start | bytes 1572868
  49.0 6.0 %copy-start.21 = (s32[8,768]{1,0:T(8,128)S(1)}, s32[8,768]{1,0:T(8,128)}, u32[]{:S(2)}) copy-start(s32[8,768]{1,0:T(8,128)} %copy-done.20) | copy-start | bytes 73732
  50.8 0.8 copy-start.12
  51.6 0.6 copy-start.28
  52.2 7.5 %collective-permute-start = (bf16[832,128]{1,0:T(8,128)(2,1)}, bf16[832,128]{1,0:T(8,128)(2,1)S(1)}, u32[]{:S(2)}, u32[]{:S(2)}) collective-permute-start(bf16[832,128]{1,0:T(8,128)(2,1)} %bitcast.9), channel_id=1, source_target_pairs={{0,16},{16,0},{1,17},{17,1},{2,18},{18,2},{3,19},{19,3},{4,20},{20... | collective-permute-start | bytes 638984 | tf_op jit(solution)/shard_map/ppermute | solution.py:415
  55.1 2.9 %copy-start.15 = (bf16[1152,128]{1,0:T(8,128)(2,1)S(1)}, bf16[1152,128]{1,0:T(8,128)(2,1)}, u32[]{:S(2)}) copy-start(bf16[1152,128]{1,0:T(8,128)(2,1)} %copy-done.14) | copy-start | bytes 884740
  55.1 2.9 %copy-start.25 = (s32[8,640]{1,0:T(8,128)S(1)}, s32[8,640]{1,0:T(8,128)}, u32[]{:S(2)}) copy-start(s32[8,640]{1,0:T(8,128)} %copy-done.23) | copy-start | bytes 61444
  56.7 4.7 %copy-start.13 = (f32[832,128]{1,0:T(8,128)S(1)}, f32[832,128]{1,0:T(8,128)}, u32[]{:S(2)}) copy-start(f32[832,128]{1,0:T(8,128)} %copy-done.12) | copy-start | bytes 1277956
  56.7 4.7 %collective-permute-start.1 = (bf16[576,128]{1,0:T(8,128)(2,1)S(1)}, bf16[576,128]{1,0:T(8,128)(2,1)S(1)}, u32[]{:S(2)}, u32[]{:S(2)}) collective-permute-start(bf16[576,128]{1,0:T(8,128)(2,1)S(1)} %bitcast.24), channel_id=1, source_target_pairs={{0,16},{16,0},{1,17},{17,1},{2,18},{18,2},{3,19},{19,3},{4,20},{20... | collective-permute-start | bytes 442376 | tf_op jit(solution)/shard_map/ppermute | solution.py:415
  86.6 3.9 %copy-start.29 = (bf16[256,128]{1,0:T(8,128)(2,1)S(1)}, bf16[256,128]{1,0:T(8,128)(2,1)}, u32[]{:S(2)}) copy-start(bf16[256,128]{1,0:T(8,128)(2,1)} %copy-done.28) | copy-start | bytes 196612
  86.6 15.8 %all-to-all-start.4 = ((bf16[16,96,128]{2,1,0:T(8,128)(2,1)}), bf16[16,96,128]{2,1,0:T(8,128)(2,1)S(1)}, u32[]{:S(2)}, u32[]{:S(2)}) async-start(bf16[16,96,128]{2,1,0:T(8,128)(2,1)} %sum.1), calls=%async_computation.4 | async-start | bytes 786432 | tf_op jit(solution)/shard_map/all_to_all | solution.py:409
  90.5 0.7 copy-start.22
where the time goes:
time: 104 us; the launch traced here: 103 us
  blocking collectives  35.7 us (34%)
  starting transfers between devices  18.3 us (18%)
  Pallas kernels  17.6 us (17%)
  waiting for transfers between devices  17.6 us (17%)
  local copies, waits for them, and re-layouts  13.3 us (13%)
    all_to_all x2, blocking collectives, exchange(): return lax.all_to_all(x, 'tile', split_axis=0, concat_axis=0, tiled=True)  35.7 us
    pallas_call x11, Pallas kernels, run(): pl.pallas_call(body, out_shape=[jax.ShapeDtypeStruct(shape, dtype) for sh...  17.6 us
    all_to_all x3, waiting for transfers between devices, exchange(): return lax.all_to_all(x, 'tile', split_axis=0, concat_axis=0, tiled=True)  15.9 us
    all_to_all x3, starting transfers between devices, exchange(): return lax.all_to_all(x, 'tile', split_axis=0, concat_axis=0, tiled=True)  15.8 us
    unnamed x72, local copies, waits for them, and re-layouts  12.6 us
    ppermute x2, starting transfers between devices, to_samples(): lax.ppermute(others[k], 'dp', [(s, (s + k + 1) % samples) for s in range(...  2.49 us
  transfers between devices with their start and end apart: 5, of which 4 were waited for; matrix products, arithmetic and copies ran while one was open for 1% of the time, Pallas kernels for 7%

commit v1 on v0

v1 whole, which is shorter than its diff:
```python
import functools
import jax
import jax.numpy as jnp
from jax import lax
from jax.experimental import pallas as pl
from jax.experimental.pallas import tpu as pltpu
from jax.sharding import PartitionSpec as P

F32, BF16, I32 = jnp.float32, jnp.bfloat16, jnp.int32
LANES = 128


class Sizes:
    def __init__(self, tiles, side, chan, devices, samples):
        self.tiles, self.side, self.chan = tiles, side, chan
        self.devices, self.samples = devices, samples
        self.slots = max(2, 4 * tiles // devices + 1)
        self.pair = -(-self.slots * (side + 1) // 16) * 16
        self.sent = devices * self.pair
        self.line = tiles * side
        self.pixels = side * self.line
        self.column = (side + 2) * tiles
        self.cells = 2 * self.line + 2 * self.column
        self.cells_up = -(-self.cells // LANES) * LANES
        self.tap_rows = 9 * chan // samples
        self.down_rows = 4 * chan // samples
        self.late = self.tap_rows // 2
        self.early = (self.tap_rows + self.down_rows) // 2
        self.chunk = -(-(self.early + self.late) // (16 * devices)) * 16
        self.parts = [(s, c) for s in range(samples) for c in range(2)]
        self.slot_rows = -(-self.slots // 8) * 8


def iota(shape, dim):
    return lax.broadcasted_iota(I32, shape, dim)


def mm(a, b):
    return jnp.dot(a.astype(BF16), b.astype(BF16), preferred_element_type=F32)


def mm_t(a, b):
    return lax.dot_general(a, b, (((0,), (0,)), ((), ())), preferred_element_type=F32)


def flag(cond):
    return jnp.where(cond, 1.0, 0.0).astype(BF16)


def pick_rows(index, width):
    rows = index.shape[0]
    lane = iota((rows, LANES), 1)
    return jnp.concatenate([flag(index == lane + at) for at in range(0, width, LANES)], axis=1)


def pick_columns(index, height):
    shape = (height, index.shape[1])
    return flag(jnp.broadcast_to(index, shape) == iota(shape, 0))


def row_first(x):
    tiles, side, _, chan = x.shape
    x = x.astype(F32)
    return jnp.stack([x[:, r].reshape(tiles * side, chan) for r in range(side)], axis=0)


def sender_index(me, owners, local_ids, turns, z):
    requests = z.devices * z.tiles
    row8 = iota((8, requests), 0)
    matched = owners == me
    code = jnp.where(matched, local_ids * 16 + turns * 4 + (row8 & 3) + 1, 0).astype(F32)
    found = jnp.where(matched, 1.0, 0.0)

    def both(values):
        edge = jnp.sum(values[:4], axis=0, keepdims=True)
        corner = jnp.sum(values[4:], axis=0, keepdims=True)
        shape = (z.slot_rows, requests)
        return jnp.concatenate([jnp.broadcast_to(edge, shape), jnp.broadcast_to(corner, shape)], axis=0)

    column = iota((1, 1, requests), 2)
    cube = (z.devices, z.tiles, requests)
    earlier = (iota(cube, 0) == lax.div(column, z.tiles)) & (iota(cube, 1) < lax.rem(column, z.tiles))
    rank = mm(both(found), flag(earlier).reshape(requests, requests))
    slot = iota((2 * z.slot_rows, requests), 0)
    slot = jnp.where(slot < z.slot_rows, slot, slot - z.slot_rows)
    placed = jnp.where(slot.astype(F32) == rank, both(code), 0.0)
    row = iota((1, z.sent), 1)
    device, at = lax.div(row, z.pair), lax.rem(row, z.pair)
    cube = (z.devices, z.tiles, z.sent)
    rows = mm(placed, flag(iota(cube, 0) == device.reshape(1, 1, z.sent)).reshape(requests, z.sent))
    edges = z.slots * z.side
    is_edge = at < edges
    wanted = jnp.where(is_edge, lax.div(at, z.side), at - edges + z.slot_rows)
    wanted = jnp.where(at < edges + z.slots, wanted, -1)
    here = iota((2 * z.slot_rows, z.sent), 0) == wanted
    code = jnp.sum(jnp.where(here, rows, 0.0), axis=0, keepdims=True).astype(I32) - 1
    along = lax.rem(at, z.side)
    source, turn, towards = code >> 4, (code >> 2) & 3, code & 3
    end = z.side - 1
    i_edge = jnp.where(towards == 0, end, jnp.where(towards == 2, 0, along))
    j_edge = jnp.where(towards == 1, 0, jnp.where(towards == 3, end, along))
    i_corner = jnp.where((towards == 0) | (towards == 3), end, 0)
    j_corner = jnp.where(towards >= 2, end, 0)
    i = jnp.where(is_edge, i_edge, i_corner)
    j = jnp.where(is_edge, j_edge, j_corner)
    row = jnp.where(turn == 0, i, jnp.where(turn == 1, j, jnp.where(turn == 2, end - i, end - j)))
    col = jnp.where(turn == 0, j, jnp.where(turn == 1, end - i, jnp.where(turn == 2, end - j, i)))
    return jnp.where(code >= 0, row * z.line + source * z.side + col, -1)


def receiver_index(own, z):
    lane = iota((z.tiles, LANES), 1)
    lower = flag(iota((z.tiles, z.tiles), 1) < iota((z.tiles, z.tiles), 0))
    values = jnp.zeros((z.tiles, LANES), F32)
    for base in (0, 4):
        hits = [jnp.broadcast_to(own[:, base + k : base + k + 1], (z.tiles, LANES)) == lane for k in range(4)]
        named = sum(jnp.where(hit, 1.0, 0.0) for hit in hits)
        before = mm(lower, named)
        for k in range(4):
            rank = jnp.sum(jnp.where(hits[k], before, 0.0), axis=1, keepdims=True)
            values = jnp.where(lane == 2 * base + k, own[:, base + k : base + k + 1].astype(F32), values)
            values = jnp.where(lane == 2 * base + 4 + k, rank, values)
    ones = jnp.ones((LANES, LANES), BF16)

    def spread(tile, own_lane, is_edge, along):
        rows = tile.shape[0]
        lane = iota((rows, LANES), 1)
        here = mm(flag(tile[:, : z.tiles] == iota((rows, z.tiles), 1)), values)
        own = mm(jnp.where(lane == own_lane, here, 0.0), ones).astype(I32)
        rank = mm(jnp.where(lane == own_lane + 4, here, 0.0), ones).astype(I32)
        return own * z.pair + jnp.where(is_edge, rank * z.side + along, z.slots * z.side + rank)

    line = (z.tiles, z.side, LANES)
    tile = iota(line, 0).reshape(z.line, LANES)
    along = iota(line, 1).reshape(z.line, LANES)
    parts = [spread(tile, k, jnp.full(tile.shape, True), along) for k in (0, 2)]
    column = (z.side + 2, z.tiles, LANES)
    row = iota(column, 0).reshape(z.column, LANES)
    tile = iota(column, 1).reshape(z.column, LANES)
    is_edge = (row > 0) & (row <= z.side)
    for edge, top, bottom in ((3, 3, 2), (1, 0, 1)):
        own_lane = jnp.where(is_edge, edge, jnp.where(row == 0, 8 + top, 8 + bottom))
        parts.append(spread(tile, own_lane, is_edge, row - 1))
    parts.append(jnp.full((z.cells_up - z.cells, LANES), -1, I32))
    return jnp.concatenate(parts, axis=0)


def as_column(index):
    return jnp.transpose(jnp.broadcast_to(index.astype(F32), (LANES, index.shape[1]))).astype(I32)


def as_row(index):
    return jnp.transpose(index.astype(F32))[0:8].astype(I32)


def pack_kernel(z, me_ref, eo_ref, co_ref, ids_ref, turn_ref, x_ref, send_ref):
    owners = jnp.concatenate([eo_ref[...], co_ref[...]], axis=0)
    index = sender_index(me_ref[0], owners, ids_ref[...], turn_ref[...], z)
    pixels = row_first(x_ref[...]).reshape(z.pixels, z.chan)
    send_ref[...] = mm(pick_rows(as_column(index), z.pixels), pixels).astype(BF16).reshape(send_ref.shape)


def side_kernel(
    z, me_ref, eo_ref, co_ref, ids_ref, turn_ref, cot_ref, wd_ref, w1_ref, w2_ref,
    column_ref, pix_row_ref, cell_row_ref, back_ref, t1_ref, t2_ref,
):
    me = me_ref[0]
    owners = jnp.concatenate([eo_ref[...], co_ref[...]], axis=0)
    index = sender_index(me, owners, ids_ref[...], turn_ref[...], z)
    column_ref[: z.sent, :] = as_column(index)
    pix_row_ref[...] = jnp.broadcast_to(index, pix_row_ref.shape)
    shape = (z.tiles, z.devices * z.tiles)
    mine = flag(iota(shape, 1) == iota(shape, 0) + me * z.tiles)
    own = lax.dot_general(
        mine, owners.astype(F32).astype(BF16), (((1,), (1,)), ((), ())), preferred_element_type=F32
    )
    index = receiver_index(own.astype(I32), z)
    column_ref[z.sent :, :] = index
    cell_row_ref[...] = as_row(index)
    chan, half = z.chan, z.side // 2
    for taps, out in ((w1_ref, t1_ref), (w2_ref, t2_ref)):
        for tap in range(9):
            rows = slice(tap * chan, (tap + 1) * chan)
            out[rows, :] = jnp.transpose(taps[rows, :].astype(F32)).astype(BF16)
    cot = cot_ref[...]
    part = half * z.tiles
    for p in range(2):
        for q in range(2):
            tap = wd_ref[(2 * p + q) * chan : (2 * p + q + 1) * chan, :]
            back = lax.dot_general(cot, tap, (((1,), (1,)), ((), ())), preferred_element_type=F32)
            for i in range(half):
                back_ref[pl.ds((2 * i + p) * z.line + q, part, stride=2), :] = back[i * part : (i + 1) * part]


def padded_columns(z, center, arrived, index, west_ref, east_ref, out_ref):
    rims = mm(pick_rows(index, z.sent), arrived)
    north, south = rims[: z.line], rims[z.line : 2 * z.line]
    at = 2 * z.line
    west_ref[pl.ds(0, z.column, stride=z.side), :] = rims[at : at + z.column]
    east_ref[pl.ds(z.side - 1, z.column, stride=z.side), :] = rims[at + z.column : at + 2 * z.column]
    shape = (z.column, z.side, z.chan)
    middle = jnp.concatenate([north, center, south], axis=0).reshape(shape)
    place = iota(shape, 1)
    flat = (z.column * z.side, z.chan)
    left = jnp.where(place == 0, west_ref[...].reshape(shape), pltpu.roll(middle, 1, 1))
    right = jnp.where(place == z.side - 1, east_ref[...].reshape(shape), pltpu.roll(middle, z.side - 1, 1))
    out_ref[:, : z.chan] = left.reshape(flat).astype(BF16)
    out_ref[:, z.chan : 2 * z.chan] = middle.reshape(flat).astype(BF16)
    out_ref[:, 2 * z.chan :] = right.reshape(flat).astype(BF16)


def conv(z, columns_ref, w_ref):
    total = None
    for p in range(3):
        part = jnp.dot(
            columns_ref[p * z.line : p * z.line + z.pixels, :],
            w_ref[3 * p * z.chan : 3 * (p + 1) * z.chan, :],
            preferred_element_type=F32,
        )
        total = part if total is None else total + part
    return total


def silu_slope(v):
    s = 1.0 / (1.0 + jnp.exp(-v))
    return s * (1.0 + v * (1.0 - s))


def first_kernel(z, got_ref, index_ref, x_ref, w_ref, send_ref, hidden_ref, columns_ref, west_ref, east_ref):
    center = row_first(x_ref[...]).reshape(z.pixels, z.chan)
    padded_columns(z, center, got_ref[...].reshape(z.sent, z.chan), index_ref[z.sent :, :], west_ref, east_ref, columns_ref)
    v = conv(z, columns_ref, w_ref)
    hidden = (v / (1.0 + jnp.exp(-v))).astype(BF16)
    send_ref[...] = mm(pick_rows(index_ref[: z.sent, :], z.pixels), hidden).astype(BF16).reshape(send_ref.shape)
    hidden_ref[...] = hidden


def again_kernel(z, columns_ref, w_ref, slope_ref):
    slope_ref[...] = silu_slope(conv(z, columns_ref, w_ref))


def shifted(z, slope):
    cube = slope.reshape(slope.shape[0] // z.side, z.side, z.chan)
    place = iota(cube.shape, 1)
    after = jnp.where(place == z.side - 1, 0.0, pltpu.roll(cube, z.side - 1, 1))
    before = jnp.where(place == 0, 0.0, pltpu.roll(cube, 1, 1))
    return [part.reshape(slope.shape).astype(BF16) for part in (after, cube, before)]


def rims_back(z, slope, turned_ref, slope_ref):
    chan = z.chan
    parts = []
    for p, row in ((0, 0), (2, z.side - 1)):
        wide = jnp.concatenate(shifted(z, slope[row * z.line : (row + 1) * z.line]), axis=1)
        parts.append(jnp.dot(wide, turned_ref[3 * p * chan : 3 * (p + 1) * chan, :], preferred_element_type=F32))
    slope_ref[...] = slope
    blank = jnp.zeros((2 * z.tiles, chan), F32)
    for start, q in ((0, 0), (z.side - 1, 2)):
        line = slope_ref[pl.ds(start, z.side * z.tiles, stride=z.side), :]
        line = jnp.concatenate([blank, line, blank], axis=0).astype(BF16)
        side = None
        for p in range(3):
            part = jnp.dot(
                line[(2 - p) * z.tiles : (2 - p) * z.tiles + z.column],
                turned_ref[(3 * p + q) * chan : (3 * p + q + 1) * chan, :],
                preferred_element_type=F32,
            )
            side = part if side is None else side + part
        parts.append(side)
    parts.append(jnp.zeros((z.cells_up - z.cells, chan), F32))
    return jnp.concatenate(parts, axis=0).astype(BF16)


def inner_back(z, slope, turned_ref, wide_ref):
    chan = z.chan
    zero = jnp.zeros((z.line, 3 * chan), BF16)
    wide_ref[: z.line, :] = zero
    wide_ref[z.line + z.pixels :, :] = zero
    for q, part in enumerate(shifted(z, slope)):
        wide_ref[z.line : z.line + z.pixels, q * chan : (q + 1) * chan] = part
    total = None
    for p in range(3):
        part = jnp.dot(
            wide_ref[(2 - p) * z.line : (2 - p) * z.line + z.pixels, :],
            turned_ref[3 * p * chan : 3 * (p + 1) * chan, :],
            preferred_element_type=F32,
        )
        total = part if total is None else total + part
    return total


def second_kernel(
    z, got_ref, index_ref, cell_row_ref, hidden_ref, w_ref, turned_ref, back_ref,
    send_ref, slope_ref, out_ref, columns_ref, west_ref, east_ref, scratch_ref,
):
    center = hidden_ref[...].astype(F32)
    padded_columns(z, center, got_ref[...].reshape(z.sent, z.chan), index_ref[z.sent :, :], west_ref, east_ref, columns_ref)
    push(columns_ref)
    v = conv(z, columns_ref, w_ref)
    s = 1.0 / (1.0 + jnp.exp(-v))
    out_ref[...] = (v * s).astype(BF16)
    push(out_ref)
    slope = (back_ref[...] * (s * (1.0 + v * (1.0 - s)))).astype(BF16)
    slope_ref[...] = slope
    push(slope_ref)
    rims = rims_back(z, slope.astype(F32), turned_ref, scratch_ref)
    send_ref[...] = mm(pick_columns(cell_row_ref[0:1, :], z.sent), rims).astype(BF16).reshape(send_ref.shape)


def tap_products(z, columns_ref, slope, scale, total_ref):
    for p in range(3):
        part = mm_t(columns_ref[p * z.line : p * z.line + z.pixels, :], slope)
        total_ref[3 * p * z.chan : 3 * (p + 1) * z.chan, :] = part * scale


def deal_parts(z, sample_ref, me_ref, source_ref, own_ref, other_refs):
    rows = own_ref.shape[0]
    for k, (shift, core) in enumerate(z.parts):
        whose = lax.rem(sample_ref[0] + shift, z.samples)
        half = jnp.bitwise_xor(me_ref[0] & 1, core)
        part = source_ref[pl.ds((2 * whose + half) * rows, rows), :]
        if k == 0:
            own_ref[...] = part
        else:
            other_refs[k - 1][...] = part.astype(BF16)


def early_kernel(
    z, scale, sample_ref, me_ref, columns_ref, slope_ref, hidden_ref, cot_ref, wd_ref, feature_ref, own_ref, *refs
):
    other_refs, (taps_ref, total_ref, flat_ref, block_ref) = refs[:-4], refs[-4:]
    chan, half = z.chan, z.side // 2
    part = half * z.tiles
    tap_products(z, columns_ref, slope_ref[...], scale, taps_ref)
    flat_ref[...] = hidden_ref[...].astype(F32)
    for i in range(half):
        for p in range(2):
            for q in range(2):
                block_ref[i * part : (i + 1) * part, (2 * p + q) * chan : (2 * p + q + 1) * chan] = flat_ref[
                    pl.ds((2 * i + p) * z.line + q, part, stride=2), :
                ].astype(BF16)
    block = block_ref[...]
    feature_ref[...] = jnp.dot(block, wd_ref[...], preferred_element_type=F32).astype(BF16)
    down = mm_t(block, cot_ref[...]) * scale
    both = z.tap_rows + z.down_rows
    for s in range(z.samples):
        total_ref[s * both : s * both + z.tap_rows, :] = taps_ref[s * z.tap_rows : (s + 1) * z.tap_rows, :]
        total_ref[s * both + z.tap_rows : (s + 1) * both, :] = down[s * z.down_rows : (s + 1) * z.down_rows]
    deal_parts(z, sample_ref, me_ref, total_ref, own_ref, other_refs)


def inner_kernel(z, slope_ref, turned_ref, inner_ref, wide_ref):
    inner_ref[...] = inner_back(z, slope_ref[...].astype(F32), turned_ref, wide_ref)


def slope_kernel(
    z, scale, sample_ref, me_ref, got_ref, pix_row_ref, inner_ref, slope_in_ref, columns_ref,
    slope_ref, own_ref, *refs,
):
    other_refs, total_ref = refs[:-1], refs[-1]
    back = inner_ref[...] + mm(pick_columns(pix_row_ref[0:1, :], z.pixels), got_ref[...].reshape(z.sent, z.chan))
    slope = (back * slope_in_ref[...]).astype(BF16)
    slope_ref[...] = slope
    tap_products(z, columns_ref, slope, scale, total_ref)
    deal_parts(z, sample_ref, me_ref, total_ref, own_ref, other_refs)


def last_kernel(z, slope_ref, turned_ref, cell_row_ref, send_ref, scratch_ref):
    rims = rims_back(z, slope_ref[...].astype(F32), turned_ref, scratch_ref)
    send_ref[...] = mm(pick_columns(cell_row_ref[0:1, :], z.sent), rims).astype(BF16).reshape(send_ref.shape)


def join_kernel(z, rim_ref, early_ref, late_ref, *refs):
    others = len(z.parts) - 1
    send_ref, total_ref = refs[2 * others :]
    early, late = early_ref[...], late_ref[...]
    for k in range(others):
        early = early + refs[k][...].astype(F32)
        late = late + refs[others + k][...].astype(F32)
    total_ref[: z.early, :] = early
    total_ref[z.early : z.early + z.late, :] = late
    spare = z.devices * z.chunk - z.early - z.late
    if spare:
        total_ref[z.early + z.late :, :] = jnp.zeros((spare, z.chan), F32)
    send_ref[:, : z.pair, :] = rim_ref[...]
    send_ref[:, z.pair :, :] = total_ref[...].astype(BF16).reshape(z.devices, z.chunk, z.chan)


def sum_kernel(z, got_ref, out_ref):
    sums = []
    for core in range(2):
        total = got_ref[core, z.pair :, :].astype(F32)
        for k in range(core + 2, z.devices, 2):
            total = total + got_ref[k, z.pair :, :].astype(F32)
        sums.append(total.astype(BF16))
    for k in range(z.devices // 2):
        for core in range(2):
            out_ref[k, core * z.chunk : (core + 1) * z.chunk, :] = sums[core]


def input_kernel(z, got_ref, pix_row_ref, inner_ref, out_ref):
    arrived = got_ref[:, : z.pair, :].reshape(z.sent, z.chan)
    total = inner_ref[...] + mm(pick_columns(pix_row_ref[0:1, :], z.pixels), arrived)
    for r in range(z.side):
        out_ref[:, r] = total[r * z.line : (r + 1) * z.line].reshape(z.tiles, z.side, z.chan)


def spread_kernel(z, me_ref, mine_ref, other_ref, one_ref, two_ref, low_ref):
    first = (me_ref[0] & 1) == 0
    mine, other = mine_ref[...].astype(F32), other_ref[...].astype(F32)
    halves = []
    for core in range(2):
        rows = slice(core * z.chunk, (core + 1) * z.chunk)
        a, b = mine[:, rows], other[:, rows]
        pairs = jnp.stack([jnp.where(first, a, b), jnp.where(first, b, a)], axis=1)
        halves.append(pairs.reshape(z.devices * z.chunk, z.chan))
    one_ref[...] = jnp.concatenate([half[z.early : z.early + z.late] for half in halves], axis=0)
    early = jnp.concatenate([half[: z.early] for half in halves], axis=0)
    two_ref[...] = early[: z.tap_rows]
    low_ref[...] = early[z.tap_rows :]


def vmem(*shape, dtype=F32):
    return pltpu.VMEM(shape, dtype)


class Pulled:
    def __init__(self, source, buffer, semaphore):
        self.buffer, self.shape, self.waits = buffer, buffer.shape, True
        self.copy = pltpu.make_async_copy(source, buffer, semaphore)
        self.copy.start()

    def __getitem__(self, at):
        if self.waits:
            self.copy.wait()
            self.waits = False
        return self.buffer[at]


class Pushed:
    def __init__(self, target, buffer, semaphore):
        self.buffer, self.shape, self.started = buffer, buffer.shape, False
        self.copy = pltpu.make_async_copy(buffer, target, semaphore)

    def __getitem__(self, at):
        return self.buffer[at]

    def __setitem__(self, at, value):
        self.buffer[at] = value

    def send(self):
        if not self.started:
            self.copy.start()
            self.started = True


def push(ref):
    if isinstance(ref, Pushed):
        ref.send()


def call(body, outs, scratch=(), scalars=0, fetch=0, name=None):
    def run(*operands):
        first = len(operands) - fetch
        far = [len(out) == 3 for out in outs]
        fetched = operands[first:]
        sent = [out for out in outs if len(out) == 3]
        ends = (first, fetch, len(outs), fetch, len(sent), len(scratch), 1, 1)

        def kernel(*refs):
            groups, at = [], 0
            for count in ends:
                groups.append(refs[at : at + count])
                at += count
            here, there, results, in_buffers, out_buffers, rest, (in_sems,), (out_sems,) = groups
            pulled = [Pulled(ref, in_buffers[k], in_sems.at[k]) for k, ref in enumerate(there)]
            made, pushed = [], []
            for ref, is_far in zip(results, far):
                if is_far:
                    k = len(pushed)
                    pushed.append(Pushed(ref, out_buffers[k], out_sems.at[k]))
                    ref = pushed[k]
                made.append(ref)
            body(*here, *pulled, *made, *rest)
            for ref in pushed:
                ref.send()
            for ref in pushed:
                ref.copy.wait()

        spec = pl.BlockSpec(memory_space=pltpu.VMEM)
        small = pl.BlockSpec(memory_space=pltpu.SMEM)
        apart = pl.BlockSpec(memory_space=pltpu.HBM)
        return pl.pallas_call(
            kernel,
            out_shape=[
                pltpu.HBM(out[0], out[1]) if is_far else jax.ShapeDtypeStruct(out[0], out[1])
                for out, is_far in zip(outs, far)
            ],
            in_specs=[small] * scalars + [spec] * (first - scalars) + [apart] * fetch,
            out_specs=[apart if is_far else spec for is_far in far],
            scratch_shapes=[pltpu.VMEM(x.shape, x.dtype) for x in fetched]
            + [pltpu.VMEM(out[0], out[1]) for out in sent]
            + list(scratch)
            + [pltpu.SemaphoreType.DMA((max(1, fetch),)), pltpu.SemaphoreType.DMA((max(1, len(sent)),))],
            compiler_params=pltpu.CompilerParams(vmem_limit_bytes=24 * 1024 * 1024),
            name=name,
        )(*operands[:first], *[pltpu.with_memory_space_constraint(x, pltpu.HBM) for x in fetched])

    return run


def array(*shape, dtype=F32):
    return shape, dtype


def far(*shape, dtype=F32):
    return shape, dtype, True


def exchange(x):
    return lax.all_to_all(x, "tile", split_axis=0, concat_axis=0, tiled=True)


def deal(others, z):
    got = []
    for k, (shift, core) in enumerate(z.parts[1:]):
        pairs = [
            (s * z.devices + t, (s + shift) % z.samples * z.devices + (t ^ core))
            for s in range(z.samples)
            for t in range(z.devices)
        ]
        got.append(lax.ppermute(others[k], ("dp", "tile"), pairs))
    return got


def local(inputs, cotangent, w_first, w_second, w_down, edge_owner, corner_owner, neighbour_tile, seam_rotation):
    tiles_in, cot = inputs[0], cotangent[0]
    tiles, side, _, chan = tiles_in.shape
    z = Sizes(tiles, side, chan, lax.axis_size("tile"), lax.axis_size("dp"))
    scale = float(z.samples * z.devices * z.pixels) ** -0.5
    me = lax.axis_index("tile").astype(I32).reshape(1)
    sample = lax.axis_index("dp").astype(I32).reshape(1)
    half = side // 2
    down_pixels = half * half * tiles
    sent = array(z.devices, z.pair, chan, dtype=BF16)
    sent_far = far(z.devices, z.pair, chan, dtype=BF16)
    field, field16 = array(z.pixels, chan), array(z.pixels, chan, dtype=BF16)
    field16_far = far(z.pixels, chan, dtype=BF16)
    columns = array(z.column * side, 3 * chan, dtype=BF16)
    columns_far = far(z.column * side, 3 * chan, dtype=BF16)
    turned = array(9 * chan, chan, dtype=BF16)
    wide = vmem((side + 2) * z.line, 3 * chan, dtype=BF16)
    side_columns = (vmem(z.column * side, chan), vmem(z.column * side, chan))
    flat = vmem(z.pixels, chan)
    taps = vmem(9 * chan, chan)
    bind = functools.partial
    tables = (edge_owner.T, corner_owner.T, neighbour_tile.T, seam_rotation.T)
    others = len(z.parts) - 1

    (send,) = call(bind(pack_kernel, z), [sent_far], scalars=1, fetch=5, name="pack")(me, *tables, tiles_in)
    got = exchange(send)
    cot_rows = cot.transpose(1, 0, 2, 3).reshape(down_pixels, chan)
    index_col, pix_row, cell_row, back_second, turned_first, turned_second = call(
        bind(side_kernel, z),
        [
            array(z.sent + z.cells_up, LANES, dtype=I32),
            array(8, z.sent, dtype=I32),
            array(8, z.cells_up, dtype=I32),
            field,
            turned,
            turned,
        ],
        scalars=1,
        name="aside",
    )(me, *tables, cot_rows, w_down, w_first, w_second)
    send, hidden, columns_first = call(
        bind(first_kernel, z), [sent, field16, columns], side_columns, name="first"
    )(got, index_col, tiles_in, w_first)
    got = exchange(send)
    (slope_in,) = call(bind(again_kernel, z), [field], name="again")(columns_first, w_first)
    send, slope_second, hidden_second, columns_second = call(
        bind(second_kernel, z), [sent_far, field16_far, field16_far, columns_far], side_columns + (flat,), name="second"
    )(got, index_col, cell_row, hidden, w_second, turned_second, back_second)
    got = exchange(send)
    (inner,) = call(bind(inner_kernel, z), [field], (wide,), name="inner")(slope_second, turned_second)
    features, early_own, *early_other = call(
        bind(early_kernel, z, scale),
        [array(down_pixels, chan, dtype=BF16), array(z.early, chan)] + [array(z.early, chan, dtype=BF16)] * others,
        (taps, vmem(2 * z.samples * z.early, chan), flat, vmem(down_pixels, 4 * chan, dtype=BF16)),
        scalars=2,
        name="early",
    )(sample, me, columns_second, slope_second, hidden_second, cot_rows, w_down)
    features = features.reshape(half, tiles, half, chan).transpose(1, 0, 2, 3)
    early_got = deal(early_other, z)
    slope_first, late_own, *late_other = call(
        bind(slope_kernel, z, scale),
        [field16, array(z.late, chan)] + [array(z.late, chan, dtype=BF16)] * others,
        (taps,),
        scalars=2,
        name="slope",
    )(sample, me, got, pix_row, inner, slope_in, columns_first)
    late_got = deal(late_other, z)
    (send,) = call(bind(last_kernel, z), [sent], (flat,), name="last")(slope_first, turned_first, cell_row)
    (send,) = call(
        bind(join_kernel, z),
        [array(z.devices, z.pair + z.chunk, chan, dtype=BF16)],
        (vmem(z.devices * z.chunk, chan),),
        name="join",
    )(send, early_own, late_own, *early_got, *late_got)
    got = exchange(send)
    (inner,) = call(bind(inner_kernel, z), [field], (wide,), name="inner")(slope_first, turned_first)
    (chunk,) = call(bind(sum_kernel, z), [array(z.devices // 2, 2 * z.chunk, chan, dtype=BF16)], name="sum")(got)
    same_core = [list(range(core, z.devices, 2)) for core in range(2)]
    mine = lax.all_to_all(chunk, "tile", split_axis=0, concat_axis=0, tiled=True, axis_index_groups=same_core)
    (input_grad,) = call(bind(input_kernel, z), [array(tiles, side, side, chan)], name="input")(got, pix_row, inner)
    mine, input_grad = lax.optimization_barrier((mine, input_grad))
    other = lax.ppermute(mine, "tile", [(t, t ^ 1) for t in range(z.devices)])
    grad_first, grad_second, grad_down = call(
        bind(spread_kernel, z),
        [array(z.tap_rows, chan), array(z.tap_rows, chan), array(z.down_rows, chan)],
        scalars=1,
        name="spread",
    )(me, mine, other)
    return features[None], input_grad[None], grad_first, grad_second, grad_down


def solution(mesh):
    split = P("dp", "tile", None, None, None)
    return jax.shard_map(
        local,
        mesh=mesh,
        in_specs=(split, split, P(), P(), P(), P(), P(), P(), P()),
        out_specs=(split, split, P("dp", None), P("dp", None), P("dp", None)),
        check_vma=False,
    )
```

time: 104 us -> 90.2 us (0.87)
  local copies, waits for them, and re-layouts: 13.3 us -> 5.69 us
  blocking collectives: 35.7 us -> 28.3 us
  waiting for transfers between devices: 17.6 us -> 12.7 us
  starting transfers between devices: 18.3 us -> 22.5 us
  Pallas kernels: 17.6 us -> 19 us
    all_to_all x3 -> x2, waiting for transfers between devices: 15.9 us -> 4.27 us  [exchange(): return lax.all_to_all(x, 'tile', split_axis=0, concat_axis=0, tiled=True)]
    unnamed x72 -> x46, local copies, waits for them, and re-layouts: 12.6 us -> 5.01 us
    all_to_all x2, blocking collectives: 35.7 us -> 28.3 us  [exchange(): return lax.all_to_all(x, 'tile', split_axis=0, concat_axis=0, tiled=True)]
    all_to_all x0 -> x1, waiting for transfers between devices: none -> 4.73 us  [local(): lax.all_to_all(chunk, 'tile', split_axis=0, concat_axis=0, tiled=True, ax...]
    ppermute x2 -> x7, starting transfers between devices: 2.49 us -> 7.02 us  [the longest x6 5.14 us: deal(): got.append(lax.ppermute(others[k], ('dp', 'tile'), pairs))]
    all_to_all x3 -> x2, starting transfers between devices: 15.8 us -> 12.1 us  [exchange(): return lax.all_to_all(x, 'tile', split_axis=0, concat_axis=0, tiled=True)]
    all_to_all x0 -> x1, starting transfers between devices: none -> 3.4 us  [local(): lax.all_to_all(chunk, 'tile', split_axis=0, concat_axis=0, tiled=True, ax...]
    ppermute x2 -> x7, waiting for transfers between devices: 1.69 us -> 3.69 us  [the longest x6 3.27 us: deal(): got.append(lax.ppermute(others[k], ('dp', 'tile'), pairs))]
  transfers between devices with their start and end apart: 5 -> 10, of which waited for: 4 -> 6; matrix products, arithmetic and copies ran while one was open for 1% -> 1% of each run, Pallas kernels for 7% -> 10%
where the time goes in v1:
time: 90.2 us; the launch traced here: 89.2 us
  blocking collectives  28.3 us (31%)
  starting transfers between devices  22.5 us (25%)
  Pallas kernels  19 us (21%)
  waiting for transfers between devices  12.7 us (14%)
  local copies, waits for them, and re-layouts  5.69 us (6%)
  between operations  1 us (1%)
    all_to_all x2, blocking collectives, exchange(): return lax.all_to_all(x, 'tile', split_axis=0, concat_axis=0, tiled=True)  28.3 us
    pallas_call x14, Pallas kernels, run(): pl.pallas_call(kernel, out_shape=[pltpu.HBM(out[0], out[1]) if is_far els...  19 us
    all_to_all x2, starting transfers between devices, exchange(): return lax.all_to_all(x, 'tile', split_axis=0, concat_axis=0, tiled=True)  12.1 us
    ppermute x6, starting transfers between devices, deal(): got.append(lax.ppermute(others[k], ('dp', 'tile'), pairs))  5.14 us
    unnamed x46, local copies, waits for them, and re-layouts  5.01 us
    all_to_all x1, waiting for transfers between devices, local(): lax.all_to_all(chunk, 'tile', split_axis=0, concat_axis=0, tiled=True, ax...  4.73 us
    all_to_all x2, waiting for transfers between devices, exchange(): return lax.all_to_all(x, 'tile', split_axis=0, concat_axis=0, tiled=True)  4.27 us
    all_to_all x1, starting transfers between devices, local(): lax.all_to_all(chunk, 'tile', split_axis=0, concat_axis=0, tiled=True, ax...  3.4 us
  transfers between devices with their start and end apart: 10, of which 6 were waited for; matrix products, arithmetic and copies ran while one was open for 1% of the time, Pallas kernels for 10%

profile of v1, /device:TPU:1, one launch (start us, length us, event | category | flops | bytes accessed | tf_op | source)
XLA Modules:
  0.0 89.2 jit_solution(3461437657576042297)
XLA Ops:
  0.6 0.0 copy-start.1
  0.6 2.5 %pack.1 = bf16[16,48,128]{2,1,0:T(8,128)(2,1)} custom-call(s32[1]{0:T(128)} %bitcast.1.refs_0_.refs_1_, s32[4,256]{1,0:T(4,128)} %bitcast.27, s32[4,256]{1,0:T(4,128)} %bitcast.29, s32[8,256]{1,0:T(8,128)} %bitcast.23, s32[8,256]{1,0:T(8,128)} %bitcast.25, bf16[16,8,8,128]{3,2,1,0:T(8,128)(2,1)} %bitcast.18), custom_call_target="tpu_custom_call" | custom-call | tf_op jit(solution)/shard_map/pack/pallas_call | solution.py:493
  3.1 0.0 copy-start.22
  3.1 0.0 copy-start
  3.2 0.0 copy-start.18
  3.2 0.0 copy-start.19
  3.2 0.0 copy-start.20
  3.2 0.0 copy-start.21
  3.2 7.5 %all-to-all-start = ((bf16[16,48,128]{2,1,0:T(8,128)(2,1)}), bf16[16,48,128]{2,1,0:T(8,128)(2,1)S(1)}, u32[]{:S(2)}, u32[]{:S(2)}) async-start(bf16[16,48,128]{2,1,0:T(8,128)(2,1)} %pack.1), calls=%async_computation | async-start | bytes 393216 | tf_op jit(solution)/shard_map/all_to_all | solution.py:521
  10.7 0.0 copy-done.22
  10.8 0.0 copy-done.1
  10.8 0.0 copy-done
  10.8 0.8 copy-done.5
  11.6 1.2 %aside.1 = (s32[1408,128]{1,0:T(8,128)S(1)}, s32[8,768]{1,0:T(8,128)S(1)}, s32[8,640]{1,0:T(8,128)S(1)}, f32[1024,128]{1,0:T(8,128)S(1)}, bf16[1152,128]{1,0:T(8,128)(2,1)S(1)}, /*index=5*/bf16[1152,128]{1,0:T(8,128)(2,1)S(1)}) custom-call(s32[1]{0:T(128)} %bitcast.1.refs_0_.refs_1_, s32[4,256]{1,0:T(4,128)S(1)} %bitcast.28, s32[4,256]{1,0:T(4,128)S(1)} %bitcast.30, ...), custom_call_target="tpu_custom_call" | custom-call | tf_op jit(solution)/shard_map/aside/pallas_call | solution.py:493
  12.8 0.0 copy-start.6
  12.8 0.8 copy-done.6
  13.6 0.6 copy-done.11
  14.2 0.6 copy-done.13
  14.8 4.2 %all-to-all-done.refs_0_ = bf16[16,48,128]{2,1,0:T(8,128)(2,1)S(1)} async-done(((bf16[16,48,128]{2,1,0:T(8,128)(2,1)}), bf16[16,48,128]{2,1,0:T(8,128)(2,1)S(1)}, u32[]{:S(2)}, u32[]{:S(2)}) %all-to-all-start) | async-done | bytes 196640 | tf_op jit(solution)/shard_map/all_to_all | solution.py:521
  19.0 2.3 %first.1 = (bf16[16,48,128]{2,1,0:T(8,128)(2,1)S(1)}, bf16[1024,128]{1,0:T(8,128)(2,1)S(1)}, bf16[1280,384]{1,0:T(8,128)(2,1)S(1)}) custom-call(bf16[16,48,128]{2,1,0:T(8,128)(2,1)S(1)} %all-to-all-done.refs_0_, s32[1408,128]{1,0:T(8,128)S(1)} %get-tuple-element.33.refs_1_, bf16[16,8,8,128]{3,2,1,0:T(8,128)(2,1)S(1)} %bitcast.19, bf16[1152,128]{1,0:T(8,128)(2,1)S(1)} %copy-done), custom_call_target="tpu_custom_call" | custom-call | tf_op jit(solution)/shard_map/first/pallas_call | solution.py:493
  21.4 11.2 %all_to_all.25.refs_0_ = bf16[16,48,128]{2,1,0:T(8,128)(2,1)S(1)} all-to-all(bf16[16,48,128]{2,1,0:T(8,128)(2,1)S(1)} %get-tuple-element.34), channel_id=1, replica_groups=mesh['dp'=2,'tile'=16] {'tile'}, dimensions={0} | all-to-all | bytes 393216 | tf_op jit(solution)/shard_map/all_to_all | solution.py:521
  32.5 0.0 copy-done.14
  32.6 3.3 %second.1 = (bf16[16,48,128]{2,1,0:T(8,128)(2,1)}, bf16[1024,128]{1,0:T(8,128)(2,1)}, bf16[1024,128]{1,0:T(8,128)(2,1)}, bf16[1280,384]{1,0:T(8,128)(2,1)}) custom-call(bf16[16,48,128]{2,1,0:T(8,128)(2,1)S(1)} %all_to_all.25.refs_0_, s32[1408,128]{1,0:T(8,128)S(1)} %get-tuple-element.33.refs_1_, s32[8,640]{1,0:T(8,128)S(1)} %copy-done.14, ...), custom_call_target="tpu_custom_call" | custom-call | tf_op jit(solution)/shard_map/second/pallas_call | solution.py:493
  35.9 0.0 copy-start.3
  35.9 4.6 %all-to-all-start.2 = ((bf16[16,48,128]{2,1,0:T(8,128)(2,1)}), bf16[16,48,128]{2,1,0:T(8,128)(2,1)S(1)}, u32[]{:S(2)}, u32[]{:S(2)}) async-start(bf16[16,48,128]{2,1,0:T(8,128)(2,1)} %get-tuple-element.43), calls=%async_computation.2 | async-start | bytes 393216 | tf_op jit(solution)/shard_map/all_to_all | solution.py:521
  40.5 1.2 %copy-done.4 = bf16[1280,384]{1,0:T(8,128)(2,1)S(1)} copy-done((bf16[1280,384]{1,0:T(8,128)(2,1)S(1)}, bf16[1280,384]{1,0:T(8,128)(2,1)}, u32[]{:S(2)}) %copy-start.4) | copy-done | bytes 983064
  41.7 0.9 %copy-done.8 = bf16[1024,128]{1,0:T(8,128)(2,1)S(1)} copy-done((bf16[1024,128]{1,0:T(8,128)(2,1)S(1)}, bf16[1024,128]{1,0:T(8,128)(2,1)}, u32[]{:S(2)}) %copy-start.8) | copy-done | bytes 262168
  42.7 1.8 %early.1 = (bf16[256,128]{1,0:T(8,128)(2,1)S(1)}, f32[416,128]{1,0:T(8,128)S(1)}, bf16[416,128]{1,0:T(8,128)(2,1)}, bf16[416,128]{1,0:T(8,128)(2,1)}, bf16[416,128]{1,0:T(8,128)(2,1)}) custom-call(s32[1]{0:T(128)} %bitcast.refs_0_, s32[1]{0:T(128)} %bitcast.1.refs_0_.refs_1_, bf16[1280,384]{1,0:T(8,128)(2,1)S(1)} %copy-done.4, ...), custom_call_target="tpu_custom_call" | custom-call | tf_op jit(solution)/shard_map/early/pallas_call | solution.py:493
  44.5 0.0 copy-start.9
  44.5 0.0 copy-start.16
  44.5 0.3 collective-permute-start
  44.8 1.2 %collective-permute-start.1 = (bf16[416,128]{1,0:T(8,128)(2,1)}, bf16[416,128]{1,0:T(8,128)(2,1)S(1)}, u32[]{:S(2)}, u32[]{:S(2)}) collective-permute-start(bf16[416,128]{1,0:T(8,128)(2,1)} %get-tuple-element.51), channel_id=1, source_target_pairs={{0,16},{1,17},{2,18},{3,19},{4,20},{5,21},{6,22},{7,23},{8,24},{9,... | collective-permute-start | bytes 319496 | tf_op jit(solution)/shard_map/ppermute | solution.py:532
  46.0 0.7 collective-permute-start.2
  46.7 0.9 again.1.refs_5_
  47.6 0.0 copy-done.9
  47.6 0.0 copy-done.16
  47.6 0.0 copy-start.12
  47.6 0.8 inner.2.refs_4_
  48.4 0.1 all-to-all-done.2.refs_2_
  48.5 0.0 copy-done.12
  48.5 1.6 %slope.1 = (bf16[1024,128]{1,0:T(8,128)(2,1)S(1)}, f32[288,128]{1,0:T(8,128)S(1)}, bf16[288,128]{1,0:T(8,128)(2,1)S(1)}, bf16[288,128]{1,0:T(8,128)(2,1)S(1)}, bf16[288,128]{1,0:T(8,128)(2,1)S(1)}) custom-call(s32[1]{0:T(128)} %bitcast.refs_0_, s32[1]{0:T(128)} %bitcast.1.refs_0_.refs_1_, bf16[16,48,128]{2,1,0:T(8,128)(2,1)S(1)} %all-to-all-done.2.refs_2_, ...), custom_call_target="tpu_custom_call" | custom-call | tf_op jit(solution)/shard_map/slope/pallas_call | solution.py:493
  50.1 1.2 %collective-permute-start.3 = (bf16[288,128]{1,0:T(8,128)(2,1)S(1)}, bf16[288,128]{1,0:T(8,128)(2,1)S(1)}, u32[]{:S(2)}, u32[]{:S(2)}) collective-permute-start(bf16[288,128]{1,0:T(8,128)(2,1)S(1)} %get-tuple-element.53), channel_id=1, source_target_pairs={{0,1},{1,0},{2,3},{3,2},{4,5},{5,4},{6,7},{7,6},{8,9},{9,8},{10,11... | collective-permute-start | bytes 221192 | tf_op jit(solution)/shard_map/ppermute | solution.py:532
  51.4 1.2 %collective-permute-start.4 = (bf16[288,128]{1,0:T(8,128)(2,1)S(1)}, bf16[288,128]{1,0:T(8,128)(2,1)S(1)}, u32[]{:S(2)}, u32[]{:S(2)}) collective-permute-start(bf16[288,128]{1,0:T(8,128)(2,1)S(1)} %get-tuple-element.54), channel_id=1, source_target_pairs={{0,16},{1,17},{2,18},{3,19},{4,20},{5,21},{6,22},{7,23},{8,24},{9,... | collective-permute-start | bytes 221192 | tf_op jit(solution)/shard_map/ppermute | solution.py:532
  52.6 0.0 collective-permute-done.refs_3_
  52.6 0.5 collective-permute-start.5
  53.1 0.6 last.1.refs_0_
  53.7 0.0 collective-permute-done.1.refs_4_
  53.7 0.0 collective-permute-done.2.refs_5_
  53.8 0.0 collective-permute-done.3.refs_6_
  53.8 1.4 %collective-permute-done.4.refs_7_ = bf16[288,128]{1,0:T(8,128)(2,1)S(1)} collective-permute-done((bf16[288,128]{1,0:T(8,128)(2,1)S(1)}, bf16[288,128]{1,0:T(8,128)(2,1)S(1)}, u32[]{:S(2)}, u32[]{:S(2)}) %collective-permute-start.4) | collective-permute-done | bytes 73760 | tf_op jit(solution)/shard_map/ppermute | solution.py:532
  55.2 1.8 %collective-permute-done.5.refs_8_ = bf16[288,128]{1,0:T(8,128)(2,1)S(1)} collective-permute-done((bf16[288,128]{1,0:T(8,128)(2,1)S(1)}, bf16[288,128]{1,0:T(8,128)(2,1)S(1)}, u32[]{:S(2)}, u32[]{:S(2)}) %collective-permute-start.5) | collective-permute-done | bytes 73760 | tf_op jit(solution)/shard_map/ppermute | solution.py:532
  57.0 0.0 copy-done.10
  57.0 0.1 join.1
  57.2 17.1 %all_to_all.26.refs_0_ = bf16[16,96,128]{2,1,0:T(8,128)(2,1)S(1)} all-to-all(bf16[16,96,128]{2,1,0:T(8,128)(2,1)S(1)} %join.1), channel_id=1, replica_groups=mesh['dp'=2,'tile'=16] {'tile'}, dimensions={0} | all-to-all | bytes 786432 | tf_op jit(solution)/shard_map/all_to_all | solution.py:521
  74.3 0.7 sum.1
  75.0 3.4 %all-to-all-start.4 = ((bf16[8,96,128]{2,1,0:T(8,128)(2,1)}), bf16[8,96,128]{2,1,0:T(8,128)(2,1)S(1)}, u32[]{:S(2)}, u32[]{:S(2)}) async-start(bf16[8,96,128]{2,1,0:T(8,128)(2,1)} %sum.1), calls=%async_computation.4 | async-start | bytes 393216 | tf_op jit(solution)/shard_map/all_to_all | solution.py:614
  78.4 0.8 inner.3.refs_2_
  79.3 0.0 copy-start.17
  79.3 1.4 %input.1 = f32[16,8,8,128]{3,2,1,0:T(8,128)} custom-call(bf16[16,96,128]{2,1,0:T(8,128)(2,1)S(1)} %all_to_all.26.refs_0_, s32[8,768]{1,0:T(8,128)S(1)} %copy-done.12, f32[1024,128]{1,0:T(8,128)S(1)} %inner.3.refs_2_), custom_call_target="tpu_custom_call" | custom-call | tf_op jit(solution)/shard_map/input/pallas_call | solution.py:493
  80.7 4.7 %all-to-all-done.4.refs_1_ = bf16[8,96,128]{2,1,0:T(8,128)(2,1)S(1)} async-done(((bf16[8,96,128]{2,1,0:T(8,128)(2,1)}), bf16[8,96,128]{2,1,0:T(8,128)(2,1)S(1)}, u32[]{:S(2)}, u32[]{:S(2)}) %all-to-all-start.4) | async-done | bytes 196640 | tf_op jit(solution)/shard_map/all_to_all | solution.py:614
  85.4 1.9 %collective-permute-start.6 = (bf16[8,96,128]{2,1,0:T(8,128)(2,1)S(1)}, bf16[8,96,128]{2,1,0:T(8,128)(2,1)S(1)}, u32[]{:S(2)}, u32[]{:S(2)}) collective-permute-start(bf16[8,96,128]{2,1,0:T(8,128)(2,1)S(1)} %all-to-all-done.4.refs_1_), channel_id=1, source_target_pairs={{0,1},{1,0},{2,3},{3,2},{4,5},{5,4},{6,7},{7,6},{8,9},{9,8},{10,11... | collective-permute-start | bytes 589832 | tf_op jit(solution)/shard_map/ppermute | solution.py:617
  87.3 0.7 copy.17
  87.9 0.4 collective-permute-done.6.refs_2_
  88.3 0.9 spread.1
  (20 shorter events, 0.1 us)
Async XLA Ops:
  0.6 10.1 %copy-start.1 = (bf16[1152,128]{1,0:T(8,128)(2,1)S(1)}, bf16[1152,128]{1,0:T(8,128)(2,1)}, u32[]{:S(2)}) copy-start(bf16[1152,128]{1,0:T(8,128)(2,1)} %refs_4_.1) | copy-start | bytes 884740
  3.1 7.6 %copy-start.22 = (bf16[1,16,4,4,128]{4,3,2,1,0:T(4,128)(2,1)S(1)}, bf16[1,16,4,4,128]{4,3,2,1,0:T(4,128)(2,1)}, u32[]{:S(2)}) copy-start(bf16[1,16,4,4,128]{4,3,2,1,0:T(4,128)(2,1)} %param.10) | copy-start | bytes 196612
  3.1 7.6 %copy-start = (bf16[1152,128]{1,0:T(8,128)(2,1)S(1)}, bf16[1152,128]{1,0:T(8,128)(2,1)}, u32[]{:S(2)}) copy-start(bf16[1152,128]{1,0:T(8,128)(2,1)} %refs_1_.1) | copy-start | bytes 884740
  3.2 7.6 %copy-start.18 = (s32[256,8]{0,1:T(8,128)S(1)}, s32[256,8]{0,1:T(8,128)}, u32[]{:S(2)}) copy-start(s32[256,8]{0,1:T(8,128)} %param.16) | copy-start | bytes 24580
  3.2 7.6 %copy-start.19 = (s32[256,8]{0,1:T(8,128)S(1)}, s32[256,8]{0,1:T(8,128)}, u32[]{:S(2)}) copy-start(s32[256,8]{0,1:T(8,128)} %param.17) | copy-start | bytes 24580
  3.2 7.6 %copy-start.20 = (s32[256,4]{0,1:T(4,128)S(1)}, s32[256,4]{0,1:T(4,128)}, u32[]{:S(2)}) copy-start(s32[256,4]{0,1:T(4,128)} %param.14) | copy-start | bytes 12292
  3.2 7.6 %copy-start.21 = (s32[256,4]{0,1:T(4,128)S(1)}, s32[256,4]{0,1:T(4,128)}, u32[]{:S(2)}) copy-start(s32[256,4]{0,1:T(4,128)} %param.15) | copy-start | bytes 12292
  3.2 15.8 %all-to-all-start = ((bf16[16,48,128]{2,1,0:T(8,128)(2,1)}), bf16[16,48,128]{2,1,0:T(8,128)(2,1)S(1)}, u32[]{:S(2)}, u32[]{:S(2)}) async-start(bf16[16,48,128]{2,1,0:T(8,128)(2,1)} %pack.1), calls=%async_computation | async-start | bytes 393216 | tf_op jit(solution)/shard_map/all_to_all | solution.py:521
  10.7 0.9 %copy-start.5 = (bf16[512,128]{1,0:T(8,128)(2,1)S(1)}, bf16[512,128]{1,0:T(8,128)(2,1)}, u32[]{:S(2)}) copy-start(bf16[512,128]{1,0:T(8,128)(2,1)} %refs_6_.3) | copy-start | bytes 393220
  11.6 7.4 %copy-start.2 = (bf16[1,16,8,8,128]{4,3,2,1,0:T(8,128)(2,1)S(1)}, bf16[1,16,8,8,128]{4,3,2,1,0:T(8,128)(2,1)}, u32[]{:S(2)}) copy-start(bf16[1,16,8,8,128]{4,3,2,1,0:T(8,128)(2,1)} %param.9) | copy-start | bytes 786436
  12.8 0.8 copy-start.6
  13.6 0.6 copy-start.11
  14.2 0.6 copy-start.13
  19.0 13.5 %copy-start.7 = (f32[1024,128]{1,0:T(8,128)S(1)}, f32[1024,128]{1,0:T(8,128)}, u32[]{:S(2)}) copy-start(f32[1024,128]{1,0:T(8,128)} %copy-done.6) | copy-start | bytes 1572868
  21.3 11.2 %copy-start.14 = (s32[8,640]{1,0:T(8,128)S(1)}, s32[8,640]{1,0:T(8,128)}, u32[]{:S(2)}) copy-start(s32[8,640]{1,0:T(8,128)} %copy-done.13) | copy-start | bytes 61444
  35.9 4.6 %copy-start.3 = (bf16[1024,128]{1,0:T(8,128)(2,1)S(1)}, bf16[1024,128]{1,0:T(8,128)(2,1)}, u32[]{:S(2)}) copy-start(bf16[1024,128]{1,0:T(8,128)(2,1)} %get-tuple-element.40.refs_3_.refs_0_) | copy-start | bytes 786436
  35.9 12.6 %all-to-all-start.2 = ((bf16[16,48,128]{2,1,0:T(8,128)(2,1)}), bf16[16,48,128]{2,1,0:T(8,128)(2,1)S(1)}, u32[]{:S(2)}, u32[]{:S(2)}) async-start(bf16[16,48,128]{2,1,0:T(8,128)(2,1)} %get-tuple-element.43), calls=%async_computation.2 | async-start | bytes 393216 | tf_op jit(solution)/shard_map/all_to_all | solution.py:521
  40.5 1.2 %copy-start.4 = (bf16[1280,384]{1,0:T(8,128)(2,1)S(1)}, bf16[1280,384]{1,0:T(8,128)(2,1)}, u32[]{:S(2)}) copy-start(bf16[1280,384]{1,0:T(8,128)(2,1)} %get-tuple-element.39.refs_2_) | copy-start | bytes 2949124
  41.7 0.9 %copy-start.8 = (bf16[1024,128]{1,0:T(8,128)(2,1)S(1)}, bf16[1024,128]{1,0:T(8,128)(2,1)}, u32[]{:S(2)}) copy-start(bf16[1024,128]{1,0:T(8,128)(2,1)} %get-tuple-element.41.refs_4_) | copy-start | bytes 786436
  44.5 3.1 %copy-start.9 = (f32[416,128]{1,0:T(8,128)}, f32[416,128]{1,0:T(8,128)S(1)}, u32[]{:S(2)}) copy-start(f32[416,128]{1,0:T(8,128)S(1)} %get-tuple-element.48.refs_1_) | copy-start | bytes 638980
  44.5 3.1 %copy-start.16 = (bf16[256,128]{1,0:T(8,128)(2,1)}, bf16[256,128]{1,0:T(8,128)(2,1)S(1)}, u32[]{:S(2)}) copy-start(bf16[256,128]{1,0:T(8,128)(2,1)S(1)} %get-tuple-element.42) | copy-start | bytes 196612
  44.5 8.1 %collective-permute-start = (bf16[416,128]{1,0:T(8,128)(2,1)}, bf16[416,128]{1,0:T(8,128)(2,1)S(1)}, u32[]{:S(2)}, u32[]{:S(2)}) collective-permute-start(bf16[416,128]{1,0:T(8,128)(2,1)} %get-tuple-element.50), channel_id=1, source_target_pairs={{0,1},{1,0},{2,3},{3,2},{4,5},{5,4},{6,7},{7,6},{8,9},{9,8},{10,11... | collective-permute-start | bytes 319496 | tf_op jit(solution)/shard_map/ppermute | solution.py:532
  44.8 8.9 %collective-permute-start.1 = (bf16[416,128]{1,0:T(8,128)(2,1)}, bf16[416,128]{1,0:T(8,128)(2,1)S(1)}, u32[]{:S(2)}, u32[]{:S(2)}) collective-permute-start(bf16[416,128]{1,0:T(8,128)(2,1)} %get-tuple-element.51), channel_id=1, source_target_pairs={{0,16},{1,17},{2,18},{3,19},{4,20},{5,21},{6,22},{7,23},{8,24},{9,... | collective-permute-start | bytes 319496 | tf_op jit(solution)/shard_map/ppermute | solution.py:532
  46.0 7.7 %collective-permute-start.2 = (bf16[416,128]{1,0:T(8,128)(2,1)}, bf16[416,128]{1,0:T(8,128)(2,1)S(1)}, u32[]{:S(2)}, u32[]{:S(2)}) collective-permute-start(bf16[416,128]{1,0:T(8,128)(2,1)} %get-tuple-element.52), channel_id=1, source_target_pairs={{0,17},{1,16},{2,19},{3,18},{4,21},{5,20},{6,23},{7,22},{8,25},{9,... | collective-permute-start | bytes 319496 | tf_op jit(solution)/shard_map/ppermute | solution.py:532
  47.6 0.9 %copy-start.12 = (s32[8,768]{1,0:T(8,128)S(1)}, s32[8,768]{1,0:T(8,128)}, u32[]{:S(2)}) copy-start(s32[8,768]{1,0:T(8,128)} %copy-done.11) | copy-start | bytes 73732
  48.5 4.5 %copy-start.15 = (s32[8,640]{1,0:T(8,128)S(1)}, s32[8,640]{1,0:T(8,128)}, u32[]{:S(2)}) copy-start(s32[8,640]{1,0:T(8,128)} %copy-done.13) | copy-start | bytes 61444
  50.1 3.6 %collective-permute-start.3 = (bf16[288,128]{1,0:T(8,128)(2,1)S(1)}, bf16[288,128]{1,0:T(8,128)(2,1)S(1)}, u32[]{:S(2)}, u32[]{:S(2)}) collective-permute-start(bf16[288,128]{1,0:T(8,128)(2,1)S(1)} %get-tuple-element.53), channel_id=1, source_target_pairs={{0,1},{1,0},{2,3},{3,2},{4,5},{5,4},{6,7},{7,6},{8,9},{9,8},{10,11... | collective-permute-start | bytes 221192 | tf_op jit(solution)/shard_map/ppermute | solution.py:532
  51.4 3.8 %collective-permute-start.4 = (bf16[288,128]{1,0:T(8,128)(2,1)S(1)}, bf16[288,128]{1,0:T(8,128)(2,1)S(1)}, u32[]{:S(2)}, u32[]{:S(2)}) collective-permute-start(bf16[288,128]{1,0:T(8,128)(2,1)S(1)} %get-tuple-element.54), channel_id=1, source_target_pairs={{0,16},{1,17},{2,18},{3,19},{4,20},{5,21},{6,22},{7,23},{8,24},{9,... | collective-permute-start | bytes 221192 | tf_op jit(solution)/shard_map/ppermute | solution.py:532
  52.6 4.4 %collective-permute-start.5 = (bf16[288,128]{1,0:T(8,128)(2,1)S(1)}, bf16[288,128]{1,0:T(8,128)(2,1)S(1)}, u32[]{:S(2)}, u32[]{:S(2)}) collective-permute-start(bf16[288,128]{1,0:T(8,128)(2,1)S(1)} %get-tuple-element.55), channel_id=1, source_target_pairs={{0,17},{1,16},{2,19},{3,18},{4,21},{5,20},{6,23},{7,22},{8,25},{9,... | collective-permute-start | bytes 221192 | tf_op jit(solution)/shard_map/ppermute | solution.py:532
  53.1 4.0 %copy-start.10 = (f32[416,128]{1,0:T(8,128)S(1)}, f32[416,128]{1,0:T(8,128)}, u32[]{:S(2)}) copy-start(f32[416,128]{1,0:T(8,128)} %copy-done.9) | copy-start | bytes 638980
  75.0 10.4 %all-to-all-start.4 = ((bf16[8,96,128]{2,1,0:T(8,128)(2,1)}), bf16[8,96,128]{2,1,0:T(8,128)(2,1)S(1)}, u32[]{:S(2)}, u32[]{:S(2)}) async-start(bf16[8,96,128]{2,1,0:T(8,128)(2,1)} %sum.1), calls=%async_computation.4 | async-start | bytes 393216 | tf_op jit(solution)/shard_map/all_to_all | solution.py:614
  79.3 8.0 %copy-start.17 = (bf16[256,128]{1,0:T(8,128)(2,1)S(1)}, bf16[256,128]{1,0:T(8,128)(2,1)}, u32[]{:S(2)}) copy-start(bf16[256,128]{1,0:T(8,128)(2,1)} %copy-done.16) | copy-start | bytes 196612
  85.4 3.0 %collective-permute-start.6 = (bf16[8,96,128]{2,1,0:T(8,128)(2,1)S(1)}, bf16[8,96,128]{2,1,0:T(8,128)(2,1)S(1)}, u32[]{:S(2)}, u32[]{:S(2)}) collective-permute-start(bf16[8,96,128]{2,1,0:T(8,128)(2,1)S(1)} %all-to-all-done.4.refs_1_), channel_id=1, source_target_pairs={{0,1},{1,0},{2,3},{3,2},{4,5},{5,4},{6,7},{7,6},{8,9},{9,8},{10,11... | collective-permute-start | bytes 589832 | tf_op jit(solution)/shard_map/ppermute | solution.py:617

commit v2 on v1

--- a/solution.py
+++ b/solution.py
@@ -21,7 +21,7 @@
         self.pixels = side * self.line
         self.column = (side + 2) * tiles
         self.cells = 2 * self.line + 2 * self.column
-        self.cells_up = -(-self.cells // LANES) * LANES
+        self.cells_up = -(-self.cells // (2 * LANES)) * 2 * LANES
         self.tap_rows = 9 * chan // samples
         self.down_rows = 4 * chan // samples
         self.late = self.tap_rows // 2
@@ -51,6 +51,14 @@
     rows = index.shape[0]
     lane = iota((rows, LANES), 1)
     return jnp.concatenate([flag(index == lane + at) for at in range(0, width, LANES)], axis=1)
+
+
+def gather(index, source):
+    half, chan = source.shape[0] // 2, source.shape[1]
+    source = source.astype(BF16)
+    right = index >= half
+    wide = mm(pick_rows(jnp.where(right, index - half, index), half), jnp.concatenate([source[:half], source[half:]], axis=1))
+    return jnp.where(right, wide[:, chan:], wide[:, :chan])
 
 
 def pick_columns(index, height):
@@ -149,34 +157,32 @@
     return jnp.transpose(jnp.broadcast_to(index.astype(F32), (LANES, index.shape[1]))).astype(I32)
 
 
-def as_row(index):
-    return jnp.transpose(index.astype(F32))[0:8].astype(I32)
-
-
 def pack_kernel(z, me_ref, eo_ref, co_ref, ids_ref, turn_ref, x_ref, send_ref):
     owners = jnp.concatenate([eo_ref[...], co_ref[...]], axis=0)
     index = sender_index(me_ref[0], owners, ids_ref[...], turn_ref[...], z)
     pixels = row_first(x_ref[...]).reshape(z.pixels, z.chan)
-    send_ref[...] = mm(pick_rows(as_column(index), z.pixels), pixels).astype(BF16).reshape(send_ref.shape)
+    send_ref[...] = gather(as_column(index), pixels).astype(BF16).reshape(send_ref.shape)
 
 
 def side_kernel(
     z, me_ref, eo_ref, co_ref, ids_ref, turn_ref, cot_ref, wd_ref, w1_ref, w2_ref,
-    column_ref, pix_row_ref, cell_row_ref, back_ref, t1_ref, t2_ref,
+    table_ref, back_ref, t1_ref, t2_ref,
 ):
     me = me_ref[0]
     owners = jnp.concatenate([eo_ref[...], co_ref[...]], axis=0)
     index = sender_index(me, owners, ids_ref[...], turn_ref[...], z)
-    column_ref[: z.sent, :] = as_column(index)
-    pix_row_ref[...] = jnp.broadcast_to(index, pix_row_ref.shape)
+    table_ref[0:8, : z.sent] = jnp.broadcast_to(index, (8, z.sent))
     shape = (z.tiles, z.devices * z.tiles)
     mine = flag(iota(shape, 1) == iota(shape, 0) + me * z.tiles)
     own = lax.dot_general(
         mine, owners.astype(F32).astype(BF16), (((1,), (1,)), ((), ())), preferred_element_type=F32
     )
     index = receiver_index(own.astype(I32), z)
-    column_ref[z.sent :, :] = index
-    cell_row_ref[...] = as_row(index)
+    table_ref[8:16, : z.cells_up] = jnp.transpose(index.astype(F32))[0:8].astype(I32)
+    cell = iota((16, z.cells_up), 1) + 1
+    digits = jnp.where(iota((16, z.cells_up), 0) < 8, cell >> 4, cell & 15).astype(F32)
+    found = mm(digits, pick_rows(index, z.sent))
+    table_ref[16:24, : z.sent] = jnp.broadcast_to(found[0:1] * 16.0 + found[8:9] - 1.0, (8, z.sent)).astype(I32)
     chan, half = z.chan, z.side // 2
     for taps, out in ((w1_ref, t1_ref), (w2_ref, t2_ref)):
         for tap in range(9):
@@ -193,7 +199,7 @@
 
 
 def padded_columns(z, center, arrived, index, west_ref, east_ref, out_ref):
-    rims = mm(pick_rows(index, z.sent), arrived)
+    rims = gather(index, arrived)
     north, south = rims[: z.line], rims[z.line : 2 * z.line]
     at = 2 * z.line
     west_ref[pl.ds(0, z.column, stride=z.side), :] = rims[at : at + z.column]
@@ -228,10 +234,10 @@
 
 def first_kernel(z, got_ref, index_ref, x_ref, w_ref, send_ref, hidden_ref, columns_ref, west_ref, east_ref):
     center = row_first(x_ref[...]).reshape(z.pixels, z.chan)
-    padded_columns(z, center, got_ref[...].reshape(z.sent, z.chan), index_ref[z.sent :, :], west_ref, east_ref, columns_ref)
+    padded_columns(z, center, got_ref[...].reshape(z.sent, z.chan), as_column(index_ref[8:9, : z.cells_up]), west_ref, east_ref, columns_ref)
     v = conv(z, columns_ref, w_ref)
     hidden = (v / (1.0 + jnp.exp(-v))).astype(BF16)
-    send_ref[...] = mm(pick_rows(index_ref[: z.sent, :], z.pixels), hidden).astype(BF16).reshape(send_ref.shape)
+    send_ref[...] = gather(as_column(index_ref[0:1, : z.sent]), hidden).astype(BF16).reshape(send_ref.shape)
     hidden_ref[...] = hidden
 
 
@@ -290,11 +296,11 @@
 
 
 def second_kernel(
-    z, got_ref, index_ref, cell_row_ref, hidden_ref, w_ref, turned_ref, back_ref,
+    z, got_ref, index_ref, hidden_ref, w_ref, turned_ref, back_ref,
     send_ref, slope_ref, out_ref, columns_ref, west_ref, east_ref, scratch_ref,
 ):
     center = hidden_ref[...].astype(F32)
-    padded_columns(z, center, got_ref[...].reshape(z.sent, z.chan), index_ref[z.sent :, :], west_ref, east_ref, columns_ref)
+    padded_columns(z, center, got_ref[...].reshape(z.sent, z.chan), as_column(index_ref[8:9, : z.cells_up]), west_ref, east_ref, columns_ref)
     push(columns_ref)
     v = conv(z, columns_ref, w_ref)
     s = 1.0 / (1.0 + jnp.exp(-v))
@@ -304,13 +310,14 @@
     slope_ref[...] = slope
     push(slope_ref)
     rims = rims_back(z, slope.astype(F32), turned_ref, scratch_ref)
-    send_ref[...] = mm(pick_columns(cell_row_ref[0:1, :], z.sent), rims).astype(BF16).reshape(send_ref.shape)
+    send_ref[...] = gather(as_column(index_ref[16:17, : z.sent]), rims).astype(BF16).reshape(send_ref.shape)
 
 
 def tap_products(z, columns_ref, slope, scale, total_ref):
+    turned = jnp.transpose(slope.astype(F32)).astype(BF16)
     for p in range(3):
-        part = mm_t(columns_ref[p * z.line : p * z.line + z.pixels, :], slope)
-        total_ref[3 * p * z.chan : 3 * (p + 1) * z.chan, :] = part * scale
+        part = jnp.dot(turned, columns_ref[p * z.line : p * z.line + z.pixels, :], preferred_element_type=F32)
+        total_ref[3 * p * z.chan : 3 * (p + 1) * z.chan, :] = jnp.transpose(part * scale)
 
 
 def deal_parts(z, sample_ref, me_ref, source_ref, own_ref, other_refs):
@@ -358,26 +365,32 @@
     slope_ref, own_ref, *refs,
 ):
     other_refs, total_ref = refs[:-1], refs[-1]
-    back = inner_ref[...] + mm(pick_columns(pix_row_ref[0:1, :], z.pixels), got_ref[...].reshape(z.sent, z.chan))
+    back = inner_ref[...] + mm(pick_columns(pix_row_ref[0:1, : z.sent], z.pixels), got_ref[...].reshape(z.sent, z.chan))
     slope = (back * slope_in_ref[...]).astype(BF16)
     slope_ref[...] = slope
     tap_products(z, columns_ref, slope, scale, total_ref)
     deal_parts(z, sample_ref, me_ref, total_ref, own_ref, other_refs)
 
 
-def last_kernel(z, slope_ref, turned_ref, cell_row_ref, send_ref, scratch_ref):
+def last_kernel(z, slope_ref, turned_ref, index_ref, send_ref, scratch_ref):
     rims = rims_back(z, slope_ref[...].astype(F32), turned_ref, scratch_ref)
-    send_ref[...] = mm(pick_columns(cell_row_ref[0:1, :], z.sent), rims).astype(BF16).reshape(send_ref.shape)
+    send_ref[...] = gather(as_column(index_ref[16:17, : z.sent]), rims).astype(BF16).reshape(send_ref.shape)
+
+
+def gain_kernel(own_ref, *refs):
+    others, out_ref = refs[:-1], refs[-1]
+    total = own_ref[...]
+    for other in others:
+        total = total + other[...].astype(F32)
+    out_ref[...] = total
 
 
 def join_kernel(z, rim_ref, early_ref, late_ref, *refs):
-    others = len(z.parts) - 1
-    send_ref, total_ref = refs[2 * others :]
-    early, late = early_ref[...], late_ref[...]
-    for k in range(others):
-        early = early + refs[k][...].astype(F32)
-        late = late + refs[others + k][...].astype(F32)
-    total_ref[: z.early, :] = early
+    others, (send_ref, total_ref) = refs[:-2], refs[-2:]
+    late = late_ref[...]
+    for other in others:
+        late = late + other[...].astype(F32)
+    total_ref[: z.early, :] = early_ref[...]
     total_ref[z.early : z.early + z.late, :] = late
     spare = z.devices * z.chunk - z.early - z.late
     if spare:
@@ -400,7 +413,7 @@
 
 def input_kernel(z, got_ref, pix_row_ref, inner_ref, out_ref):
     arrived = got_ref[:, : z.pair, :].reshape(z.sent, z.chan)
-    total = inner_ref[...] + mm(pick_columns(pix_row_ref[0:1, :], z.pixels), arrived)
+    total = inner_ref[...] + mm(pick_columns(pix_row_ref[0:1, : z.sent], z.pixels), arrived)
     for r in range(z.side):
         out_ref[:, r] = total[r * z.line : (r + 1) * z.line].reshape(z.tiles, z.side, z.chan)
 
@@ -560,12 +573,10 @@
     (send,) = call(bind(pack_kernel, z), [sent_far], scalars=1, fetch=5, name="pack")(me, *tables, tiles_in)
     got = exchange(send)
     cot_rows = cot.transpose(1, 0, 2, 3).reshape(down_pixels, chan)
-    index_col, pix_row, cell_row, back_second, turned_first, turned_second = call(
+    index, back_second, turned_first, turned_second = call(
         bind(side_kernel, z),
         [
-            array(z.sent + z.cells_up, LANES, dtype=I32),
-            array(8, z.sent, dtype=I32),
-            array(8, z.cells_up, dtype=I32),
+            array(24, max(z.sent, z.cells_up), dtype=I32),
             field,
             turned,
             turned,
@@ -575,12 +586,12 @@
     )(me, *tables, cot_rows, w_down, w_first, w_second)
     send, hidden, columns_first = call(
         bind(first_kernel, z), [sent, field16, columns], side_columns, name="first"
-    )(got, index_col, tiles_in, w_first)
+    )(got, index, tiles_in, w_first)
     got = exchange(send)
     (slope_in,) = call(bind(again_kernel, z), [field], name="again")(columns_first, w_first)
     send, slope_second, hidden_second, columns_second = call(
-        bind(second_kernel, z), [sent_far, field16_far, field16_far, columns_far], side_columns + (flat,), name="second"
-    )(got, index_col, cell_row, hidden, w_second, turned_second, back_second)
+        bind(second_kernel, z), [sent_far, field16, field16, columns_far], side_columns + (flat,), name="second"
+    )(got, index, hidden, w_second, turned_second, back_second)
     got = exchange(send)
     (inner,) = call(bind(inner_kernel, z), [field], (wide,), name="inner")(slope_second, turned_second)
     features, early_own, *early_other = call(
@@ -591,29 +602,29 @@
         name="early",
     )(sample, me, columns_second, slope_second, hidden_second, cot_rows, w_down)
     features = features.reshape(half, tiles, half, chan).transpose(1, 0, 2, 3)
-    early_got = deal(early_other, z)
+    (early,) = call(gain_kernel, [array(z.early, chan)], name="gain")(early_own, *deal(early_other, z))
     slope_first, late_own, *late_other = call(
         bind(slope_kernel, z, scale),
         [field16, array(z.late, chan)] + [array(z.late, chan, dtype=BF16)] * others,
         (taps,),
         scalars=2,
         name="slope",
-    )(sample, me, got, pix_row, inner, slope_in, columns_first)
+    )(sample, me, got, index, inner, slope_in, columns_first)
     late_got = deal(late_other, z)
-    (send,) = call(bind(last_kernel, z), [sent], (flat,), name="last")(slope_first, turned_first, cell_row)
+    (send,) = call(bind(last_kernel, z), [sent], (flat,), name="last")(slope_first, turned_first, index)
+    (inner,) = call(bind(inner_kernel, z), [field], (wide,), name="inner")(slope_first, turned_first)
+    send, inner, features = lax.optimization_barrier((send, inner, features))
     (send,) = call(
         bind(join_kernel, z),
         [array(z.devices, z.pair + z.chunk, chan, dtype=BF16)],
         (vmem(z.devices * z.chunk, chan),),
         name="join",
-    )(send, early_own, late_own, *early_got, *late_got)
+    )(send, early, late_own, *late_got)
     got = exchange(send)
-    (inner,) = call(bind(inner_kernel, z), [field], (wide,), name="inner")(slope_first, turned_first)
     (chunk,) = call(bind(sum_kernel, z), [array(z.devices // 2, 2 * z.chunk, chan, dtype=BF16)], name="sum")(got)
     same_core = [list(range(core, z.devices, 2)) for core in range(2)]
     mine = lax.all_to_all(chunk, "tile", split_axis=0, concat_axis=0, tiled=True, axis_index_groups=same_core)
-    (input_grad,) = call(bind(input_kernel, z), [array(tiles, side, side, chan)], name="input")(got, pix_row, inner)
-    mine, input_grad = lax.optimization_barrier((mine, input_grad))
+    (input_grad,) = call(bind(input_kernel, z), [array(tiles, side, side, chan)], name="input")(got, index, inner)
     other = lax.ppermute(mine, "tile", [(t, t ^ 1) for t in range(z.devices)])
     grad_first, grad_second, grad_down = call(
         bind(spread_kernel, z),

time: 90.2 us -> 86.6 us (0.960)
  blocking collectives: 28.3 us -> 37.3 us
  waiting for transfers between devices: 12.7 us -> 7.2 us
  starting transfers between devices: 22.5 us -> 19 us
  local copies, waits for them, and re-layouts: 5.69 us -> 3.53 us
  Pallas kernels: 19 us -> 18 us
    all_to_all x0 -> x1, blocking collectives: none -> 10.1 us  [local(): lax.all_to_all(chunk, 'tile', split_axis=0, concat_axis=0, tiled=True, ax...]
    all_to_all x1 -> x0, waiting for transfers between devices: 4.73 us -> none  [local(): lax.all_to_all(chunk, 'tile', split_axis=0, concat_axis=0, tiled=True, ax...]
    all_to_all x1 -> x0, starting transfers between devices: 3.4 us -> none  [local(): lax.all_to_all(chunk, 'tile', split_axis=0, concat_axis=0, tiled=True, ax...]
    ppermute x6, waiting for transfers between devices: 3.27 us -> 0.78 us  [deal(): got.append(lax.ppermute(others[k], ('dp', 'tile'), pairs))]
    unnamed x46 -> x32, local copies, waits for them, and re-layouts: 5.01 us -> 2.85 us
    all_to_all x2, waiting for transfers between devices: 4.27 us -> 6.42 us  [exchange(): return lax.all_to_all(x, 'tile', split_axis=0, concat_axis=0, tiled=True)]
    all_to_all x2, blocking collectives: 28.3 us -> 27.2 us  [exchange(): return lax.all_to_all(x, 'tile', split_axis=0, concat_axis=0, tiled=True)]
    pallas_call x14 -> x15, Pallas kernels: 19 us -> 18 us  [run(): pl.pallas_call(kernel, out_shape=[pltpu.HBM(out[0], out[1]) if is_far els...]
  transfers between devices with their start and end apart: 10 -> 9, of which waited for: 6 -> 3; matrix products, arithmetic and copies ran while one was open for 1% -> 1% of each run, Pallas kernels for 10% -> 12%
where the time goes in v2:
time: 86.6 us; the launch traced here: 86 us
  blocking collectives  37.3 us (43%)
  starting transfers between devices  19 us (22%)
  Pallas kernels  18 us (21%)
  waiting for transfers between devices  7.2 us (8%)
  local copies, waits for them, and re-layouts  3.53 us (4%)
  between operations  0.96 us (1%)
    all_to_all x2, blocking collectives, exchange(): return lax.all_to_all(x, 'tile', split_axis=0, concat_axis=0, tiled=True)  27.2 us
    pallas_call x15, Pallas kernels, run(): pl.pallas_call(kernel, out_shape=[pltpu.HBM(out[0], out[1]) if is_far els...  18 us
    all_to_all x2, starting transfers between devices, exchange(): return lax.all_to_all(x, 'tile', split_axis=0, concat_axis=0, tiled=True)  12 us
    all_to_all x1, blocking collectives, local(): lax.all_to_all(chunk, 'tile', split_axis=0, concat_axis=0, tiled=True, ax...  10.1 us
    all_to_all x2, waiting for transfers between devices, exchange(): return lax.all_to_all(x, 'tile', split_axis=0, concat_axis=0, tiled=True)  6.42 us
    ppermute x6, starting transfers between devices, deal(): got.append(lax.ppermute(others[k], ('dp', 'tile'), pairs))  5.15 us
    unnamed x32, local copies, waits for them, and re-layouts  2.85 us
    ppermute x1, starting transfers between devices, local(): other = lax.ppermute(mine, 'tile', [(t, t ^ 1) for t in range(z.devices)])  1.9 us
  transfers between devices with their start and end apart: 9, of which 3 were waited for; matrix products, arithmetic and copies ran while one was open for 1% of the time, Pallas kernels for 12%

profile of v2, /device:TPU:1, one launch (start us, length us, event | category | flops | bytes accessed | tf_op | source)
XLA Modules:
  0.0 86.0 jit_solution(12752187606293107580)
XLA Ops:
  0.6 0.0 copy-start.1
  0.6 2.3 %pack.1 = bf16[16,48,128]{2,1,0:T(8,128)(2,1)} custom-call(s32[1]{0:T(128)} %bitcast.1.refs_0_.refs_1_, s32[4,256]{1,0:T(4,128)} %bitcast.26, s32[4,256]{1,0:T(4,128)} %bitcast.28, s32[8,256]{1,0:T(8,128)} %bitcast.22, s32[8,256]{1,0:T(8,128)} %bitcast.24, bf16[16,8,8,128]{3,2,1,0:T(8,128)(2,1)} %bitcast.17), custom_call_target="tpu_custom_call" | custom-call | tf_op jit(solution)/shard_map/pack/pallas_call | solution.py:506
  2.9 0.0 copy-start.15
  2.9 0.0 copy-start
  2.9 0.0 copy-start.11
  3.0 0.0 copy-start.12
  3.0 0.0 copy-start.13
  3.0 0.0 copy-start.14
  3.0 7.5 %all-to-all-start = ((bf16[16,48,128]{2,1,0:T(8,128)(2,1)}), bf16[16,48,128]{2,1,0:T(8,128)(2,1)S(1)}, u32[]{:S(2)}, u32[]{:S(2)}) async-start(bf16[16,48,128]{2,1,0:T(8,128)(2,1)} %pack.1), calls=%async_computation | async-start | bytes 393216 | tf_op jit(solution)/shard_map/all_to_all | solution.py:534
  10.5 0.0 copy-done.15
  10.5 0.0 copy-done.1
  10.6 0.0 copy-done
  10.6 0.0 copy-done.11
  10.6 0.0 copy-done.12
  10.6 0.0 copy-done.13
  10.6 0.0 copy-done.14
  10.6 0.8 copy-done.6
  11.4 1.4 %aside.1 = (s32[24,768]{1,0:T(8,128)S(1)}, f32[1024,128]{1,0:T(8,128)S(1)}, bf16[1152,128]{1,0:T(8,128)(2,1)S(1)}, bf16[1152,128]{1,0:T(8,128)(2,1)S(1)}) custom-call(s32[1]{0:T(128)} %bitcast.1.refs_0_.refs_1_, s32[4,256]{1,0:T(4,128)S(1)} %bitcast.27, s32[4,256]{1,0:T(4,128)S(1)} %bitcast.29, s32[8,256]{1,0:T(8,128)S(1)} %bitcast.23, ...), custom_call_target="tpu_custom_call" | custom-call | tf_op jit(solution)/shard_map/aside/pallas_call | solution.py:506
  12.8 0.0 copy-start.4
  12.8 0.8 copy-done.4
  13.6 5.2 %all-to-all-done.refs_0_ = bf16[16,48,128]{2,1,0:T(8,128)(2,1)S(1)} async-done(((bf16[16,48,128]{2,1,0:T(8,128)(2,1)}), bf16[16,48,128]{2,1,0:T(8,128)(2,1)S(1)}, u32[]{:S(2)}, u32[]{:S(2)}) %all-to-all-start) | async-done | bytes 196640 | tf_op jit(solution)/shard_map/all_to_all | solution.py:534
  18.8 0.0 copy-done.2
  18.8 1.8 %first.1 = (bf16[16,48,128]{2,1,0:T(8,128)(2,1)S(1)}, bf16[1024,128]{1,0:T(8,128)(2,1)S(1)}, bf16[1280,384]{1,0:T(8,128)(2,1)S(1)}) custom-call(bf16[16,48,128]{2,1,0:T(8,128)(2,1)S(1)} %all-to-all-done.refs_0_, s32[24,768]{1,0:T(8,128)S(1)} %get-tuple-element.32.refs_1_.refs_3_.refs_2_, bf16[16,8,8,128]{3,2,1,0:T(8,128)(2,1)S(1)} %bitcast.18, ...), custom_call_target="tpu_custom_call" | custom-call | tf_op jit(solution)/shard_map/first/pallas_call | solution.py:506
  20.7 11.2 %all_to_all.25.refs_0_ = bf16[16,48,128]{2,1,0:T(8,128)(2,1)S(1)} all-to-all(bf16[16,48,128]{2,1,0:T(8,128)(2,1)S(1)} %get-tuple-element.33), channel_id=1, replica_groups=mesh['dp'=2,'tile'=16] {'tile'}, dimensions={0} | all-to-all | bytes 393216 | tf_op jit(solution)/shard_map/all_to_all | solution.py:534
  31.8 0.0 copy-done.5
  31.8 2.8 %second.1 = (bf16[16,48,128]{2,1,0:T(8,128)(2,1)}, bf16[1024,128]{1,0:T(8,128)(2,1)S(1)}, bf16[1024,128]{1,0:T(8,128)(2,1)S(1)}, bf16[1280,384]{1,0:T(8,128)(2,1)}) custom-call(bf16[16,48,128]{2,1,0:T(8,128)(2,1)S(1)} %all_to_all.25.refs_0_, s32[24,768]{1,0:T(8,128)S(1)} %get-tuple-element.32.refs_1_.refs_3_.refs_2_, ...), custom_call_target="tpu_custom_call" | custom-call | tf_op jit(solution)/shard_map/second/pallas_call | solution.py:506
  34.7 4.5 %all-to-all-start.2 = ((bf16[16,48,128]{2,1,0:T(8,128)(2,1)}), bf16[16,48,128]{2,1,0:T(8,128)(2,1)S(1)}, u32[]{:S(2)}, u32[]{:S(2)}) async-start(bf16[16,48,128]{2,1,0:T(8,128)(2,1)} %get-tuple-element.37), calls=%async_computation.2 | async-start | bytes 393216 | tf_op jit(solution)/shard_map/all_to_all | solution.py:534
  39.2 1.2 %copy-done.3 = bf16[1280,384]{1,0:T(8,128)(2,1)S(1)} copy-done((bf16[1280,384]{1,0:T(8,128)(2,1)S(1)}, bf16[1280,384]{1,0:T(8,128)(2,1)}, u32[]{:S(2)}) %copy-start.3) | copy-done | bytes 983064
  40.4 1.6 %early.1 = (bf16[256,128]{1,0:T(8,128)(2,1)S(1)}, f32[416,128]{1,0:T(8,128)S(1)}, bf16[416,128]{1,0:T(8,128)(2,1)}, bf16[416,128]{1,0:T(8,128)(2,1)}, bf16[416,128]{1,0:T(8,128)(2,1)}) custom-call(s32[1]{0:T(128)} %bitcast.refs_0_, s32[1]{0:T(128)} %bitcast.1.refs_0_.refs_1_, bf16[1280,384]{1,0:T(8,128)(2,1)S(1)} %copy-done.3, ...), custom_call_target="tpu_custom_call" | custom-call | tf_op jit(solution)/shard_map/early/pallas_call | solution.py:506
  42.0 0.0 copy-start.7
  42.0 0.0 copy-start.9
  42.0 0.3 collective-permute-start
  42.3 1.2 %collective-permute-start.1 = (bf16[416,128]{1,0:T(8,128)(2,1)}, bf16[416,128]{1,0:T(8,128)(2,1)}, u32[]{:S(2)}, u32[]{:S(2)}) collective-permute-start(bf16[416,128]{1,0:T(8,128)(2,1)} %get-tuple-element.49), channel_id=1, source_target_pairs={{0,16},{1,17},{2,18},{3,19},{4,20},{5,21},{6,22},{7,23},{8,24},{9,... | collective-permute-start | bytes 319496 | tf_op jit(solution)/shard_map/ppermute | solution.py:545
  43.5 0.7 collective-permute-start.2
  44.2 0.9 again.1.refs_5_
  45.1 0.0 copy-done.7
  45.1 0.0 copy-done.9
  45.1 0.8 inner.2.refs_4_
  45.9 0.0 copy-start.10
  46.0 1.2 %all-to-all-done.2.refs_2_ = bf16[16,48,128]{2,1,0:T(8,128)(2,1)S(1)} async-done(((bf16[16,48,128]{2,1,0:T(8,128)(2,1)}), bf16[16,48,128]{2,1,0:T(8,128)(2,1)S(1)}, u32[]{:S(2)}, u32[]{:S(2)}) %all-to-all-start.2) | async-done | bytes 196640 | tf_op jit(solution)/shard_map/all_to_all | solution.py:534
  47.2 1.5 %slope.1 = (bf16[1024,128]{1,0:T(8,128)(2,1)S(1)}, f32[288,128]{1,0:T(8,128)S(1)}, bf16[288,128]{1,0:T(8,128)(2,1)S(1)}, bf16[288,128]{1,0:T(8,128)(2,1)S(1)}, bf16[288,128]{1,0:T(8,128)(2,1)S(1)}) custom-call(s32[1]{0:T(128)} %bitcast.refs_0_, s32[1]{0:T(128)} %bitcast.1.refs_0_.refs_1_, bf16[16,48,128]{2,1,0:T(8,128)(2,1)S(1)} %all-to-all-done.2.refs_2_, ...), custom_call_target="tpu_custom_call" | custom-call | tf_op jit(solution)/shard_map/slope/pallas_call | solution.py:506
  48.7 1.2 %collective-permute-start.3 = (bf16[288,128]{1,0:T(8,128)(2,1)S(1)}, bf16[288,128]{1,0:T(8,128)(2,1)S(1)}, u32[]{:S(2)}, u32[]{:S(2)}) collective-permute-start(bf16[288,128]{1,0:T(8,128)(2,1)S(1)} %get-tuple-element.52), channel_id=1, source_target_pairs={{0,1},{1,0},{2,3},{3,2},{4,5},{5,4},{6,7},{7,6},{8,9},{9,8},{10,11... | collective-permute-start | bytes 221192 | tf_op jit(solution)/shard_map/ppermute | solution.py:545
  49.9 1.2 %collective-permute-start.4 = (bf16[288,128]{1,0:T(8,128)(2,1)S(1)}, bf16[288,128]{1,0:T(8,128)(2,1)S(1)}, u32[]{:S(2)}, u32[]{:S(2)}) collective-permute-start(bf16[288,128]{1,0:T(8,128)(2,1)S(1)} %get-tuple-element.53), channel_id=1, source_target_pairs={{0,16},{1,17},{2,18},{3,19},{4,20},{5,21},{6,22},{7,23},{8,24},{9,... | collective-permute-start | bytes 221192 | tf_op jit(solution)/shard_map/ppermute | solution.py:545
  51.2 0.0 collective-permute-done.refs_1_
  51.2 0.5 collective-permute-start.5
  51.7 0.0 copy-done.10
  51.7 0.7 copy.17
  52.3 0.0 collective-permute-done.1.refs_2_
  52.3 0.0 collective-permute-done.2.refs_3_
  52.3 0.0 copy-done.8
  52.3 1.0 %gain.1.refs_1_ = f32[416,128]{1,0:T(8,128)S(1)} custom-call(f32[416,128]{1,0:T(8,128)S(1)} %copy-done.8, bf16[416,128]{1,0:T(8,128)(2,1)S(1)} %collective-permute-done.refs_1_, bf16[416,128]{1,0:T(8,128)(2,1)} %collective-permute-done.1.refs_2_, bf16[416,128]{1,0:T(8,128)(2,1)} %collective-permute-done.2.refs_3_), custom_call_target="tpu_custom_call" | custom-call | tf_op jit(solution)/shard_map/gain/pallas_call | solution.py:506
  53.3 0.8 inner.3.refs_2_
  54.2 0.6 last.1.refs_0_
  54.8 0.0 collective-permute-done.3.refs_3_
  54.8 0.0 collective-permute-done.4.refs_4_
  54.8 0.8 collective-permute-done.5.refs_5_
  55.6 0.1 join.1
  55.7 16.0 %all_to_all.26.refs_0_ = bf16[16,96,128]{2,1,0:T(8,128)(2,1)S(1)} all-to-all(bf16[16,96,128]{2,1,0:T(8,128)(2,1)S(1)} %join.1), channel_id=1, replica_groups=mesh['dp'=2,'tile'=16] {'tile'}, dimensions={0} | all-to-all | bytes 786432 | tf_op jit(solution)/shard_map/all_to_all | solution.py:534
  71.7 0.1 sum.1
  71.7 10.1 %all_to_all.27.refs_1_ = bf16[8,96,128]{2,1,0:T(8,128)(2,1)S(1)} all-to-all(bf16[8,96,128]{2,1,0:T(8,128)(2,1)S(1)} %sum.1), channel_id=1, replica_groups={{0,2,4,6,8,10,12,14},{1,3,5,7,9,11,13,15},{16,18,20,22,24,26,28,30},{17..., dimensions={0} | all-to-all | bytes 393216 | tf_op jit(solution)/shard_map/all_to_all | solution.py:626
  81.8 1.9 %collective-permute-start.6 = (bf16[8,96,128]{2,1,0:T(8,128)(2,1)S(1)}, bf16[8,96,128]{2,1,0:T(8,128)(2,1)S(1)}, u32[]{:S(2)}, u32[]{:S(2)}) collective-permute-start(bf16[8,96,128]{2,1,0:T(8,128)(2,1)S(1)} %all_to_all.27.refs_1_), channel_id=1, source_target_pairs={{0,1},{1,0},{2,3},{3,2},{4,5},{5,4},{6,7},{7,6},{8,9},{9,8},{10,11... | collective-permute-start | bytes 589832 | tf_op jit(solution)/shard_map/ppermute | solution.py:628
  83.7 1.4 %input.1 = f32[16,8,8,128]{3,2,1,0:T(8,128)} custom-call(bf16[16,96,128]{2,1,0:T(8,128)(2,1)S(1)} %all_to_all.26.refs_0_, s32[24,768]{1,0:T(8,128)S(1)} %get-tuple-element.32.refs_1_.refs_3_.refs_2_, f32[1024,128]{1,0:T(8,128)S(1)} %inner.3.refs_2_), custom_call_target="tpu_custom_call" | custom-call | tf_op jit(solution)/shard_map/input/pallas_call | solution.py:506
  85.1 0.0 collective-permute-done.6.refs_2_
  85.2 0.9 %spread.1 = (f32[576,128]{1,0:T(8,128)}, f32[576,128]{1,0:T(8,128)}, f32[256,128]{1,0:T(8,128)}) custom-call(s32[1]{0:T(128)} %bitcast.1.refs_0_.refs_1_, bf16[8,96,128]{2,1,0:T(8,128)(2,1)S(1)} %all_to_all.27.refs_1_, bf16[8,96,128]{2,1,0:T(8,128)(2,1)S(1)} %collective-permute-done.6.refs_2_), custom_call_target="tpu_custom_call" | custom-call | tf_op jit(solution)/shard_map/spread/pallas_call | solution.py:506
  (6 shorter events, 0.0 us)
Async XLA Ops:
  0.6 9.9 %copy-start.1 = (bf16[1152,128]{1,0:T(8,128)(2,1)S(1)}, bf16[1152,128]{1,0:T(8,128)(2,1)}, u32[]{:S(2)}) copy-start(bf16[1152,128]{1,0:T(8,128)(2,1)} %refs_3_.3) | copy-start | bytes 884740
  2.9 7.6 %copy-start.15 = (bf16[1,16,4,4,128]{4,3,2,1,0:T(4,128)(2,1)S(1)}, bf16[1,16,4,4,128]{4,3,2,1,0:T(4,128)(2,1)}, u32[]{:S(2)}) copy-start(bf16[1,16,4,4,128]{4,3,2,1,0:T(4,128)(2,1)} %param.10) | copy-start | bytes 196612
  2.9 7.6 %copy-start = (bf16[1152,128]{1,0:T(8,128)(2,1)S(1)}, bf16[1152,128]{1,0:T(8,128)(2,1)}, u32[]{:S(2)}) copy-start(bf16[1152,128]{1,0:T(8,128)(2,1)} %refs_1_.1) | copy-start | bytes 884740
  2.9 7.6 %copy-start.11 = (s32[256,8]{0,1:T(8,128)S(1)}, s32[256,8]{0,1:T(8,128)}, u32[]{:S(2)}) copy-start(s32[256,8]{0,1:T(8,128)} %param.16) | copy-start | bytes 24580
  3.0 7.6 %copy-start.12 = (s32[256,8]{0,1:T(8,128)S(1)}, s32[256,8]{0,1:T(8,128)}, u32[]{:S(2)}) copy-start(s32[256,8]{0,1:T(8,128)} %param.17) | copy-start | bytes 24580
  3.0 7.6 %copy-start.13 = (s32[256,4]{0,1:T(4,128)S(1)}, s32[256,4]{0,1:T(4,128)}, u32[]{:S(2)}) copy-start(s32[256,4]{0,1:T(4,128)} %param.14) | copy-start | bytes 12292
  3.0 7.6 %copy-start.14 = (s32[256,4]{0,1:T(4,128)S(1)}, s32[256,4]{0,1:T(4,128)}, u32[]{:S(2)}) copy-start(s32[256,4]{0,1:T(4,128)} %param.15) | copy-start | bytes 12292
  3.0 15.8 %all-to-all-start = ((bf16[16,48,128]{2,1,0:T(8,128)(2,1)}), bf16[16,48,128]{2,1,0:T(8,128)(2,1)S(1)}, u32[]{:S(2)}, u32[]{:S(2)}) async-start(bf16[16,48,128]{2,1,0:T(8,128)(2,1)} %pack.1), calls=%async_computation | async-start | bytes 393216 | tf_op jit(solution)/shard_map/all_to_all | solution.py:534
  10.5 0.9 %copy-start.6 = (bf16[512,128]{1,0:T(8,128)(2,1)S(1)}, bf16[512,128]{1,0:T(8,128)(2,1)}, u32[]{:S(2)}) copy-start(bf16[512,128]{1,0:T(8,128)(2,1)} %refs_6_.3) | copy-start | bytes 393220
  11.4 7.4 %copy-start.2 = (bf16[1,16,8,8,128]{4,3,2,1,0:T(8,128)(2,1)S(1)}, bf16[1,16,8,8,128]{4,3,2,1,0:T(8,128)(2,1)}, u32[]{:S(2)}) copy-start(bf16[1,16,8,8,128]{4,3,2,1,0:T(8,128)(2,1)} %param.9) | copy-start | bytes 786436
  12.8 0.8 copy-start.4
  18.8 13.0 %copy-start.5 = (f32[1024,128]{1,0:T(8,128)S(1)}, f32[1024,128]{1,0:T(8,128)}, u32[]{:S(2)}) copy-start(f32[1024,128]{1,0:T(8,128)} %copy-done.4) | copy-start | bytes 1572868
  34.7 12.5 %all-to-all-start.2 = ((bf16[16,48,128]{2,1,0:T(8,128)(2,1)}), bf16[16,48,128]{2,1,0:T(8,128)(2,1)S(1)}, u32[]{:S(2)}, u32[]{:S(2)}) async-start(bf16[16,48,128]{2,1,0:T(8,128)(2,1)} %get-tuple-element.37), calls=%async_computation.2 | async-start | bytes 393216 | tf_op jit(solution)/shard_map/all_to_all | solution.py:534
  39.2 1.2 %copy-start.3 = (bf16[1280,384]{1,0:T(8,128)(2,1)S(1)}, bf16[1280,384]{1,0:T(8,128)(2,1)}, u32[]{:S(2)}) copy-start(bf16[1280,384]{1,0:T(8,128)(2,1)} %get-tuple-element.42.refs_2_) | copy-start | bytes 2949124
  42.0 3.1 %copy-start.7 = (f32[416,128]{1,0:T(8,128)}, f32[416,128]{1,0:T(8,128)S(1)}, u32[]{:S(2)}) copy-start(f32[416,128]{1,0:T(8,128)S(1)} %get-tuple-element.47.refs_0_) | copy-start | bytes 638980
  42.0 3.1 %copy-start.9 = (bf16[256,128]{1,0:T(8,128)(2,1)}, bf16[256,128]{1,0:T(8,128)(2,1)S(1)}, u32[]{:S(2)}) copy-start(bf16[256,128]{1,0:T(8,128)(2,1)S(1)} %get-tuple-element.44) | copy-start | bytes 196612
  42.0 9.1 %collective-permute-start = (bf16[416,128]{1,0:T(8,128)(2,1)}, bf16[416,128]{1,0:T(8,128)(2,1)S(1)}, u32[]{:S(2)}, u32[]{:S(2)}) collective-permute-start(bf16[416,128]{1,0:T(8,128)(2,1)} %get-tuple-element.48), channel_id=1, source_target_pairs={{0,1},{1,0},{2,3},{3,2},{4,5},{5,4},{6,7},{7,6},{8,9},{9,8},{10,11... | collective-permute-start | bytes 319496 | tf_op jit(solution)/shard_map/ppermute | solution.py:545
  42.3 10.0 %collective-permute-start.1 = (bf16[416,128]{1,0:T(8,128)(2,1)}, bf16[416,128]{1,0:T(8,128)(2,1)}, u32[]{:S(2)}, u32[]{:S(2)}) collective-permute-start(bf16[416,128]{1,0:T(8,128)(2,1)} %get-tuple-element.49), channel_id=1, source_target_pairs={{0,16},{1,17},{2,18},{3,19},{4,20},{5,21},{6,22},{7,23},{8,24},{9,... | collective-permute-start | bytes 319496 | tf_op jit(solution)/shard_map/ppermute | solution.py:545
  43.5 8.8 %collective-permute-start.2 = (bf16[416,128]{1,0:T(8,128)(2,1)}, bf16[416,128]{1,0:T(8,128)(2,1)}, u32[]{:S(2)}, u32[]{:S(2)}) collective-permute-start(bf16[416,128]{1,0:T(8,128)(2,1)} %get-tuple-element.50), channel_id=1, source_target_pairs={{0,17},{1,16},{2,19},{3,18},{4,21},{5,20},{6,23},{7,22},{8,25},{9,... | collective-permute-start | bytes 319496 | tf_op jit(solution)/shard_map/ppermute | solution.py:545
  45.9 5.7 %copy-start.10 = (bf16[256,128]{1,0:T(8,128)(2,1)S(1)}, bf16[256,128]{1,0:T(8,128)(2,1)}, u32[]{:S(2)}) copy-start(bf16[256,128]{1,0:T(8,128)(2,1)} %copy-done.9) | copy-start | bytes 196612
  47.2 5.1 %copy-start.8 = (f32[416,128]{1,0:T(8,128)S(1)}, f32[416,128]{1,0:T(8,128)}, u32[]{:S(2)}) copy-start(f32[416,128]{1,0:T(8,128)} %copy-done.7) | copy-start | bytes 638980
  48.7 6.1 %collective-permute-start.3 = (bf16[288,128]{1,0:T(8,128)(2,1)S(1)}, bf16[288,128]{1,0:T(8,128)(2,1)S(1)}, u32[]{:S(2)}, u32[]{:S(2)}) collective-permute-start(bf16[288,128]{1,0:T(8,128)(2,1)S(1)} %get-tuple-element.52), channel_id=1, source_target_pairs={{0,1},{1,0},{2,3},{3,2},{4,5},{5,4},{6,7},{7,6},{8,9},{9,8},{10,11... | collective-permute-start | bytes 221192 | tf_op jit(solution)/shard_map/ppermute | solution.py:545
  49.9 4.9 %collective-permute-start.4 = (bf16[288,128]{1,0:T(8,128)(2,1)S(1)}, bf16[288,128]{1,0:T(8,128)(2,1)S(1)}, u32[]{:S(2)}, u32[]{:S(2)}) collective-permute-start(bf16[288,128]{1,0:T(8,128)(2,1)S(1)} %get-tuple-element.53), channel_id=1, source_target_pairs={{0,16},{1,17},{2,18},{3,19},{4,20},{5,21},{6,22},{7,23},{8,24},{9,... | collective-permute-start | bytes 221192 | tf_op jit(solution)/shard_map/ppermute | solution.py:545
  51.2 4.4 %collective-permute-start.5 = (bf16[288,128]{1,0:T(8,128)(2,1)S(1)}, bf16[288,128]{1,0:T(8,128)(2,1)S(1)}, u32[]{:S(2)}, u32[]{:S(2)}) collective-permute-start(bf16[288,128]{1,0:T(8,128)(2,1)S(1)} %get-tuple-element.54), channel_id=1, source_target_pairs={{0,17},{1,16},{2,19},{3,18},{4,21},{5,20},{6,23},{7,22},{8,25},{9,... | collective-permute-start | bytes 221192 | tf_op jit(solution)/shard_map/ppermute | solution.py:545
  81.8 3.3 %collective-permute-start.6 = (bf16[8,96,128]{2,1,0:T(8,128)(2,1)S(1)}, bf16[8,96,128]{2,1,0:T(8,128)(2,1)S(1)}, u32[]{:S(2)}, u32[]{:S(2)}) collective-permute-start(bf16[8,96,128]{2,1,0:T(8,128)(2,1)S(1)} %all_to_all.27.refs_1_), channel_id=1, source_target_pairs={{0,1},{1,0},{2,3},{3,2},{4,5},{5,4},{6,7},{7,6},{8,9},{9,8},{10,11... | collective-permute-start | bytes 589832 | tf_op jit(solution)/shard_map/ppermute | solution.py:628

commit v3 on v2

--- a/solution.py
+++ b/solution.py
@@ -314,10 +314,13 @@
 
 
 def tap_products(z, columns_ref, slope, scale, total_ref):
-    turned = jnp.transpose(slope.astype(F32)).astype(BF16)
+    blank = jnp.zeros((2 * z.line, z.chan), BF16)
+    padded = jnp.concatenate([blank, slope, blank], axis=0)
+    rows = (z.side + 2) * z.line
+    wide = jnp.concatenate([padded[(2 - p) * z.line : (2 - p) * z.line + rows] for p in range(3)], axis=1)
+    total = mm_t(columns_ref[...], wide) * scale
     for p in range(3):
-        part = jnp.dot(turned, columns_ref[p * z.line : p * z.line + z.pixels, :], preferred_element_type=F32)
-        total_ref[3 * p * z.chan : 3 * (p + 1) * z.chan, :] = jnp.transpose(part * scale)
+        total_ref[3 * p * z.chan : 3 * (p + 1) * z.chan, :] = total[:, p * z.chan : (p + 1) * z.chan]
 
 
 def deal_parts(z, sample_ref, me_ref, source_ref, own_ref, other_refs):

time: 86.6 us -> 86.3 us (level)
  transfers between devices with their start and end apart: 9 -> 9, of which waited for: 3 -> 3; matrix products, arithmetic and copies ran while one was open for 1% -> 1% of each run, Pallas kernels for 12% -> 11%
where the time goes in v3:
time: 86.3 us; the launch traced here: 85.8 us
  blocking collectives  37.3 us (43%)
  starting transfers between devices  19 us (22%)
  Pallas kernels  17.8 us (21%)
  waiting for transfers between devices  7.11 us (8%)
  local copies, waits for them, and re-layouts  3.53 us (4%)
  between operations  0.96 us (1%)
    all_to_all x2, blocking collectives, exchange(): return lax.all_to_all(x, 'tile', split_axis=0, concat_axis=0, tiled=True)  27.2 us
    pallas_call x15, Pallas kernels, run(): pl.pallas_call(kernel, out_shape=[pltpu.HBM(out[0], out[1]) if is_far els...  17.8 us
    all_to_all x2, starting transfers between devices, exchange(): return lax.all_to_all(x, 'tile', split_axis=0, concat_axis=0, tiled=True)  12 us
    all_to_all x1, blocking collectives, local(): lax.all_to_all(chunk, 'tile', split_axis=0, concat_axis=0, tiled=True, ax...  10.1 us
    all_to_all x2, waiting for transfers between devices, exchange(): return lax.all_to_all(x, 'tile', split_axis=0, concat_axis=0, tiled=True)  6.34 us
    ppermute x6, starting transfers between devices, deal(): got.append(lax.ppermute(others[k], ('dp', 'tile'), pairs))  5.16 us
    unnamed x32, local copies, waits for them, and re-layouts  2.85 us
    ppermute x1, starting transfers between devices, local(): other = lax.ppermute(mine, 'tile', [(t, t ^ 1) for t in range(z.devices)])  1.9 us
  transfers between devices with their start and end apart: 9, of which 3 were waited for; matrix products, arithmetic and copies ran while one was open for 1% of the time, Pallas kernels for 11%

profile of v3, /device:TPU:1, one launch (start us, length us, event | category | flops | bytes accessed | tf_op | source)
XLA Modules:
  0.0 85.8 jit_solution(11869000181449781336)
XLA Ops:
  0.6 0.0 copy-start.1
  0.6 2.3 %pack.1 = bf16[16,48,128]{2,1,0:T(8,128)(2,1)} custom-call(s32[1]{0:T(128)} %bitcast.1.refs_0_.refs_1_, s32[4,256]{1,0:T(4,128)} %bitcast.26, s32[4,256]{1,0:T(4,128)} %bitcast.28, s32[8,256]{1,0:T(8,128)} %bitcast.22, s32[8,256]{1,0:T(8,128)} %bitcast.24, bf16[16,8,8,128]{3,2,1,0:T(8,128)(2,1)} %bitcast.17), custom_call_target="tpu_custom_call" | custom-call | tf_op jit(solution)/shard_map/pack/pallas_call | solution.py:509
  2.9 0.0 copy-start.15
  2.9 0.0 copy-start
  2.9 0.0 copy-start.11
  3.0 0.0 copy-start.12
  3.0 0.0 copy-start.13
  3.0 0.0 copy-start.14
  3.0 7.5 %all-to-all-start = ((bf16[16,48,128]{2,1,0:T(8,128)(2,1)}), bf16[16,48,128]{2,1,0:T(8,128)(2,1)S(1)}, u32[]{:S(2)}, u32[]{:S(2)}) async-start(bf16[16,48,128]{2,1,0:T(8,128)(2,1)} %pack.1), calls=%async_computation | async-start | bytes 393216 | tf_op jit(solution)/shard_map/all_to_all | solution.py:537
  10.5 0.0 copy-done.15
  10.5 0.0 copy-done.1
  10.6 0.0 copy-done
  10.6 0.0 copy-done.11
  10.6 0.0 copy-done.12
  10.6 0.0 copy-done.13
  10.6 0.0 copy-done.14
  10.6 0.8 copy-done.6
  11.4 1.4 %aside.1 = (s32[24,768]{1,0:T(8,128)S(1)}, f32[1024,128]{1,0:T(8,128)S(1)}, bf16[1152,128]{1,0:T(8,128)(2,1)S(1)}, bf16[1152,128]{1,0:T(8,128)(2,1)S(1)}) custom-call(s32[1]{0:T(128)} %bitcast.1.refs_0_.refs_1_, s32[4,256]{1,0:T(4,128)S(1)} %bitcast.27, s32[4,256]{1,0:T(4,128)S(1)} %bitcast.29, s32[8,256]{1,0:T(8,128)S(1)} %bitcast.23, ...), custom_call_target="tpu_custom_call" | custom-call | tf_op jit(solution)/shard_map/aside/pallas_call | solution.py:509
  12.8 0.0 copy-start.4
  12.8 0.8 copy-done.4
  13.6 5.2 %all-to-all-done.refs_0_ = bf16[16,48,128]{2,1,0:T(8,128)(2,1)S(1)} async-done(((bf16[16,48,128]{2,1,0:T(8,128)(2,1)}), bf16[16,48,128]{2,1,0:T(8,128)(2,1)S(1)}, u32[]{:S(2)}, u32[]{:S(2)}) %all-to-all-start) | async-done | bytes 196640 | tf_op jit(solution)/shard_map/all_to_all | solution.py:537
  18.8 0.0 copy-done.2
  18.8 1.8 %first.1 = (bf16[16,48,128]{2,1,0:T(8,128)(2,1)S(1)}, bf16[1024,128]{1,0:T(8,128)(2,1)S(1)}, bf16[1280,384]{1,0:T(8,128)(2,1)S(1)}) custom-call(bf16[16,48,128]{2,1,0:T(8,128)(2,1)S(1)} %all-to-all-done.refs_0_, s32[24,768]{1,0:T(8,128)S(1)} %get-tuple-element.32.refs_1_.refs_3_.refs_2_, bf16[16,8,8,128]{3,2,1,0:T(8,128)(2,1)S(1)} %bitcast.18, ...), custom_call_target="tpu_custom_call" | custom-call | tf_op jit(solution)/shard_map/first/pallas_call | solution.py:509
  20.7 11.2 %all_to_all.25.refs_0_ = bf16[16,48,128]{2,1,0:T(8,128)(2,1)S(1)} all-to-all(bf16[16,48,128]{2,1,0:T(8,128)(2,1)S(1)} %get-tuple-element.33), channel_id=1, replica_groups=mesh['dp'=2,'tile'=16] {'tile'}, dimensions={0} | all-to-all | bytes 393216 | tf_op jit(solution)/shard_map/all_to_all | solution.py:537
  31.8 0.0 copy-done.5
  31.8 2.8 %second.1 = (bf16[16,48,128]{2,1,0:T(8,128)(2,1)}, bf16[1024,128]{1,0:T(8,128)(2,1)S(1)}, bf16[1024,128]{1,0:T(8,128)(2,1)S(1)}, bf16[1280,384]{1,0:T(8,128)(2,1)}) custom-call(bf16[16,48,128]{2,1,0:T(8,128)(2,1)S(1)} %all_to_all.25.refs_0_, s32[24,768]{1,0:T(8,128)S(1)} %get-tuple-element.32.refs_1_.refs_3_.refs_2_, ...), custom_call_target="tpu_custom_call" | custom-call | tf_op jit(solution)/shard_map/second/pallas_call | solution.py:509
  34.7 4.5 %all-to-all-start.2 = ((bf16[16,48,128]{2,1,0:T(8,128)(2,1)}), bf16[16,48,128]{2,1,0:T(8,128)(2,1)S(1)}, u32[]{:S(2)}, u32[]{:S(2)}) async-start(bf16[16,48,128]{2,1,0:T(8,128)(2,1)} %get-tuple-element.37), calls=%async_computation.2 | async-start | bytes 393216 | tf_op jit(solution)/shard_map/all_to_all | solution.py:537
  39.2 1.2 %copy-done.3 = bf16[1280,384]{1,0:T(8,128)(2,1)S(1)} copy-done((bf16[1280,384]{1,0:T(8,128)(2,1)S(1)}, bf16[1280,384]{1,0:T(8,128)(2,1)}, u32[]{:S(2)}) %copy-start.3) | copy-done | bytes 983064
  40.4 1.7 %early.1 = (bf16[256,128]{1,0:T(8,128)(2,1)S(1)}, f32[416,128]{1,0:T(8,128)S(1)}, bf16[416,128]{1,0:T(8,128)(2,1)}, bf16[416,128]{1,0:T(8,128)(2,1)}, bf16[416,128]{1,0:T(8,128)(2,1)}) custom-call(s32[1]{0:T(128)} %bitcast.refs_0_, s32[1]{0:T(128)} %bitcast.1.refs_0_.refs_1_, bf16[1280,384]{1,0:T(8,128)(2,1)S(1)} %copy-done.3, ...), custom_call_target="tpu_custom_call" | custom-call | tf_op jit(solution)/shard_map/early/pallas_call | solution.py:509
  42.1 0.0 copy-start.7
  42.1 0.0 copy-start.9
  42.1 0.3 collective-permute-start
  42.4 1.2 %collective-permute-start.1 = (bf16[416,128]{1,0:T(8,128)(2,1)}, bf16[416,128]{1,0:T(8,128)(2,1)}, u32[]{:S(2)}, u32[]{:S(2)}) collective-permute-start(bf16[416,128]{1,0:T(8,128)(2,1)} %get-tuple-element.49), channel_id=1, source_target_pairs={{0,16},{1,17},{2,18},{3,19},{4,20},{5,21},{6,22},{7,23},{8,24},{9,... | collective-permute-start | bytes 319496 | tf_op jit(solution)/shard_map/ppermute | solution.py:548
  43.6 0.7 collective-permute-start.2
  44.3 0.9 again.1.refs_5_
  45.2 0.0 copy-done.7
  45.2 0.0 copy-done.9
  45.2 0.8 inner.2.refs_4_
  46.0 0.0 copy-start.10
  46.0 1.2 %all-to-all-done.2.refs_2_ = bf16[16,48,128]{2,1,0:T(8,128)(2,1)S(1)} async-done(((bf16[16,48,128]{2,1,0:T(8,128)(2,1)}), bf16[16,48,128]{2,1,0:T(8,128)(2,1)S(1)}, u32[]{:S(2)}, u32[]{:S(2)}) %all-to-all-start.2) | async-done | bytes 196640 | tf_op jit(solution)/shard_map/all_to_all | solution.py:537
  47.2 1.2 %slope.1 = (bf16[1024,128]{1,0:T(8,128)(2,1)S(1)}, f32[288,128]{1,0:T(8,128)S(1)}, bf16[288,128]{1,0:T(8,128)(2,1)S(1)}, bf16[288,128]{1,0:T(8,128)(2,1)S(1)}, bf16[288,128]{1,0:T(8,128)(2,1)S(1)}) custom-call(s32[1]{0:T(128)} %bitcast.refs_0_, s32[1]{0:T(128)} %bitcast.1.refs_0_.refs_1_, bf16[16,48,128]{2,1,0:T(8,128)(2,1)S(1)} %all-to-all-done.2.refs_2_, ...), custom_call_target="tpu_custom_call" | custom-call | tf_op jit(solution)/shard_map/slope/pallas_call | solution.py:509
  48.4 1.2 %collective-permute-start.3 = (bf16[288,128]{1,0:T(8,128)(2,1)S(1)}, bf16[288,128]{1,0:T(8,128)(2,1)S(1)}, u32[]{:S(2)}, u32[]{:S(2)}) collective-permute-start(bf16[288,128]{1,0:T(8,128)(2,1)S(1)} %get-tuple-element.52), channel_id=1, source_target_pairs={{0,1},{1,0},{2,3},{3,2},{4,5},{5,4},{6,7},{7,6},{8,9},{9,8},{10,11... | collective-permute-start | bytes 221192 | tf_op jit(solution)/shard_map/ppermute | solution.py:548
  49.6 1.2 %collective-permute-start.4 = (bf16[288,128]{1,0:T(8,128)(2,1)S(1)}, bf16[288,128]{1,0:T(8,128)(2,1)S(1)}, u32[]{:S(2)}, u32[]{:S(2)}) collective-permute-start(bf16[288,128]{1,0:T(8,128)(2,1)S(1)} %get-tuple-element.53), channel_id=1, source_target_pairs={{0,16},{1,17},{2,18},{3,19},{4,20},{5,21},{6,22},{7,23},{8,24},{9,... | collective-permute-start | bytes 221192 | tf_op jit(solution)/shard_map/ppermute | solution.py:548
  50.8 0.0 collective-permute-done.refs_1_
  50.9 0.5 collective-permute-start.5
  51.3 0.0 copy-done.10
  51.3 0.7 copy.17
  52.0 0.0 collective-permute-done.1.refs_2_
  52.0 0.0 collective-permute-done.2.refs_3_
  52.0 0.0 copy-done.8
  52.0 1.0 %gain.1.refs_1_ = f32[416,128]{1,0:T(8,128)S(1)} custom-call(f32[416,128]{1,0:T(8,128)S(1)} %copy-done.8, bf16[416,128]{1,0:T(8,128)(2,1)S(1)} %collective-permute-done.refs_1_, bf16[416,128]{1,0:T(8,128)(2,1)} %collective-permute-done.1.refs_2_, bf16[416,128]{1,0:T(8,128)(2,1)} %collective-permute-done.2.refs_3_), custom_call_target="tpu_custom_call" | custom-call | tf_op jit(solution)/shard_map/gain/pallas_call | solution.py:509
  53.0 0.8 inner.3.refs_2_
  53.8 0.6 last.1.refs_0_
  54.5 0.0 collective-permute-done.3.refs_3_
  54.5 0.0 collective-permute-done.4.refs_4_
  54.5 0.8 collective-permute-done.5.refs_5_
  55.3 0.1 join.1
  55.4 16.0 %all_to_all.26.refs_0_ = bf16[16,96,128]{2,1,0:T(8,128)(2,1)S(1)} all-to-all(bf16[16,96,128]{2,1,0:T(8,128)(2,1)S(1)} %join.1), channel_id=1, replica_groups=mesh['dp'=2,'tile'=16] {'tile'}, dimensions={0} | all-to-all | bytes 786432 | tf_op jit(solution)/shard_map/all_to_all | solution.py:537
  71.4 0.1 sum.1
  71.5 10.1 %all_to_all.27.refs_1_ = bf16[8,96,128]{2,1,0:T(8,128)(2,1)S(1)} all-to-all(bf16[8,96,128]{2,1,0:T(8,128)(2,1)S(1)} %sum.1), channel_id=1, replica_groups={{0,2,4,6,8,10,12,14},{1,3,5,7,9,11,13,15},{16,18,20,22,24,26,28,30},{17..., dimensions={0} | all-to-all | bytes 393216 | tf_op jit(solution)/shard_map/all_to_all | solution.py:629
  81.6 1.9 %collective-permute-start.6 = (bf16[8,96,128]{2,1,0:T(8,128)(2,1)S(1)}, bf16[8,96,128]{2,1,0:T(8,128)(2,1)S(1)}, u32[]{:S(2)}, u32[]{:S(2)}) collective-permute-start(bf16[8,96,128]{2,1,0:T(8,128)(2,1)S(1)} %all_to_all.27.refs_1_), channel_id=1, source_target_pairs={{0,1},{1,0},{2,3},{3,2},{4,5},{5,4},{6,7},{7,6},{8,9},{9,8},{10,11... | collective-permute-start | bytes 589832 | tf_op jit(solution)/shard_map/ppermute | solution.py:631
  83.5 1.4 %input.1 = f32[16,8,8,128]{3,2,1,0:T(8,128)} custom-call(bf16[16,96,128]{2,1,0:T(8,128)(2,1)S(1)} %all_to_all.26.refs_0_, s32[24,768]{1,0:T(8,128)S(1)} %get-tuple-element.32.refs_1_.refs_3_.refs_2_, f32[1024,128]{1,0:T(8,128)S(1)} %inner.3.refs_2_), custom_call_target="tpu_custom_call" | custom-call | tf_op jit(solution)/shard_map/input/pallas_call | solution.py:509
  84.9 0.0 collective-permute-done.6.refs_2_
  84.9 0.9 %spread.1 = (f32[576,128]{1,0:T(8,128)}, f32[576,128]{1,0:T(8,128)}, f32[256,128]{1,0:T(8,128)}) custom-call(s32[1]{0:T(128)} %bitcast.1.refs_0_.refs_1_, bf16[8,96,128]{2,1,0:T(8,128)(2,1)S(1)} %all_to_all.27.refs_1_, bf16[8,96,128]{2,1,0:T(8,128)(2,1)S(1)} %collective-permute-done.6.refs_2_), custom_call_target="tpu_custom_call" | custom-call | tf_op jit(solution)/shard_map/spread/pallas_call | solution.py:509
  (6 shorter events, 0.0 us)
Async XLA Ops:
  0.6 9.9 %copy-start.1 = (bf16[1152,128]{1,0:T(8,128)(2,1)S(1)}, bf16[1152,128]{1,0:T(8,128)(2,1)}, u32[]{:S(2)}) copy-start(bf16[1152,128]{1,0:T(8,128)(2,1)} %refs_3_.3) | copy-start | bytes 884740
  2.9 7.6 %copy-start.15 = (bf16[1,16,4,4,128]{4,3,2,1,0:T(4,128)(2,1)S(1)}, bf16[1,16,4,4,128]{4,3,2,1,0:T(4,128)(2,1)}, u32[]{:S(2)}) copy-start(bf16[1,16,4,4,128]{4,3,2,1,0:T(4,128)(2,1)} %param.10) | copy-start | bytes 196612
  2.9 7.6 %copy-start = (bf16[1152,128]{1,0:T(8,128)(2,1)S(1)}, bf16[1152,128]{1,0:T(8,128)(2,1)}, u32[]{:S(2)}) copy-start(bf16[1152,128]{1,0:T(8,128)(2,1)} %refs_1_.1) | copy-start | bytes 884740
  2.9 7.6 %copy-start.11 = (s32[256,8]{0,1:T(8,128)S(1)}, s32[256,8]{0,1:T(8,128)}, u32[]{:S(2)}) copy-start(s32[256,8]{0,1:T(8,128)} %param.16) | copy-start | bytes 24580
  3.0 7.6 %copy-start.12 = (s32[256,8]{0,1:T(8,128)S(1)}, s32[256,8]{0,1:T(8,128)}, u32[]{:S(2)}) copy-start(s32[256,8]{0,1:T(8,128)} %param.17) | copy-start | bytes 24580
  3.0 7.6 %copy-start.13 = (s32[256,4]{0,1:T(4,128)S(1)}, s32[256,4]{0,1:T(4,128)}, u32[]{:S(2)}) copy-start(s32[256,4]{0,1:T(4,128)} %param.14) | copy-start | bytes 12292
  3.0 7.6 %copy-start.14 = (s32[256,4]{0,1:T(4,128)S(1)}, s32[256,4]{0,1:T(4,128)}, u32[]{:S(2)}) copy-start(s32[256,4]{0,1:T(4,128)} %param.15) | copy-start | bytes 12292
  3.0 15.8 %all-to-all-start = ((bf16[16,48,128]{2,1,0:T(8,128)(2,1)}), bf16[16,48,128]{2,1,0:T(8,128)(2,1)S(1)}, u32[]{:S(2)}, u32[]{:S(2)}) async-start(bf16[16,48,128]{2,1,0:T(8,128)(2,1)} %pack.1), calls=%async_computation | async-start | bytes 393216 | tf_op jit(solution)/shard_map/all_to_all | solution.py:537
  10.5 0.9 %copy-start.6 = (bf16[512,128]{1,0:T(8,128)(2,1)S(1)}, bf16[512,128]{1,0:T(8,128)(2,1)}, u32[]{:S(2)}) copy-start(bf16[512,128]{1,0:T(8,128)(2,1)} %refs_6_.3) | copy-start | bytes 393220
  11.4 7.4 %copy-start.2 = (bf16[1,16,8,8,128]{4,3,2,1,0:T(8,128)(2,1)S(1)}, bf16[1,16,8,8,128]{4,3,2,1,0:T(8,128)(2,1)}, u32[]{:S(2)}) copy-start(bf16[1,16,8,8,128]{4,3,2,1,0:T(8,128)(2,1)} %param.9) | copy-start | bytes 786436
  12.8 0.8 copy-start.4
  18.8 13.0 %copy-start.5 = (f32[1024,128]{1,0:T(8,128)S(1)}, f32[1024,128]{1,0:T(8,128)}, u32[]{:S(2)}) copy-start(f32[1024,128]{1,0:T(8,128)} %copy-done.4) | copy-start | bytes 1572868
  34.7 12.5 %all-to-all-start.2 = ((bf16[16,48,128]{2,1,0:T(8,128)(2,1)}), bf16[16,48,128]{2,1,0:T(8,128)(2,1)S(1)}, u32[]{:S(2)}, u32[]{:S(2)}) async-start(bf16[16,48,128]{2,1,0:T(8,128)(2,1)} %get-tuple-element.37), calls=%async_computation.2 | async-start | bytes 393216 | tf_op jit(solution)/shard_map/all_to_all | solution.py:537
  39.2 1.2 %copy-start.3 = (bf16[1280,384]{1,0:T(8,128)(2,1)S(1)}, bf16[1280,384]{1,0:T(8,128)(2,1)}, u32[]{:S(2)}) copy-start(bf16[1280,384]{1,0:T(8,128)(2,1)} %get-tuple-element.42.refs_2_) | copy-start | bytes 2949124
  42.1 3.1 %copy-start.7 = (f32[416,128]{1,0:T(8,128)}, f32[416,128]{1,0:T(8,128)S(1)}, u32[]{:S(2)}) copy-start(f32[416,128]{1,0:T(8,128)S(1)} %get-tuple-element.47.refs_0_) | copy-start | bytes 638980
  42.1 3.1 %copy-start.9 = (bf16[256,128]{1,0:T(8,128)(2,1)}, bf16[256,128]{1,0:T(8,128)(2,1)S(1)}, u32[]{:S(2)}) copy-start(bf16[256,128]{1,0:T(8,128)(2,1)S(1)} %get-tuple-element.44) | copy-start | bytes 196612
  42.1 8.7 %collective-permute-start = (bf16[416,128]{1,0:T(8,128)(2,1)}, bf16[416,128]{1,0:T(8,128)(2,1)S(1)}, u32[]{:S(2)}, u32[]{:S(2)}) collective-permute-start(bf16[416,128]{1,0:T(8,128)(2,1)} %get-tuple-element.48), channel_id=1, source_target_pairs={{0,1},{1,0},{2,3},{3,2},{4,5},{5,4},{6,7},{7,6},{8,9},{9,8},{10,11... | collective-permute-start | bytes 319496 | tf_op jit(solution)/shard_map/ppermute | solution.py:548
  42.4 9.6 %collective-permute-start.1 = (bf16[416,128]{1,0:T(8,128)(2,1)}, bf16[416,128]{1,0:T(8,128)(2,1)}, u32[]{:S(2)}, u32[]{:S(2)}) collective-permute-start(bf16[416,128]{1,0:T(8,128)(2,1)} %get-tuple-element.49), channel_id=1, source_target_pairs={{0,16},{1,17},{2,18},{3,19},{4,20},{5,21},{6,22},{7,23},{8,24},{9,... | collective-permute-start | bytes 319496 | tf_op jit(solution)/shard_map/ppermute | solution.py:548
  43.6 8.4 %collective-permute-start.2 = (bf16[416,128]{1,0:T(8,128)(2,1)}, bf16[416,128]{1,0:T(8,128)(2,1)}, u32[]{:S(2)}, u32[]{:S(2)}) collective-permute-start(bf16[416,128]{1,0:T(8,128)(2,1)} %get-tuple-element.50), channel_id=1, source_target_pairs={{0,17},{1,16},{2,19},{3,18},{4,21},{5,20},{6,23},{7,22},{8,25},{9,... | collective-permute-start | bytes 319496 | tf_op jit(solution)/shard_map/ppermute | solution.py:548
  46.0 5.3 %copy-start.10 = (bf16[256,128]{1,0:T(8,128)(2,1)S(1)}, bf16[256,128]{1,0:T(8,128)(2,1)}, u32[]{:S(2)}) copy-start(bf16[256,128]{1,0:T(8,128)(2,1)} %copy-done.9) | copy-start | bytes 196612
  47.2 4.8 %copy-start.8 = (f32[416,128]{1,0:T(8,128)S(1)}, f32[416,128]{1,0:T(8,128)}, u32[]{:S(2)}) copy-start(f32[416,128]{1,0:T(8,128)} %copy-done.7) | copy-start | bytes 638980
  48.4 6.1 %collective-permute-start.3 = (bf16[288,128]{1,0:T(8,128)(2,1)S(1)}, bf16[288,128]{1,0:T(8,128)(2,1)S(1)}, u32[]{:S(2)}, u32[]{:S(2)}) collective-permute-start(bf16[288,128]{1,0:T(8,128)(2,1)S(1)} %get-tuple-element.52), channel_id=1, source_target_pairs={{0,1},{1,0},{2,3},{3,2},{4,5},{5,4},{6,7},{7,6},{8,9},{9,8},{10,11... | collective-permute-start | bytes 221192 | tf_op jit(solution)/shard_map/ppermute | solution.py:548
  49.6 4.9 %collective-permute-start.4 = (bf16[288,128]{1,0:T(8,128)(2,1)S(1)}, bf16[288,128]{1,0:T(8,128)(2,1)S(1)}, u32[]{:S(2)}, u32[]{:S(2)}) collective-permute-start(bf16[288,128]{1,0:T(8,128)(2,1)S(1)} %get-tuple-element.53), channel_id=1, source_target_pairs={{0,16},{1,17},{2,18},{3,19},{4,20},{5,21},{6,22},{7,23},{8,24},{9,... | collective-permute-start | bytes 221192 | tf_op jit(solution)/shard_map/ppermute | solution.py:548
  50.9 4.4 %collective-permute-start.5 = (bf16[288,128]{1,0:T(8,128)(2,1)S(1)}, bf16[288,128]{1,0:T(8,128)(2,1)S(1)}, u32[]{:S(2)}, u32[]{:S(2)}) collective-permute-start(bf16[288,128]{1,0:T(8,128)(2,1)S(1)} %get-tuple-element.54), channel_id=1, source_target_pairs={{0,17},{1,16},{2,19},{3,18},{4,21},{5,20},{6,23},{7,22},{8,25},{9,... | collective-permute-start | bytes 221192 | tf_op jit(solution)/shard_map/ppermute | solution.py:548
  81.6 3.3 %collective-permute-start.6 = (bf16[8,96,128]{2,1,0:T(8,128)(2,1)S(1)}, bf16[8,96,128]{2,1,0:T(8,128)(2,1)S(1)}, u32[]{:S(2)}, u32[]{:S(2)}) collective-permute-start(bf16[8,96,128]{2,1,0:T(8,128)(2,1)S(1)} %all_to_all.27.refs_1_), channel_id=1, source_target_pairs={{0,1},{1,0},{2,3},{3,2},{4,5},{5,4},{6,7},{7,6},{8,9},{9,8},{10,11... | collective-permute-start | bytes 589832 | tf_op jit(solution)/shard_map/ppermute | solution.py:631

commit v4 on v3

--- a/solution.py
+++ b/solution.py
@@ -8,6 +8,14 @@
 
 F32, BF16, I32 = jnp.float32, jnp.bfloat16, jnp.int32
 LANES = 128
+ORDERS = {
+    16: (9, 7, 8, 12, 5, 4, 0, 6, 10, 13, 15, 2, 11, 3, 1, 14),
+    8: (4, 2, 6, 3, 0, 1, 5, 7),
+}
+
+
+def order_of(count):
+    return ORDERS.get(count, tuple(range(count)))
 
 
 class Sizes:
@@ -28,6 +36,9 @@
         self.early = (self.tap_rows + self.down_rows) // 2
         self.chunk = -(-(self.early + self.late) // (16 * devices)) * 16
         self.parts = [(s, c) for s in range(samples) for c in range(2)]
+        self.order = order_of(devices)
+        self.place = tuple(self.order.index(device) for device in range(devices))
+        self.ring = order_of(devices // 2)
         self.slot_rows = -(-self.slots // 8) * 8
 
 
@@ -70,6 +81,15 @@
     tiles, side, _, chan = x.shape
     x = x.astype(F32)
     return jnp.stack([x[:, r].reshape(tiles * side, chan) for r in range(side)], axis=0)
+
+
+def relabel(values, table):
+    if table == tuple(range(len(table))):
+        return values
+    new = jnp.zeros_like(values)
+    for old, label in enumerate(table):
+        new = jnp.where(values == old, label, new)
+    return new
 
 
 def sender_index(me, owners, local_ids, turns, z):
@@ -93,7 +113,7 @@
     slot = jnp.where(slot < z.slot_rows, slot, slot - z.slot_rows)
     placed = jnp.where(slot.astype(F32) == rank, both(code), 0.0)
     row = iota((1, z.sent), 1)
-    device, at = lax.div(row, z.pair), lax.rem(row, z.pair)
+    device, at = relabel(lax.div(row, z.pair), z.order), lax.rem(row, z.pair)
     cube = (z.devices, z.tiles, z.sent)
     rows = mm(placed, flag(iota(cube, 0) == device.reshape(1, 1, z.sent)).reshape(requests, z.sent))
     edges = z.slots * z.side
@@ -177,7 +197,7 @@
     own = lax.dot_general(
         mine, owners.astype(F32).astype(BF16), (((1,), (1,)), ((), ())), preferred_element_type=F32
     )
-    index = receiver_index(own.astype(I32), z)
+    index = receiver_index(relabel(own.astype(I32), z.place), z)
     table_ref[8:16, : z.cells_up] = jnp.transpose(index.astype(F32))[0:8].astype(I32)
     cell = iota((16, z.cells_up), 1) + 1
     digits = jnp.where(iota((16, z.cells_up), 0) < 8, cell >> 4, cell & 15).astype(F32)
@@ -405,8 +425,9 @@
 def sum_kernel(z, got_ref, out_ref):
     sums = []
     for core in range(2):
-        total = got_ref[core, z.pair :, :].astype(F32)
-        for k in range(core + 2, z.devices, 2):
+        first, *rest = [z.place[device] for device in range(core, z.devices, 2)]
+        total = got_ref[first, z.pair :, :].astype(F32)
+        for k in rest:
             total = total + got_ref[k, z.pair :, :].astype(F32)
         sums.append(total.astype(BF16))
     for k in range(z.devices // 2):
@@ -428,8 +449,9 @@
     for core in range(2):
         rows = slice(core * z.chunk, (core + 1) * z.chunk)
         a, b = mine[:, rows], other[:, rows]
-        pairs = jnp.stack([jnp.where(first, a, b), jnp.where(first, b, a)], axis=1)
-        halves.append(pairs.reshape(z.devices * z.chunk, z.chan))
+        by_core = jnp.where(first, a, b), jnp.where(first, b, a)
+        chunks = [by_core[device % 2][z.ring.index(device // 2)] for device in z.order]
+        halves.append(jnp.concatenate(chunks, axis=0))
     one_ref[...] = jnp.concatenate([half[z.early : z.early + z.late] for half in halves], axis=0)
     early = jnp.concatenate([half[: z.early] for half in halves], axis=0)
     two_ref[...] = early[: z.tap_rows]
@@ -533,8 +555,8 @@
     return shape, dtype, True
 
 
-def exchange(x):
-    return lax.all_to_all(x, "tile", split_axis=0, concat_axis=0, tiled=True)
+def exchange(x, groups):
+    return lax.all_to_all(x, "tile", split_axis=0, concat_axis=0, tiled=True, axis_index_groups=groups)
 
 
 def deal(others, z):
@@ -572,9 +594,11 @@
     bind = functools.partial
     tables = (edge_owner.T, corner_owner.T, neighbour_tile.T, seam_rotation.T)
     others = len(z.parts) - 1
+    everyone = [list(z.order)]
+    same_core = [[2 * chip + core for chip in z.ring] for core in range(2)]
 
     (send,) = call(bind(pack_kernel, z), [sent_far], scalars=1, fetch=5, name="pack")(me, *tables, tiles_in)
-    got = exchange(send)
+    got = exchange(send, everyone)
     cot_rows = cot.transpose(1, 0, 2, 3).reshape(down_pixels, chan)
     index, back_second, turned_first, turned_second = call(
         bind(side_kernel, z),
@@ -590,12 +614,12 @@
     send, hidden, columns_first = call(
         bind(first_kernel, z), [sent, field16, columns], side_columns, name="first"
     )(got, index, tiles_in, w_first)
-    got = exchange(send)
+    got = exchange(send, everyone)
     (slope_in,) = call(bind(again_kernel, z), [field], name="again")(columns_first, w_first)
     send, slope_second, hidden_second, columns_second = call(
         bind(second_kernel, z), [sent_far, field16, field16, columns_far], side_columns + (flat,), name="second"
     )(got, index, hidden, w_second, turned_second, back_second)
-    got = exchange(send)
+    got = exchange(send, everyone)
     (inner,) = call(bind(inner_kernel, z), [field], (wide,), name="inner")(slope_second, turned_second)
     features, early_own, *early_other = call(
         bind(early_kernel, z, scale),
@@ -623,10 +647,9 @@
         (vmem(z.devices * z.chunk, chan),),
         name="join",
     )(send, early, late_own, *late_got)
-    got = exchange(send)
+    got = exchange(send, everyone)
     (chunk,) = call(bind(sum_kernel, z), [array(z.devices // 2, 2 * z.chunk, chan, dtype=BF16)], name="sum")(got)
-    same_core = [list(range(core, z.devices, 2)) for core in range(2)]
-    mine = lax.all_to_all(chunk, "tile", split_axis=0, concat_axis=0, tiled=True, axis_index_groups=same_core)
+    mine = exchange(chunk, same_core)
     (input_grad,) = call(bind(input_kernel, z), [array(tiles, side, side, chan)], name="input")(got, index, inner)
     other = lax.ppermute(mine, "tile", [(t, t ^ 1) for t in range(z.devices)])
     grad_first, grad_second, grad_down = call(

time: 86.3 us -> 78.3 us (0.907)
  blocking collectives: 37.3 us -> 33.2 us
  waiting for transfers between devices: 7.11 us -> 3.9 us
    all_to_all x3, blocking collectives: 37.3 us -> 33.2 us  [exchange(): lax.all_to_all(x, 'tile', split_axis=0, concat_axis=0, tiled=True, axis_i...]
    all_to_all x2, waiting for transfers between devices: 6.34 us -> 3.08 us  [exchange(): lax.all_to_all(x, 'tile', split_axis=0, concat_axis=0, tiled=True, axis_i...]
  transfers between devices with their start and end apart: 9 -> 9, of which waited for: 3 -> 2; matrix products, arithmetic and copies ran while one was open for 1% -> 1% of each run, Pallas kernels for 11% -> 13%
where the time goes in v4:
time: 78.3 us; the launch traced here: 77.8 us
  blocking collectives  33.2 us (42%)
  starting transfers between devices  18.3 us (23%)
  Pallas kernels  17.8 us (23%)
  waiting for transfers between devices  3.9 us (5%)
  local copies, waits for them, and re-layouts  3.53 us (5%)
  between operations  0.98 us (1%)
    all_to_all x3, blocking collectives, exchange(): lax.all_to_all(x, 'tile', split_axis=0, concat_axis=0, tiled=True, axis_i...  33.2 us
    pallas_call x15, Pallas kernels, run(): pl.pallas_call(kernel, out_shape=[pltpu.HBM(out[0], out[1]) if is_far els...  17.8 us
    all_to_all x2, starting transfers between devices, exchange(): lax.all_to_all(x, 'tile', split_axis=0, concat_axis=0, tiled=True, axis_i...  11.6 us
    ppermute x6, starting transfers between devices, deal(): got.append(lax.ppermute(others[k], ('dp', 'tile'), pairs))  4.41 us
    all_to_all x2, waiting for transfers between devices, exchange(): lax.all_to_all(x, 'tile', split_axis=0, concat_axis=0, tiled=True, axis_i...  3.08 us
    unnamed x32, local copies, waits for them, and re-layouts  2.86 us
    ppermute x1, starting transfers between devices, local(): other = lax.ppermute(mine, 'tile', [(t, t ^ 1) for t in range(z.devices)])  2.32 us
  transfers between devices with their start and end apart: 9, of which 2 were waited for; matrix products, arithmetic and copies ran while one was open for 1% of the time, Pallas kernels for 13%

profile of v4, /device:TPU:1, one launch (start us, length us, event | category | flops | bytes accessed | tf_op | source)
XLA Modules:
  0.0 77.8 jit_solution(14525426862568503280)
XLA Ops:
  0.6 0.0 copy-start.1
  0.6 2.3 %pack.1 = bf16[16,48,128]{2,1,0:T(8,128)(2,1)} custom-call(s32[1]{0:T(128)} %bitcast.1.refs_0_.refs_1_, s32[4,256]{1,0:T(4,128)} %bitcast.26, s32[4,256]{1,0:T(4,128)} %bitcast.28, s32[8,256]{1,0:T(8,128)} %bitcast.22, s32[8,256]{1,0:T(8,128)} %bitcast.24, bf16[16,8,8,128]{3,2,1,0:T(8,128)(2,1)} %bitcast.17), custom_call_target="tpu_custom_call" | custom-call | tf_op jit(solution)/shard_map/pack/pallas_call | solution.py:531
  2.9 0.0 copy-start.15
  2.9 0.0 copy-start
  2.9 0.0 copy-start.11
  3.0 0.0 copy-start.12
  3.0 0.0 copy-start.13
  3.0 0.0 copy-start.14
  3.0 7.4 %all-to-all-start = ((bf16[16,48,128]{2,1,0:T(8,128)(2,1)}), bf16[16,48,128]{2,1,0:T(8,128)(2,1)S(1)}, u32[]{:S(2)}, u32[]{:S(2)}) async-start(bf16[16,48,128]{2,1,0:T(8,128)(2,1)} %pack.1), calls=%async_computation | async-start | bytes 393216 | tf_op jit(solution)/shard_map/all_to_all | solution.py:559
  10.4 0.0 copy-done.15
  10.5 0.0 copy-done.1
  10.5 0.0 copy-done
  10.5 0.0 copy-done.11
  10.5 0.0 copy-done.12
  10.5 0.0 copy-done.13
  10.5 0.0 copy-done.14
  10.5 0.8 %copy-done.6 = bf16[512,128]{1,0:T(8,128)(2,1)S(1)} copy-done((bf16[512,128]{1,0:T(8,128)(2,1)S(1)}, bf16[512,128]{1,0:T(8,128)(2,1)}, u32[]{:S(2)}) %copy-start.6) | copy-done | bytes 131096
  11.3 1.4 %aside.1 = (s32[24,768]{1,0:T(8,128)S(1)}, f32[1024,128]{1,0:T(8,128)S(1)}, bf16[1152,128]{1,0:T(8,128)(2,1)S(1)}, bf16[1152,128]{1,0:T(8,128)(2,1)S(1)}) custom-call(s32[1]{0:T(128)} %bitcast.1.refs_0_.refs_1_, s32[4,256]{1,0:T(4,128)S(1)} %bitcast.27, s32[4,256]{1,0:T(4,128)S(1)} %bitcast.29, s32[8,256]{1,0:T(8,128)S(1)} %bitcast.23, ...), custom_call_target="tpu_custom_call" | custom-call | tf_op jit(solution)/shard_map/aside/pallas_call | solution.py:531
  12.8 0.0 copy-start.4
  12.8 0.8 %copy-done.4 = f32[1024,128]{1,0:T(8,128)} copy-done((f32[1024,128]{1,0:T(8,128)}, f32[1024,128]{1,0:T(8,128)S(1)}, u32[]{:S(2)}) %copy-start.4) | copy-done | bytes 524312
  13.6 3.1 %all-to-all-done.refs_0_ = bf16[16,48,128]{2,1,0:T(8,128)(2,1)S(1)} async-done(((bf16[16,48,128]{2,1,0:T(8,128)(2,1)}), bf16[16,48,128]{2,1,0:T(8,128)(2,1)S(1)}, u32[]{:S(2)}, u32[]{:S(2)}) %all-to-all-start) | async-done | bytes 196640 | tf_op jit(solution)/shard_map/all_to_all | solution.py:559
  16.6 0.0 copy-done.2
  16.7 1.8 %first.1 = (bf16[16,48,128]{2,1,0:T(8,128)(2,1)S(1)}, bf16[1024,128]{1,0:T(8,128)(2,1)S(1)}, bf16[1280,384]{1,0:T(8,128)(2,1)S(1)}) custom-call(bf16[16,48,128]{2,1,0:T(8,128)(2,1)S(1)} %all-to-all-done.refs_0_, s32[24,768]{1,0:T(8,128)S(1)} %get-tuple-element.32.refs_1_.refs_3_.refs_2_, bf16[16,8,8,128]{3,2,1,0:T(8,128)(2,1)S(1)} %bitcast.18, ...), custom_call_target="tpu_custom_call" | custom-call | tf_op jit(solution)/shard_map/first/pallas_call | solution.py:531
  18.5 10.0 %all_to_all.25.refs_0_ = bf16[16,48,128]{2,1,0:T(8,128)(2,1)S(1)} all-to-all(bf16[16,48,128]{2,1,0:T(8,128)(2,1)S(1)} %get-tuple-element.33), channel_id=1, replica_groups={{9,7,8,12,5,4,0,6,10,13,15,2,11,3,1,14},{25,23,24,28,21,20,16,22,26,29,..., dimensions={0} | all-to-all | bytes 393216 | tf_op jit(solution)/shard_map/all_to_all | solution.py:559
  28.5 0.0 copy-done.5
  28.5 2.8 %second.1 = (bf16[16,48,128]{2,1,0:T(8,128)(2,1)}, bf16[1024,128]{1,0:T(8,128)(2,1)S(1)}, bf16[1024,128]{1,0:T(8,128)(2,1)S(1)}, bf16[1280,384]{1,0:T(8,128)(2,1)}) custom-call(bf16[16,48,128]{2,1,0:T(8,128)(2,1)S(1)} %all_to_all.25.refs_0_, s32[24,768]{1,0:T(8,128)S(1)} %get-tuple-element.32.refs_1_.refs_3_.refs_2_, ...), custom_call_target="tpu_custom_call" | custom-call | tf_op jit(solution)/shard_map/second/pallas_call | solution.py:531
  31.3 4.2 %all-to-all-start.2 = ((bf16[16,48,128]{2,1,0:T(8,128)(2,1)}), bf16[16,48,128]{2,1,0:T(8,128)(2,1)S(1)}, u32[]{:S(2)}, u32[]{:S(2)}) async-start(bf16[16,48,128]{2,1,0:T(8,128)(2,1)} %get-tuple-element.37), calls=%async_computation.2 | async-start | bytes 393216 | tf_op jit(solution)/shard_map/all_to_all | solution.py:559
  35.5 1.2 %copy-done.3 = bf16[1280,384]{1,0:T(8,128)(2,1)S(1)} copy-done((bf16[1280,384]{1,0:T(8,128)(2,1)S(1)}, bf16[1280,384]{1,0:T(8,128)(2,1)}, u32[]{:S(2)}) %copy-start.3) | copy-done | bytes 983064
  36.7 1.7 %early.1 = (bf16[256,128]{1,0:T(8,128)(2,1)S(1)}, f32[416,128]{1,0:T(8,128)S(1)}, bf16[416,128]{1,0:T(8,128)(2,1)}, bf16[416,128]{1,0:T(8,128)(2,1)}, bf16[416,128]{1,0:T(8,128)(2,1)}) custom-call(s32[1]{0:T(128)} %bitcast.refs_0_, s32[1]{0:T(128)} %bitcast.1.refs_0_.refs_1_, bf16[1280,384]{1,0:T(8,128)(2,1)S(1)} %copy-done.3, ...), custom_call_target="tpu_custom_call" | custom-call | tf_op jit(solution)/shard_map/early/pallas_call | solution.py:531
  38.4 0.0 copy-start.7
  38.4 0.0 copy-start.9
  38.4 0.4 collective-permute-start
  38.8 1.2 %collective-permute-start.1 = (bf16[416,128]{1,0:T(8,128)(2,1)}, bf16[416,128]{1,0:T(8,128)(2,1)}, u32[]{:S(2)}, u32[]{:S(2)}) collective-permute-start(bf16[416,128]{1,0:T(8,128)(2,1)} %get-tuple-element.49), channel_id=1, source_target_pairs={{0,16},{1,17},{2,18},{3,19},{4,20},{5,21},{6,22},{7,23},{8,24},{9,... | collective-permute-start | bytes 319496 | tf_op jit(solution)/shard_map/ppermute | solution.py:570
  40.1 0.6 collective-permute-start.2
  40.6 0.9 %again.1.refs_5_ = f32[1024,128]{1,0:T(8,128)S(1)} custom-call(bf16[1280,384]{1,0:T(8,128)(2,1)S(1)} %get-tuple-element.39.refs_0_.refs_6_, bf16[1152,128]{1,0:T(8,128)(2,1)S(1)} %copy-done), custom_call_target="tpu_custom_call" | custom-call | tf_op jit(solution)/shard_map/again/pallas_call | solution.py:531
  41.5 0.0 copy-done.7
  41.5 0.0 copy-done.9
  41.5 0.8 %inner.2.refs_4_ = f32[1024,128]{1,0:T(8,128)S(1)} custom-call(bf16[1024,128]{1,0:T(8,128)(2,1)S(1)} %get-tuple-element.38.refs_0_.refs_3_, bf16[1152,128]{1,0:T(8,128)(2,1)S(1)} %get-tuple-element.35.refs_4_.refs_1_), custom_call_target="tpu_custom_call" | custom-call | tf_op jit(solution)/shard_map/inner/pallas_call | solution.py:531
  42.4 0.0 copy-start.10
  42.4 0.0 all-to-all-done.2.refs_2_
  42.4 0.0 copy-start.8
  42.4 1.2 %slope.1 = (bf16[1024,128]{1,0:T(8,128)(2,1)S(1)}, f32[288,128]{1,0:T(8,128)S(1)}, bf16[288,128]{1,0:T(8,128)(2,1)S(1)}, bf16[288,128]{1,0:T(8,128)(2,1)S(1)}, bf16[288,128]{1,0:T(8,128)(2,1)S(1)}) custom-call(s32[1]{0:T(128)} %bitcast.refs_0_, s32[1]{0:T(128)} %bitcast.1.refs_0_.refs_1_, bf16[16,48,128]{2,1,0:T(8,128)(2,1)S(1)} %all-to-all-done.2.refs_2_, ...), custom_call_target="tpu_custom_call" | custom-call | tf_op jit(solution)/shard_map/slope/pallas_call | solution.py:531
  43.6 0.1 collective-permute-start.3
  43.7 1.3 %collective-permute-start.4 = (bf16[288,128]{1,0:T(8,128)(2,1)S(1)}, bf16[288,128]{1,0:T(8,128)(2,1)S(1)}, u32[]{:S(2)}, u32[]{:S(2)}) collective-permute-start(bf16[288,128]{1,0:T(8,128)(2,1)S(1)} %get-tuple-element.53), channel_id=1, source_target_pairs={{0,16},{1,17},{2,18},{3,19},{4,20},{5,21},{6,22},{7,23},{8,24},{9,... | collective-permute-start | bytes 221192 | tf_op jit(solution)/shard_map/ppermute | solution.py:570
  44.9 0.0 collective-permute-done.refs_1_
  44.9 0.8 %collective-permute-start.5 = (bf16[288,128]{1,0:T(8,128)(2,1)S(1)}, bf16[288,128]{1,0:T(8,128)(2,1)S(1)}, u32[]{:S(2)}, u32[]{:S(2)}) collective-permute-start(bf16[288,128]{1,0:T(8,128)(2,1)S(1)} %get-tuple-element.54), channel_id=1, source_target_pairs={{0,17},{1,16},{2,19},{3,18},{4,21},{5,20},{6,23},{7,22},{8,25},{9,... | collective-permute-start | bytes 221192 | tf_op jit(solution)/shard_map/ppermute | solution.py:570
  45.8 0.7 copy.17
  46.4 0.0 collective-permute-done.1.refs_2_
  46.4 0.0 collective-permute-done.2.refs_3_
  46.4 0.0 copy-done.8
  46.4 1.0 %gain.1.refs_1_ = f32[416,128]{1,0:T(8,128)S(1)} custom-call(f32[416,128]{1,0:T(8,128)S(1)} %copy-done.8, bf16[416,128]{1,0:T(8,128)(2,1)S(1)} %collective-permute-done.refs_1_, bf16[416,128]{1,0:T(8,128)(2,1)} %collective-permute-done.1.refs_2_, bf16[416,128]{1,0:T(8,128)(2,1)} %collective-permute-done.2.refs_3_), custom_call_target="tpu_custom_call" | custom-call | tf_op jit(solution)/shard_map/gain/pallas_call | solution.py:531
  47.5 0.8 %inner.3.refs_2_ = f32[1024,128]{1,0:T(8,128)S(1)} custom-call(bf16[1024,128]{1,0:T(8,128)(2,1)S(1)} %get-tuple-element.40.refs_0_, bf16[1152,128]{1,0:T(8,128)(2,1)S(1)} %get-tuple-element.41.refs_1_), custom_call_target="tpu_custom_call" | custom-call | tf_op jit(solution)/shard_map/inner/pallas_call | solution.py:531
  48.3 0.6 last.1.refs_0_
  48.9 0.0 collective-permute-done.3.refs_3_
  49.0 0.0 collective-permute-done.4.refs_4_
  49.0 0.8 %collective-permute-done.5.refs_5_ = bf16[288,128]{1,0:T(8,128)(2,1)S(1)} collective-permute-done((bf16[288,128]{1,0:T(8,128)(2,1)S(1)}, bf16[288,128]{1,0:T(8,128)(2,1)S(1)}, u32[]{:S(2)}, u32[]{:S(2)}) %collective-permute-start.5) | collective-permute-done | bytes 73760 | tf_op jit(solution)/shard_map/ppermute | solution.py:570
  49.8 0.1 join.1
  49.9 15.0 %all_to_all.26.refs_0_ = bf16[16,96,128]{2,1,0:T(8,128)(2,1)S(1)} all-to-all(bf16[16,96,128]{2,1,0:T(8,128)(2,1)S(1)} %join.1), channel_id=1, replica_groups={{9,7,8,12,5,4,0,6,10,13,15,2,11,3,1,14},{25,23,24,28,21,20,16,22,26,29,..., dimensions={0} | all-to-all | bytes 786432 | tf_op jit(solution)/shard_map/all_to_all | solution.py:559
  64.9 0.1 sum.1
  64.9 8.2 %all_to_all.27.refs_1_ = bf16[8,96,128]{2,1,0:T(8,128)(2,1)S(1)} all-to-all(bf16[8,96,128]{2,1,0:T(8,128)(2,1)S(1)} %sum.1), channel_id=1, replica_groups={{8,4,12,6,0,2,10,14},{9,5,13,7,1,3,11,15},{24,20,28,22,16,18,26,30},{25..., dimensions={0} | all-to-all | bytes 393216 | tf_op jit(solution)/shard_map/all_to_all | solution.py:559
  73.2 2.3 %collective-permute-start.6 = (bf16[8,96,128]{2,1,0:T(8,128)(2,1)S(1)}, bf16[8,96,128]{2,1,0:T(8,128)(2,1)S(1)}, u32[]{:S(2)}, u32[]{:S(2)}) collective-permute-start(bf16[8,96,128]{2,1,0:T(8,128)(2,1)S(1)} %all_to_all.27.refs_1_), channel_id=1, source_target_pairs={{0,1},{1,0},{2,3},{3,2},{4,5},{5,4},{6,7},{7,6},{8,9},{9,8},{10,11... | collective-permute-start | bytes 589832 | tf_op jit(solution)/shard_map/ppermute | solution.py:654
  75.5 1.4 %input.1 = f32[16,8,8,128]{3,2,1,0:T(8,128)} custom-call(bf16[16,96,128]{2,1,0:T(8,128)(2,1)S(1)} %all_to_all.26.refs_0_, s32[24,768]{1,0:T(8,128)S(1)} %get-tuple-element.32.refs_1_.refs_3_.refs_2_, f32[1024,128]{1,0:T(8,128)S(1)} %inner.3.refs_2_), custom_call_target="tpu_custom_call" | custom-call | tf_op jit(solution)/shard_map/input/pallas_call | solution.py:531
  76.9 0.0 collective-permute-done.6.refs_2_
  76.9 0.9 %spread.1 = (f32[576,128]{1,0:T(8,128)}, f32[576,128]{1,0:T(8,128)}, f32[256,128]{1,0:T(8,128)}) custom-call(s32[1]{0:T(128)} %bitcast.1.refs_0_.refs_1_, bf16[8,96,128]{2,1,0:T(8,128)(2,1)S(1)} %all_to_all.27.refs_1_, bf16[8,96,128]{2,1,0:T(8,128)(2,1)S(1)} %collective-permute-done.6.refs_2_), custom_call_target="tpu_custom_call" | custom-call | tf_op jit(solution)/shard_map/spread/pallas_call | solution.py:531
  (6 shorter events, 0.0 us)
Async XLA Ops:
  0.6 9.8 %copy-start.1 = (bf16[1152,128]{1,0:T(8,128)(2,1)S(1)}, bf16[1152,128]{1,0:T(8,128)(2,1)}, u32[]{:S(2)}) copy-start(bf16[1152,128]{1,0:T(8,128)(2,1)} %refs_3_.3) | copy-start | bytes 884740
  2.9 7.5 %copy-start.15 = (bf16[1,16,4,4,128]{4,3,2,1,0:T(4,128)(2,1)S(1)}, bf16[1,16,4,4,128]{4,3,2,1,0:T(4,128)(2,1)}, u32[]{:S(2)}) copy-start(bf16[1,16,4,4,128]{4,3,2,1,0:T(4,128)(2,1)} %param.10) | copy-start | bytes 196612
  2.9 7.5 %copy-start = (bf16[1152,128]{1,0:T(8,128)(2,1)S(1)}, bf16[1152,128]{1,0:T(8,128)(2,1)}, u32[]{:S(2)}) copy-start(bf16[1152,128]{1,0:T(8,128)(2,1)} %refs_1_.1) | copy-start | bytes 884740
  2.9 7.5 %copy-start.11 = (s32[256,8]{0,1:T(8,128)S(1)}, s32[256,8]{0,1:T(8,128)}, u32[]{:S(2)}) copy-start(s32[256,8]{0,1:T(8,128)} %param.16) | copy-start | bytes 24580
  3.0 7.5 %copy-start.12 = (s32[256,8]{0,1:T(8,128)S(1)}, s32[256,8]{0,1:T(8,128)}, u32[]{:S(2)}) copy-start(s32[256,8]{0,1:T(8,128)} %param.17) | copy-start | bytes 24580
  3.0 7.5 %copy-start.13 = (s32[256,4]{0,1:T(4,128)S(1)}, s32[256,4]{0,1:T(4,128)}, u32[]{:S(2)}) copy-start(s32[256,4]{0,1:T(4,128)} %param.14) | copy-start | bytes 12292
  3.0 7.5 %copy-start.14 = (s32[256,4]{0,1:T(4,128)S(1)}, s32[256,4]{0,1:T(4,128)}, u32[]{:S(2)}) copy-start(s32[256,4]{0,1:T(4,128)} %param.15) | copy-start | bytes 12292
  3.0 13.7 %all-to-all-start = ((bf16[16,48,128]{2,1,0:T(8,128)(2,1)}), bf16[16,48,128]{2,1,0:T(8,128)(2,1)S(1)}, u32[]{:S(2)}, u32[]{:S(2)}) async-start(bf16[16,48,128]{2,1,0:T(8,128)(2,1)} %pack.1), calls=%async_computation | async-start | bytes 393216 | tf_op jit(solution)/shard_map/all_to_all | solution.py:559
  10.4 0.9 %copy-start.6 = (bf16[512,128]{1,0:T(8,128)(2,1)S(1)}, bf16[512,128]{1,0:T(8,128)(2,1)}, u32[]{:S(2)}) copy-start(bf16[512,128]{1,0:T(8,128)(2,1)} %refs_6_.3) | copy-start | bytes 393220
  11.3 5.3 %copy-start.2 = (bf16[1,16,8,8,128]{4,3,2,1,0:T(8,128)(2,1)S(1)}, bf16[1,16,8,8,128]{4,3,2,1,0:T(8,128)(2,1)}, u32[]{:S(2)}) copy-start(bf16[1,16,8,8,128]{4,3,2,1,0:T(8,128)(2,1)} %param.9) | copy-start | bytes 786436
  12.8 0.8 %copy-start.4 = (f32[1024,128]{1,0:T(8,128)}, f32[1024,128]{1,0:T(8,128)S(1)}, u32[]{:S(2)}) copy-start(f32[1024,128]{1,0:T(8,128)S(1)} %get-tuple-element.36.refs_5_) | copy-start | bytes 1572868
  16.6 11.8 %copy-start.5 = (f32[1024,128]{1,0:T(8,128)S(1)}, f32[1024,128]{1,0:T(8,128)}, u32[]{:S(2)}) copy-start(f32[1024,128]{1,0:T(8,128)} %copy-done.4) | copy-start | bytes 1572868
  31.3 11.0 %all-to-all-start.2 = ((bf16[16,48,128]{2,1,0:T(8,128)(2,1)}), bf16[16,48,128]{2,1,0:T(8,128)(2,1)S(1)}, u32[]{:S(2)}, u32[]{:S(2)}) async-start(bf16[16,48,128]{2,1,0:T(8,128)(2,1)} %get-tuple-element.37), calls=%async_computation.2 | async-start | bytes 393216 | tf_op jit(solution)/shard_map/all_to_all | solution.py:559
  35.5 1.2 %copy-start.3 = (bf16[1280,384]{1,0:T(8,128)(2,1)S(1)}, bf16[1280,384]{1,0:T(8,128)(2,1)}, u32[]{:S(2)}) copy-start(bf16[1280,384]{1,0:T(8,128)(2,1)} %get-tuple-element.42.refs_2_) | copy-start | bytes 2949124
  38.4 3.1 %copy-start.7 = (f32[416,128]{1,0:T(8,128)}, f32[416,128]{1,0:T(8,128)S(1)}, u32[]{:S(2)}) copy-start(f32[416,128]{1,0:T(8,128)S(1)} %get-tuple-element.47.refs_0_) | copy-start | bytes 638980
  38.4 3.1 %copy-start.9 = (bf16[256,128]{1,0:T(8,128)(2,1)}, bf16[256,128]{1,0:T(8,128)(2,1)S(1)}, u32[]{:S(2)}) copy-start(bf16[256,128]{1,0:T(8,128)(2,1)S(1)} %get-tuple-element.44) | copy-start | bytes 196612
  38.4 6.5 %collective-permute-start = (bf16[416,128]{1,0:T(8,128)(2,1)}, bf16[416,128]{1,0:T(8,128)(2,1)S(1)}, u32[]{:S(2)}, u32[]{:S(2)}) collective-permute-start(bf16[416,128]{1,0:T(8,128)(2,1)} %get-tuple-element.48), channel_id=1, source_target_pairs={{0,1},{1,0},{2,3},{3,2},{4,5},{5,4},{6,7},{7,6},{8,9},{9,8},{10,11... | collective-permute-start | bytes 319496 | tf_op jit(solution)/shard_map/ppermute | solution.py:570
  38.8 7.6 %collective-permute-start.1 = (bf16[416,128]{1,0:T(8,128)(2,1)}, bf16[416,128]{1,0:T(8,128)(2,1)}, u32[]{:S(2)}, u32[]{:S(2)}) collective-permute-start(bf16[416,128]{1,0:T(8,128)(2,1)} %get-tuple-element.49), channel_id=1, source_target_pairs={{0,16},{1,17},{2,18},{3,19},{4,20},{5,21},{6,22},{7,23},{8,24},{9,... | collective-permute-start | bytes 319496 | tf_op jit(solution)/shard_map/ppermute | solution.py:570
  40.1 6.4 %collective-permute-start.2 = (bf16[416,128]{1,0:T(8,128)(2,1)}, bf16[416,128]{1,0:T(8,128)(2,1)}, u32[]{:S(2)}, u32[]{:S(2)}) collective-permute-start(bf16[416,128]{1,0:T(8,128)(2,1)} %get-tuple-element.50), channel_id=1, source_target_pairs={{0,17},{1,16},{2,19},{3,18},{4,21},{5,20},{6,23},{7,22},{8,25},{9,... | collective-permute-start | bytes 319496 | tf_op jit(solution)/shard_map/ppermute | solution.py:570
  42.4 3.4 %copy-start.10 = (bf16[256,128]{1,0:T(8,128)(2,1)S(1)}, bf16[256,128]{1,0:T(8,128)(2,1)}, u32[]{:S(2)}) copy-start(bf16[256,128]{1,0:T(8,128)(2,1)} %copy-done.9) | copy-start | bytes 196612
  42.4 4.1 %copy-start.8 = (f32[416,128]{1,0:T(8,128)S(1)}, f32[416,128]{1,0:T(8,128)}, u32[]{:S(2)}) copy-start(f32[416,128]{1,0:T(8,128)} %copy-done.7) | copy-start | bytes 638980
  43.6 5.4 %collective-permute-start.3 = (bf16[288,128]{1,0:T(8,128)(2,1)S(1)}, bf16[288,128]{1,0:T(8,128)(2,1)S(1)}, u32[]{:S(2)}, u32[]{:S(2)}) collective-permute-start(bf16[288,128]{1,0:T(8,128)(2,1)S(1)} %get-tuple-element.52), channel_id=1, source_target_pairs={{0,1},{1,0},{2,3},{3,2},{4,5},{5,4},{6,7},{7,6},{8,9},{9,8},{10,11... | collective-permute-start | bytes 221192 | tf_op jit(solution)/shard_map/ppermute | solution.py:570
  43.7 5.3 %collective-permute-start.4 = (bf16[288,128]{1,0:T(8,128)(2,1)S(1)}, bf16[288,128]{1,0:T(8,128)(2,1)S(1)}, u32[]{:S(2)}, u32[]{:S(2)}) collective-permute-start(bf16[288,128]{1,0:T(8,128)(2,1)S(1)} %get-tuple-element.53), channel_id=1, source_target_pairs={{0,16},{1,17},{2,18},{3,19},{4,20},{5,21},{6,22},{7,23},{8,24},{9,... | collective-permute-start | bytes 221192 | tf_op jit(solution)/shard_map/ppermute | solution.py:570
  44.9 4.8 %collective-permute-start.5 = (bf16[288,128]{1,0:T(8,128)(2,1)S(1)}, bf16[288,128]{1,0:T(8,128)(2,1)S(1)}, u32[]{:S(2)}, u32[]{:S(2)}) collective-permute-start(bf16[288,128]{1,0:T(8,128)(2,1)S(1)} %get-tuple-element.54), channel_id=1, source_target_pairs={{0,17},{1,16},{2,19},{3,18},{4,21},{5,20},{6,23},{7,22},{8,25},{9,... | collective-permute-start | bytes 221192 | tf_op jit(solution)/shard_map/ppermute | solution.py:570
  73.2 3.7 %collective-permute-start.6 = (bf16[8,96,128]{2,1,0:T(8,128)(2,1)S(1)}, bf16[8,96,128]{2,1,0:T(8,128)(2,1)S(1)}, u32[]{:S(2)}, u32[]{:S(2)}) collective-permute-start(bf16[8,96,128]{2,1,0:T(8,128)(2,1)S(1)} %all_to_all.27.refs_1_), channel_id=1, source_target_pairs={{0,1},{1,0},{2,3},{3,2},{4,5},{5,4},{6,7},{7,6},{8,9},{9,8},{10,11... | collective-permute-start | bytes 589832 | tf_op jit(solution)/shard_map/ppermute | solution.py:654

commit v5 on v4

--- a/solution.py
+++ b/solution.py
@@ -9,8 +9,8 @@
 F32, BF16, I32 = jnp.float32, jnp.bfloat16, jnp.int32
 LANES = 128
 ORDERS = {
-    16: (9, 7, 8, 12, 5, 4, 0, 6, 10, 13, 15, 2, 11, 3, 1, 14),
-    8: (4, 2, 6, 3, 0, 1, 5, 7),
+    16: (9, 7, 8, 12, 5, 4, 0, 13, 10, 15, 6, 2, 11, 3, 1, 14),
+    8: (5, 2, 0, 6, 1, 7, 3, 4),
 }
 
 
@@ -220,14 +220,20 @@
 
 def padded_columns(z, center, arrived, index, west_ref, east_ref, out_ref):
     rims = gather(index, arrived)
-    north, south = rims[: z.line], rims[z.line : 2 * z.line]
     at = 2 * z.line
-    west_ref[pl.ds(0, z.column, stride=z.side), :] = rims[at : at + z.column]
-    east_ref[pl.ds(z.side - 1, z.column, stride=z.side), :] = rims[at + z.column : at + 2 * z.column]
+    strip = jnp.concatenate([rims[: z.line], center, rims[z.line : at], rims[at : at + 2 * z.column]], axis=0)
+    fill_columns(z, strip, west_ref, east_ref, out_ref)
+    return strip
+
+
+def fill_columns(z, strip, west_ref, east_ref, out_ref):
+    rows = z.column * z.side
+    west_ref[pl.ds(0, z.column, stride=z.side), :] = strip[rows : rows + z.column]
+    east_ref[pl.ds(z.side - 1, z.column, stride=z.side), :] = strip[rows + z.column :]
     shape = (z.column, z.side, z.chan)
-    middle = jnp.concatenate([north, center, south], axis=0).reshape(shape)
+    middle = strip[:rows].reshape(shape)
     place = iota(shape, 1)
-    flat = (z.column * z.side, z.chan)
+    flat = (rows, z.chan)
     left = jnp.where(place == 0, west_ref[...].reshape(shape), pltpu.roll(middle, 1, 1))
     right = jnp.where(place == z.side - 1, east_ref[...].reshape(shape), pltpu.roll(middle, z.side - 1, 1))
     out_ref[:, : z.chan] = left.reshape(flat).astype(BF16)
@@ -252,16 +258,18 @@
     return s * (1.0 + v * (1.0 - s))
 
 
-def first_kernel(z, got_ref, index_ref, x_ref, w_ref, send_ref, hidden_ref, columns_ref, west_ref, east_ref):
+def first_kernel(z, got_ref, index_ref, x_ref, w_ref, send_ref, hidden_ref, strip_ref, columns_ref, west_ref, east_ref):
     center = row_first(x_ref[...]).reshape(z.pixels, z.chan)
-    padded_columns(z, center, got_ref[...].reshape(z.sent, z.chan), as_column(index_ref[8:9, : z.cells_up]), west_ref, east_ref, columns_ref)
+    strip = padded_columns(z, center, got_ref[...].reshape(z.sent, z.chan), as_column(index_ref[8:9, : z.cells_up]), west_ref, east_ref, columns_ref)
+    strip_ref[...] = strip.astype(BF16)
     v = conv(z, columns_ref, w_ref)
     hidden = (v / (1.0 + jnp.exp(-v))).astype(BF16)
     send_ref[...] = gather(as_column(index_ref[0:1, : z.sent]), hidden).astype(BF16).reshape(send_ref.shape)
     hidden_ref[...] = hidden
 
 
-def again_kernel(z, columns_ref, w_ref, slope_ref):
+def again_kernel(z, strip_ref, w_ref, slope_ref, columns_ref, west_ref, east_ref):
+    fill_columns(z, strip_ref[...].astype(F32), west_ref, east_ref, columns_ref)
     slope_ref[...] = silu_slope(conv(z, columns_ref, w_ref))
 
 
@@ -317,11 +325,11 @@
 
 def second_kernel(
     z, got_ref, index_ref, hidden_ref, w_ref, turned_ref, back_ref,
-    send_ref, slope_ref, out_ref, columns_ref, west_ref, east_ref, scratch_ref,
+    send_ref, slope_ref, out_ref, strip_ref, columns_ref, west_ref, east_ref, scratch_ref,
 ):
     center = hidden_ref[...].astype(F32)
-    padded_columns(z, center, got_ref[...].reshape(z.sent, z.chan), as_column(index_ref[8:9, : z.cells_up]), west_ref, east_ref, columns_ref)
-    push(columns_ref)
+    strip = padded_columns(z, center, got_ref[...].reshape(z.sent, z.chan), as_column(index_ref[8:9, : z.cells_up]), west_ref, east_ref, columns_ref)
+    strip_ref[...] = strip.astype(BF16)
     v = conv(z, columns_ref, w_ref)
     s = 1.0 / (1.0 + jnp.exp(-v))
     out_ref[...] = (v * s).astype(BF16)
@@ -356,12 +364,11 @@
 
 
 def early_kernel(
-    z, scale, sample_ref, me_ref, columns_ref, slope_ref, hidden_ref, cot_ref, wd_ref, feature_ref, own_ref, *refs
+    z, scale, sample_ref, me_ref, slope_ref, hidden_ref, cot_ref, wd_ref, strip_ref, feature_ref, own_ref, *refs
 ):
-    other_refs, (taps_ref, total_ref, flat_ref, block_ref) = refs[:-4], refs[-4:]
+    other_refs, (taps_ref, total_ref, flat_ref, block_ref, columns_ref, west_ref, east_ref) = refs[:-7], refs[-7:]
     chan, half = z.chan, z.side // 2
     part = half * z.tiles
-    tap_products(z, columns_ref, slope_ref[...], scale, taps_ref)
     flat_ref[...] = hidden_ref[...].astype(F32)
     for i in range(half):
         for p in range(2):
@@ -372,6 +379,8 @@
     block = block_ref[...]
     feature_ref[...] = jnp.dot(block, wd_ref[...], preferred_element_type=F32).astype(BF16)
     down = mm_t(block, cot_ref[...]) * scale
+    fill_columns(z, strip_ref[...].astype(F32), west_ref, east_ref, columns_ref)
+    tap_products(z, columns_ref, slope_ref[...], scale, taps_ref)
     both = z.tap_rows + z.down_rows
     for s in range(z.samples):
         total_ref[s * both : s * both + z.tap_rows, :] = taps_ref[s * z.tap_rows : (s + 1) * z.tap_rows, :]
@@ -585,7 +594,8 @@
     field, field16 = array(z.pixels, chan), array(z.pixels, chan, dtype=BF16)
     field16_far = far(z.pixels, chan, dtype=BF16)
     columns = array(z.column * side, 3 * chan, dtype=BF16)
-    columns_far = far(z.column * side, 3 * chan, dtype=BF16)
+    wide_columns = vmem(z.column * side, 3 * chan, dtype=BF16)
+    strip = array(z.column * (side + 2), chan, dtype=BF16)
     turned = array(9 * chan, chan, dtype=BF16)
     wide = vmem((side + 2) * z.line, 3 * chan, dtype=BF16)
     side_columns = (vmem(z.column * side, chan), vmem(z.column * side, chan))
@@ -611,23 +621,26 @@
         scalars=1,
         name="aside",
     )(me, *tables, cot_rows, w_down, w_first, w_second)
-    send, hidden, columns_first = call(
-        bind(first_kernel, z), [sent, field16, columns], side_columns, name="first"
+    send, hidden, strip_first = call(
+        bind(first_kernel, z), [sent, field16, strip], (wide_columns,) + side_columns, name="first"
     )(got, index, tiles_in, w_first)
     got = exchange(send, everyone)
-    (slope_in,) = call(bind(again_kernel, z), [field], name="again")(columns_first, w_first)
-    send, slope_second, hidden_second, columns_second = call(
-        bind(second_kernel, z), [sent_far, field16, field16, columns_far], side_columns + (flat,), name="second"
+    slope_in, columns_first = call(bind(again_kernel, z), [field, columns], side_columns, name="again")(
+        strip_first, w_first
+    )
+    send, slope_second, hidden_second, strip_second = call(
+        bind(second_kernel, z), [sent_far, field16, field16, strip], (wide_columns,) + side_columns + (flat,), name="second"
     )(got, index, hidden, w_second, turned_second, back_second)
     got = exchange(send, everyone)
     (inner,) = call(bind(inner_kernel, z), [field], (wide,), name="inner")(slope_second, turned_second)
     features, early_own, *early_other = call(
         bind(early_kernel, z, scale),
         [array(down_pixels, chan, dtype=BF16), array(z.early, chan)] + [array(z.early, chan, dtype=BF16)] * others,
-        (taps, vmem(2 * z.samples * z.early, chan), flat, vmem(down_pixels, 4 * chan, dtype=BF16)),
+        (taps, vmem(2 * z.samples * z.early, chan), flat, vmem(down_pixels, 4 * chan, dtype=BF16), wide_columns)
+        + side_columns,
         scalars=2,
         name="early",
-    )(sample, me, columns_second, slope_second, hidden_second, cot_rows, w_down)
+    )(sample, me, slope_second, hidden_second, cot_rows, w_down, strip_second)
     features = features.reshape(half, tiles, half, chan).transpose(1, 0, 2, 3)
     (early,) = call(gain_kernel, [array(z.early, chan)], name="gain")(early_own, *deal(early_other, z))
     slope_first, late_own, *late_other = call(

time: 78.3 us -> 76.9 us (0.982)
  local copies, waits for them, and re-layouts: 3.53 us -> 1.53 us
  waiting for transfers between devices: 3.9 us -> 5.08 us
    unnamed x32 -> x22, local copies, waits for them, and re-layouts: 2.86 us -> 0.85 us
    all_to_all x2, waiting for transfers between devices: 3.08 us -> 4.31 us  [exchange(): lax.all_to_all(x, 'tile', split_axis=0, concat_axis=0, tiled=True, axis_i...]
  transfers between devices with their start and end apart: 9 -> 9, of which waited for: 2 -> 3; matrix products, arithmetic and copies ran while one was open for 1% -> 1% of each run, Pallas kernels for 13% -> 13%
where the time goes in v5:
time: 76.9 us; the launch traced here: 76.4 us
  blocking collectives  32.5 us (42%)
  Pallas kernels  18.2 us (24%)
  starting transfers between devices  18.2 us (24%)
  waiting for transfers between devices  5.08 us (7%)
  local copies, waits for them, and re-layouts  1.53 us (2%)
  between operations  0.93 us (1%)
    all_to_all x3, blocking collectives, exchange(): lax.all_to_all(x, 'tile', split_axis=0, concat_axis=0, tiled=True, axis_i...  32.5 us
    pallas_call x15, Pallas kernels, run(): pl.pallas_call(kernel, out_shape=[pltpu.HBM(out[0], out[1]) if is_far els...  18.2 us
    all_to_all x2, starting transfers between devices, exchange(): lax.all_to_all(x, 'tile', split_axis=0, concat_axis=0, tiled=True, axis_i...  11.6 us
    ppermute x6, starting transfers between devices, deal(): got.append(lax.ppermute(others[k], ('dp', 'tile'), pairs))  4.41 us
    all_to_all x2, waiting for transfers between devices, exchange(): lax.all_to_all(x, 'tile', split_axis=0, concat_axis=0, tiled=True, axis_i...  4.31 us
    ppermute x1, starting transfers between devices, local(): other = lax.ppermute(mine, 'tile', [(t, t ^ 1) for t in range(z.devices)])  2.24 us
  transfers between devices with their start and end apart: 9, of which 3 were waited for; matrix products, arithmetic and copies ran while one was open for 1% of the time, Pallas kernels for 13%

profile of v5, /device:TPU:1, one launch (start us, length us, event | category | flops | bytes accessed | tf_op | source)
XLA Modules:
  0.0 76.4 jit_solution(16958435867437296565)
XLA Ops:
  0.6 0.0 copy-start.1
  0.6 2.3 %pack.1 = bf16[16,48,128]{2,1,0:T(8,128)(2,1)} custom-call(s32[1]{0:T(128)} %bitcast.1.refs_0_.refs_1_, s32[4,256]{1,0:T(4,128)} %bitcast.26, s32[4,256]{1,0:T(4,128)} %bitcast.28, s32[8,256]{1,0:T(8,128)} %bitcast.22, s32[8,256]{1,0:T(8,128)} %bitcast.24, bf16[16,8,8,128]{3,2,1,0:T(8,128)(2,1)} %bitcast.17), custom_call_target="tpu_custom_call" | custom-call | tf_op jit(solution)/shard_map/pack/pallas_call | solution.py:540
  2.9 0.0 copy-start.10
  2.9 0.0 copy-start
  2.9 0.0 copy-start.6
  3.0 0.0 copy-start.7
  3.0 0.0 copy-start.8
  3.0 0.0 copy-start.9
  3.0 7.4 %all-to-all-start = ((bf16[16,48,128]{2,1,0:T(8,128)(2,1)}), bf16[16,48,128]{2,1,0:T(8,128)(2,1)S(1)}, u32[]{:S(2)}, u32[]{:S(2)}) async-start(bf16[16,48,128]{2,1,0:T(8,128)(2,1)} %pack.1), calls=%async_computation | async-start | bytes 393216 | tf_op jit(solution)/shard_map/all_to_all | solution.py:568
  10.4 0.0 copy-start.3
  10.4 0.0 copy-done.10
  10.5 0.0 copy-done.1
  10.5 0.0 copy-done
  10.5 0.0 copy-done.6
  10.5 0.0 copy-done.7
  10.5 0.0 copy-done.8
  10.5 0.0 copy-done.9
  10.5 0.8 %copy-done.3 = bf16[512,128]{1,0:T(8,128)(2,1)S(1)} copy-done((bf16[512,128]{1,0:T(8,128)(2,1)S(1)}, bf16[512,128]{1,0:T(8,128)(2,1)}, u32[]{:S(2)}) %copy-start.3) | copy-done | bytes 131096
  11.3 0.0 copy-start.2
  11.3 1.4 %aside.1 = (s32[24,768]{1,0:T(8,128)S(1)}, f32[1024,128]{1,0:T(8,128)S(1)}, bf16[1152,128]{1,0:T(8,128)(2,1)S(1)}, bf16[1152,128]{1,0:T(8,128)(2,1)S(1)}) custom-call(s32[1]{0:T(128)} %bitcast.1.refs_0_.refs_1_, s32[4,256]{1,0:T(4,128)S(1)} %bitcast.27, s32[4,256]{1,0:T(4,128)S(1)} %bitcast.29, s32[8,256]{1,0:T(8,128)S(1)} %bitcast.23, ...), custom_call_target="tpu_custom_call" | custom-call | tf_op jit(solution)/shard_map/aside/pallas_call | solution.py:540
  12.8 3.9 %all-to-all-done.refs_0_ = bf16[16,48,128]{2,1,0:T(8,128)(2,1)S(1)} async-done(((bf16[16,48,128]{2,1,0:T(8,128)(2,1)}), bf16[16,48,128]{2,1,0:T(8,128)(2,1)S(1)}, u32[]{:S(2)}, u32[]{:S(2)}) %all-to-all-start) | async-done | bytes 196640 | tf_op jit(solution)/shard_map/all_to_all | solution.py:568
  16.6 0.0 copy-done.2
  16.6 1.9 %first.1 = (bf16[16,48,128]{2,1,0:T(8,128)(2,1)S(1)}, bf16[1024,128]{1,0:T(8,128)(2,1)S(1)}, bf16[1600,128]{1,0:T(8,128)(2,1)S(1)}) custom-call(bf16[16,48,128]{2,1,0:T(8,128)(2,1)S(1)} %all-to-all-done.refs_0_, s32[24,768]{1,0:T(8,128)S(1)} %get-tuple-element.34.refs_1_.refs_3_.refs_2_, bf16[16,8,8,128]{3,2,1,0:T(8,128)(2,1)S(1)} %bitcast.18, ...), custom_call_target="tpu_custom_call" | custom-call | tf_op jit(solution)/shard_map/first/pallas_call | solution.py:540
  18.6 0.0 copy-start.4
  18.6 10.0 %all_to_all.25.refs_0_ = bf16[16,48,128]{2,1,0:T(8,128)(2,1)S(1)} all-to-all(bf16[16,48,128]{2,1,0:T(8,128)(2,1)S(1)} %get-tuple-element.35), channel_id=1, replica_groups={{9,7,8,12,5,4,0,13,10,15,6,2,11,3,1,14},{25,23,24,28,21,20,16,29,26,31,..., dimensions={0} | all-to-all | bytes 393216 | tf_op jit(solution)/shard_map/all_to_all | solution.py:568
  28.5 2.9 %second.1 = (bf16[16,48,128]{2,1,0:T(8,128)(2,1)}, bf16[1024,128]{1,0:T(8,128)(2,1)S(1)}, bf16[1024,128]{1,0:T(8,128)(2,1)S(1)}, bf16[1600,128]{1,0:T(8,128)(2,1)S(1)}) custom-call(bf16[16,48,128]{2,1,0:T(8,128)(2,1)S(1)} %all_to_all.25.refs_0_, s32[24,768]{1,0:T(8,128)S(1)} %get-tuple-element.34.refs_1_.refs_3_.refs_2_, ...), custom_call_target="tpu_custom_call" | custom-call | tf_op jit(solution)/shard_map/second/pallas_call | solution.py:540
  31.4 0.0 copy-done.4
  31.4 4.2 %all-to-all-start.2 = ((bf16[16,48,128]{2,1,0:T(8,128)(2,1)}), bf16[16,48,128]{2,1,0:T(8,128)(2,1)S(1)}, u32[]{:S(2)}, u32[]{:S(2)}) async-start(bf16[16,48,128]{2,1,0:T(8,128)(2,1)} %get-tuple-element.39), calls=%async_computation.2 | async-start | bytes 393216 | tf_op jit(solution)/shard_map/all_to_all | solution.py:568
  35.6 0.0 copy-start.5
  35.6 1.8 %early.1 = (bf16[256,128]{1,0:T(8,128)(2,1)S(1)}, f32[416,128]{1,0:T(8,128)S(1)}, bf16[416,128]{1,0:T(8,128)(2,1)}, bf16[416,128]{1,0:T(8,128)(2,1)}, bf16[416,128]{1,0:T(8,128)(2,1)}) custom-call(s32[1]{0:T(128)} %bitcast.refs_0_, s32[1]{0:T(128)} %bitcast.1.refs_0_.refs_1_, bf16[1024,128]{1,0:T(8,128)(2,1)S(1)} %get-tuple-element.40.refs_0_.refs_2_, ...), custom_call_target="tpu_custom_call" | custom-call | tf_op jit(solution)/shard_map/early/pallas_call | solution.py:540
  37.4 0.4 collective-permute-start
  37.8 1.2 %collective-permute-start.1 = (bf16[416,128]{1,0:T(8,128)(2,1)}, bf16[416,128]{1,0:T(8,128)(2,1)}, u32[]{:S(2)}, u32[]{:S(2)}) collective-permute-start(bf16[416,128]{1,0:T(8,128)(2,1)} %get-tuple-element.53), channel_id=1, source_target_pairs={{0,16},{1,17},{2,18},{3,19},{4,20},{5,21},{6,22},{7,23},{8,24},{9,... | collective-permute-start | bytes 319496 | tf_op jit(solution)/shard_map/ppermute | solution.py:579
  39.0 0.6 collective-permute-start.2
  39.6 0.0 copy-done.5
  39.6 1.0 %again.1 = (f32[1024,128]{1,0:T(8,128)S(1)}, bf16[1280,384]{1,0:T(8,128)(2,1)S(1)}) custom-call(bf16[1600,128]{1,0:T(8,128)(2,1)S(1)} %copy-done.5, bf16[1152,128]{1,0:T(8,128)(2,1)S(1)} %copy-done), custom_call_target="tpu_custom_call" | custom-call | tf_op jit(solution)/shard_map/again/pallas_call | solution.py:540
  40.6 0.8 %inner.2.refs_4_ = f32[1024,128]{1,0:T(8,128)S(1)} custom-call(bf16[1024,128]{1,0:T(8,128)(2,1)S(1)} %get-tuple-element.40.refs_0_.refs_2_, bf16[1152,128]{1,0:T(8,128)(2,1)S(1)} %get-tuple-element.37.refs_4_.refs_1_), custom_call_target="tpu_custom_call" | custom-call | tf_op jit(solution)/shard_map/inner/pallas_call | solution.py:540
  41.4 0.4 all-to-all-done.2.refs_2_
  41.8 1.2 %slope.1 = (bf16[1024,128]{1,0:T(8,128)(2,1)S(1)}, f32[288,128]{1,0:T(8,128)S(1)}, bf16[288,128]{1,0:T(8,128)(2,1)S(1)}, bf16[288,128]{1,0:T(8,128)(2,1)S(1)}, bf16[288,128]{1,0:T(8,128)(2,1)S(1)}) custom-call(s32[1]{0:T(128)} %bitcast.refs_0_, s32[1]{0:T(128)} %bitcast.1.refs_0_.refs_1_, bf16[16,48,128]{2,1,0:T(8,128)(2,1)S(1)} %all-to-all-done.2.refs_2_, ...), custom_call_target="tpu_custom_call" | custom-call | tf_op jit(solution)/shard_map/slope/pallas_call | solution.py:540
  43.0 0.1 collective-permute-start.3
  43.2 1.2 %collective-permute-start.4 = (bf16[288,128]{1,0:T(8,128)(2,1)S(1)}, bf16[288,128]{1,0:T(8,128)(2,1)S(1)}, u32[]{:S(2)}, u32[]{:S(2)}) collective-permute-start(bf16[288,128]{1,0:T(8,128)(2,1)S(1)} %get-tuple-element.57), channel_id=1, source_target_pairs={{0,16},{1,17},{2,18},{3,19},{4,20},{5,21},{6,22},{7,23},{8,24},{9,... | collective-permute-start | bytes 221192 | tf_op jit(solution)/shard_map/ppermute | solution.py:579
  44.4 0.0 collective-permute-done.refs_1_
  44.4 0.8 %collective-permute-start.5 = (bf16[288,128]{1,0:T(8,128)(2,1)S(1)}, bf16[288,128]{1,0:T(8,128)(2,1)S(1)}, u32[]{:S(2)}, u32[]{:S(2)}) collective-permute-start(bf16[288,128]{1,0:T(8,128)(2,1)S(1)} %get-tuple-element.58), channel_id=1, source_target_pairs={{0,17},{1,16},{2,19},{3,18},{4,21},{5,20},{6,23},{7,22},{8,25},{9,... | collective-permute-start | bytes 221192 | tf_op jit(solution)/shard_map/ppermute | solution.py:579
  45.2 0.7 copy.17
  45.9 0.0 collective-permute-done.1.refs_2_
  45.9 0.0 collective-permute-done.2.refs_3_
  45.9 1.1 %gain.1.refs_1_ = f32[416,128]{1,0:T(8,128)S(1)} custom-call(f32[416,128]{1,0:T(8,128)S(1)} %get-tuple-element.51.refs_0_, bf16[416,128]{1,0:T(8,128)(2,1)} %collective-permute-done.refs_1_, bf16[416,128]{1,0:T(8,128)(2,1)} %collective-permute-done.1.refs_2_, bf16[416,128]{1,0:T(8,128)(2,1)} %collective-permute-done.2.refs_3_), custom_call_target="tpu_custom_call" | custom-call | tf_op jit(solution)/shard_map/gain/pallas_call | solution.py:540
  47.0 0.6 last.1.refs_0_
  47.6 0.8 %inner.3.refs_2_ = f32[1024,128]{1,0:T(8,128)S(1)} custom-call(bf16[1024,128]{1,0:T(8,128)(2,1)S(1)} %get-tuple-element.44.refs_0_, bf16[1152,128]{1,0:T(8,128)(2,1)S(1)} %get-tuple-element.45.refs_1_), custom_call_target="tpu_custom_call" | custom-call | tf_op jit(solution)/shard_map/inner/pallas_call | solution.py:540
  48.4 0.0 collective-permute-done.3.refs_3_
  48.5 0.0 collective-permute-done.4.refs_4_
  48.5 0.8 collective-permute-done.5.refs_5_
  49.2 0.1 join.1
  49.3 14.6 %all_to_all.26.refs_0_ = bf16[16,96,128]{2,1,0:T(8,128)(2,1)S(1)} all-to-all(bf16[16,96,128]{2,1,0:T(8,128)(2,1)S(1)} %join.1), channel_id=1, replica_groups={{9,7,8,12,5,4,0,13,10,15,6,2,11,3,1,14},{25,23,24,28,21,20,16,29,26,31,..., dimensions={0} | all-to-all | bytes 786432 | tf_op jit(solution)/shard_map/all_to_all | solution.py:568
  63.9 0.1 sum.1
  63.9 7.9 %all_to_all.27.refs_1_ = bf16[8,96,128]{2,1,0:T(8,128)(2,1)S(1)} all-to-all(bf16[8,96,128]{2,1,0:T(8,128)(2,1)S(1)} %sum.1), channel_id=1, replica_groups={{10,4,0,12,2,14,6,8},{11,5,1,13,3,15,7,9},{26,20,16,28,18,30,22,24},{27..., dimensions={0} | all-to-all | bytes 393216 | tf_op jit(solution)/shard_map/all_to_all | solution.py:568
  71.9 2.2 %collective-permute-start.6 = (bf16[8,96,128]{2,1,0:T(8,128)(2,1)S(1)}, bf16[8,96,128]{2,1,0:T(8,128)(2,1)S(1)}, u32[]{:S(2)}, u32[]{:S(2)}) collective-permute-start(bf16[8,96,128]{2,1,0:T(8,128)(2,1)S(1)} %all_to_all.27.refs_1_), channel_id=1, source_target_pairs={{0,1},{1,0},{2,3},{3,2},{4,5},{5,4},{6,7},{7,6},{8,9},{9,8},{10,11... | collective-permute-start | bytes 589832 | tf_op jit(solution)/shard_map/ppermute | solution.py:667
  74.1 1.4 %input.1 = f32[16,8,8,128]{3,2,1,0:T(8,128)} custom-call(bf16[16,96,128]{2,1,0:T(8,128)(2,1)S(1)} %all_to_all.26.refs_0_, s32[24,768]{1,0:T(8,128)S(1)} %get-tuple-element.34.refs_1_.refs_3_.refs_2_, f32[1024,128]{1,0:T(8,128)S(1)} %inner.3.refs_2_), custom_call_target="tpu_custom_call" | custom-call | tf_op jit(solution)/shard_map/input/pallas_call | solution.py:540
  75.5 0.0 collective-permute-done.6.refs_2_
  75.5 0.9 %spread.1 = (f32[576,128]{1,0:T(8,128)}, f32[576,128]{1,0:T(8,128)}, f32[256,128]{1,0:T(8,128)}) custom-call(s32[1]{0:T(128)} %bitcast.1.refs_0_.refs_1_, bf16[8,96,128]{2,1,0:T(8,128)(2,1)S(1)} %all_to_all.27.refs_1_, bf16[8,96,128]{2,1,0:T(8,128)(2,1)S(1)} %collective-permute-done.6.refs_2_), custom_call_target="tpu_custom_call" | custom-call | tf_op jit(solution)/shard_map/spread/pallas_call | solution.py:540
  (1 shorter events, 0.0 us)
Async XLA Ops:
  0.6 9.8 %copy-start.1 = (bf16[1152,128]{1,0:T(8,128)(2,1)S(1)}, bf16[1152,128]{1,0:T(8,128)(2,1)}, u32[]{:S(2)}) copy-start(bf16[1152,128]{1,0:T(8,128)(2,1)} %refs_3_.3) | copy-start | bytes 884740
  2.9 7.5 %copy-start.10 = (bf16[1,16,4,4,128]{4,3,2,1,0:T(4,128)(2,1)S(1)}, bf16[1,16,4,4,128]{4,3,2,1,0:T(4,128)(2,1)}, u32[]{:S(2)}) copy-start(bf16[1,16,4,4,128]{4,3,2,1,0:T(4,128)(2,1)} %param.10) | copy-start | bytes 196612
  2.9 7.5 %copy-start = (bf16[1152,128]{1,0:T(8,128)(2,1)S(1)}, bf16[1152,128]{1,0:T(8,128)(2,1)}, u32[]{:S(2)}) copy-start(bf16[1152,128]{1,0:T(8,128)(2,1)} %refs_1_.1) | copy-start | bytes 884740
  2.9 7.5 %copy-start.6 = (s32[256,8]{0,1:T(8,128)S(1)}, s32[256,8]{0,1:T(8,128)}, u32[]{:S(2)}) copy-start(s32[256,8]{0,1:T(8,128)} %param.16) | copy-start | bytes 24580
  3.0 7.5 %copy-start.7 = (s32[256,8]{0,1:T(8,128)S(1)}, s32[256,8]{0,1:T(8,128)}, u32[]{:S(2)}) copy-start(s32[256,8]{0,1:T(8,128)} %param.17) | copy-start | bytes 24580
  3.0 7.5 %copy-start.8 = (s32[256,4]{0,1:T(4,128)S(1)}, s32[256,4]{0,1:T(4,128)}, u32[]{:S(2)}) copy-start(s32[256,4]{0,1:T(4,128)} %param.14) | copy-start | bytes 12292
  3.0 7.5 %copy-start.9 = (s32[256,4]{0,1:T(4,128)S(1)}, s32[256,4]{0,1:T(4,128)}, u32[]{:S(2)}) copy-start(s32[256,4]{0,1:T(4,128)} %param.15) | copy-start | bytes 12292
  3.0 13.7 %all-to-all-start = ((bf16[16,48,128]{2,1,0:T(8,128)(2,1)}), bf16[16,48,128]{2,1,0:T(8,128)(2,1)S(1)}, u32[]{:S(2)}, u32[]{:S(2)}) async-start(bf16[16,48,128]{2,1,0:T(8,128)(2,1)} %pack.1), calls=%async_computation | async-start | bytes 393216 | tf_op jit(solution)/shard_map/all_to_all | solution.py:568
  10.4 0.9 %copy-start.3 = (bf16[512,128]{1,0:T(8,128)(2,1)S(1)}, bf16[512,128]{1,0:T(8,128)(2,1)}, u32[]{:S(2)}) copy-start(bf16[512,128]{1,0:T(8,128)(2,1)} %refs_5_.1) | copy-start | bytes 393220
  11.3 5.3 %copy-start.2 = (bf16[1,16,8,8,128]{4,3,2,1,0:T(8,128)(2,1)S(1)}, bf16[1,16,8,8,128]{4,3,2,1,0:T(8,128)(2,1)}, u32[]{:S(2)}) copy-start(bf16[1,16,8,8,128]{4,3,2,1,0:T(8,128)(2,1)} %param.9) | copy-start | bytes 786436
  18.6 12.9 %copy-start.4 = (bf16[1600,128]{1,0:T(8,128)(2,1)}, bf16[1600,128]{1,0:T(8,128)(2,1)S(1)}, u32[]{:S(2)}) copy-start(bf16[1600,128]{1,0:T(8,128)(2,1)S(1)} %get-tuple-element.41.refs_0_) | copy-start | bytes 1228804
  31.4 10.4 %all-to-all-start.2 = ((bf16[16,48,128]{2,1,0:T(8,128)(2,1)}), bf16[16,48,128]{2,1,0:T(8,128)(2,1)S(1)}, u32[]{:S(2)}, u32[]{:S(2)}) async-start(bf16[16,48,128]{2,1,0:T(8,128)(2,1)} %get-tuple-element.39), calls=%async_computation.2 | async-start | bytes 393216 | tf_op jit(solution)/shard_map/all_to_all | solution.py:568
  35.6 4.0 %copy-start.5 = (bf16[1600,128]{1,0:T(8,128)(2,1)S(1)}, bf16[1600,128]{1,0:T(8,128)(2,1)}, u32[]{:S(2)}) copy-start(bf16[1600,128]{1,0:T(8,128)(2,1)} %copy-done.4) | copy-start | bytes 1228804
  37.4 7.0 %collective-permute-start = (bf16[416,128]{1,0:T(8,128)(2,1)}, bf16[416,128]{1,0:T(8,128)(2,1)}, u32[]{:S(2)}, u32[]{:S(2)}) collective-permute-start(bf16[416,128]{1,0:T(8,128)(2,1)} %get-tuple-element.52), channel_id=1, source_target_pairs={{0,1},{1,0},{2,3},{3,2},{4,5},{5,4},{6,7},{7,6},{8,9},{9,8},{10,11... | collective-permute-start | bytes 319496 | tf_op jit(solution)/shard_map/ppermute | solution.py:579
  37.8 8.1 %collective-permute-start.1 = (bf16[416,128]{1,0:T(8,128)(2,1)}, bf16[416,128]{1,0:T(8,128)(2,1)}, u32[]{:S(2)}, u32[]{:S(2)}) collective-permute-start(bf16[416,128]{1,0:T(8,128)(2,1)} %get-tuple-element.53), channel_id=1, source_target_pairs={{0,16},{1,17},{2,18},{3,19},{4,20},{5,21},{6,22},{7,23},{8,24},{9,... | collective-permute-start | bytes 319496 | tf_op jit(solution)/shard_map/ppermute | solution.py:579
  39.0 6.9 %collective-permute-start.2 = (bf16[416,128]{1,0:T(8,128)(2,1)}, bf16[416,128]{1,0:T(8,128)(2,1)}, u32[]{:S(2)}, u32[]{:S(2)}) collective-permute-start(bf16[416,128]{1,0:T(8,128)(2,1)} %get-tuple-element.54), channel_id=1, source_target_pairs={{0,17},{1,16},{2,19},{3,18},{4,21},{5,20},{6,23},{7,22},{8,25},{9,... | collective-permute-start | bytes 319496 | tf_op jit(solution)/shard_map/ppermute | solution.py:579
  43.0 5.4 %collective-permute-start.3 = (bf16[288,128]{1,0:T(8,128)(2,1)S(1)}, bf16[288,128]{1,0:T(8,128)(2,1)S(1)}, u32[]{:S(2)}, u32[]{:S(2)}) collective-permute-start(bf16[288,128]{1,0:T(8,128)(2,1)S(1)} %get-tuple-element.56), channel_id=1, source_target_pairs={{0,1},{1,0},{2,3},{3,2},{4,5},{5,4},{6,7},{7,6},{8,9},{9,8},{10,11... | collective-permute-start | bytes 221192 | tf_op jit(solution)/shard_map/ppermute | solution.py:579
  43.2 5.3 %collective-permute-start.4 = (bf16[288,128]{1,0:T(8,128)(2,1)S(1)}, bf16[288,128]{1,0:T(8,128)(2,1)S(1)}, u32[]{:S(2)}, u32[]{:S(2)}) collective-permute-start(bf16[288,128]{1,0:T(8,128)(2,1)S(1)} %get-tuple-element.57), channel_id=1, source_target_pairs={{0,16},{1,17},{2,18},{3,19},{4,20},{5,21},{6,22},{7,23},{8,24},{9,... | collective-permute-start | bytes 221192 | tf_op jit(solution)/shard_map/ppermute | solution.py:579
  44.4 4.8 %collective-permute-start.5 = (bf16[288,128]{1,0:T(8,128)(2,1)S(1)}, bf16[288,128]{1,0:T(8,128)(2,1)S(1)}, u32[]{:S(2)}, u32[]{:S(2)}) collective-permute-start(bf16[288,128]{1,0:T(8,128)(2,1)S(1)} %get-tuple-element.58), channel_id=1, source_target_pairs={{0,17},{1,16},{2,19},{3,18},{4,21},{5,20},{6,23},{7,22},{8,25},{9,... | collective-permute-start | bytes 221192 | tf_op jit(solution)/shard_map/ppermute | solution.py:579
  71.9 3.6 %collective-permute-start.6 = (bf16[8,96,128]{2,1,0:T(8,128)(2,1)S(1)}, bf16[8,96,128]{2,1,0:T(8,128)(2,1)S(1)}, u32[]{:S(2)}, u32[]{:S(2)}) collective-permute-start(bf16[8,96,128]{2,1,0:T(8,128)(2,1)S(1)} %all_to_all.27.refs_1_), channel_id=1, source_target_pairs={{0,1},{1,0},{2,3},{3,2},{4,5},{5,4},{6,7},{7,6},{8,9},{9,8},{10,11... | collective-permute-start | bytes 589832 | tf_op jit(solution)/shard_map/ppermute | solution.py:667

commit v6 on v5

--- a/solution.py
+++ b/solution.py
@@ -30,6 +30,7 @@
         self.column = (side + 2) * tiles
         self.cells = 2 * self.line + 2 * self.column
         self.cells_up = -(-self.cells // (2 * LANES)) * 2 * LANES
+        self.cells_read = -(-self.cells // LANES) * LANES
         self.tap_rows = 9 * chan // samples
         self.down_rows = 4 * chan // samples
         self.late = self.tap_rows // 2
@@ -260,7 +261,7 @@
 
 def first_kernel(z, got_ref, index_ref, x_ref, w_ref, send_ref, hidden_ref, strip_ref, columns_ref, west_ref, east_ref):
     center = row_first(x_ref[...]).reshape(z.pixels, z.chan)
-    strip = padded_columns(z, center, got_ref[...].reshape(z.sent, z.chan), as_column(index_ref[8:9, : z.cells_up]), west_ref, east_ref, columns_ref)
+    strip = padded_columns(z, center, got_ref[...].reshape(z.sent, z.chan), as_column(index_ref[8:9, : z.cells_read]), west_ref, east_ref, columns_ref)
     strip_ref[...] = strip.astype(BF16)
     v = conv(z, columns_ref, w_ref)
     hidden = (v / (1.0 + jnp.exp(-v))).astype(BF16)
@@ -328,7 +329,7 @@
     send_ref, slope_ref, out_ref, strip_ref, columns_ref, west_ref, east_ref, scratch_ref,
 ):
     center = hidden_ref[...].astype(F32)
-    strip = padded_columns(z, center, got_ref[...].reshape(z.sent, z.chan), as_column(index_ref[8:9, : z.cells_up]), west_ref, east_ref, columns_ref)
+    strip = padded_columns(z, center, got_ref[...].reshape(z.sent, z.chan), as_column(index_ref[8:9, : z.cells_read]), west_ref, east_ref, columns_ref)
     strip_ref[...] = strip.astype(BF16)
     v = conv(z, columns_ref, w_ref)
     s = 1.0 / (1.0 + jnp.exp(-v))

time: 76.9 us -> 76.9 us (level)
  no operation moved by 1% of the time
where the time goes in v6:
time: 76.9 us; the launch traced here: 76.4 us
  blocking collectives  32.5 us (42%)
  starting transfers between devices  18.3 us (24%)
  Pallas kernels  18.1 us (24%)
  waiting for transfers between devices  5.09 us (7%)
  local copies, waits for them, and re-layouts  1.53 us (2%)
  between operations  0.93 us (1%)
    all_to_all x3, blocking collectives, exchange(): lax.all_to_all(x, 'tile', split_axis=0, concat_axis=0, tiled=True, axis_i...  32.5 us
    pallas_call x15, Pallas kernels, run(): pl.pallas_call(kernel, out_shape=[pltpu.HBM(out[0], out[1]) if is_far els...  18.1 us
    all_to_all x2, starting transfers between devices, exchange(): lax.all_to_all(x, 'tile', split_axis=0, concat_axis=0, tiled=True, axis_i...  11.6 us
    ppermute x6, starting transfers between devices, deal(): got.append(lax.ppermute(others[k], ('dp', 'tile'), pairs))  4.41 us
    all_to_all x2, waiting for transfers between devices, exchange(): lax.all_to_all(x, 'tile', split_axis=0, concat_axis=0, tiled=True, axis_i...  4.31 us
    ppermute x1, starting transfers between devices, local(): other = lax.ppermute(mine, 'tile', [(t, t ^ 1) for t in range(z.devices)])  2.24 us
  transfers between devices with their start and end apart: 9, of which 3 were waited for; matrix products, arithmetic and copies ran while one was open for 1% of the time, Pallas kernels for 13%

profile of v6, /device:TPU:1, one launch (start us, length us, event | category | flops | bytes accessed | tf_op | source)
XLA Modules:
  0.0 76.4 jit_solution(10703197679897282127)
XLA Ops:
  0.6 0.0 copy-start.1
  0.6 2.3 %pack.1 = bf16[16,48,128]{2,1,0:T(8,128)(2,1)} custom-call(s32[1]{0:T(128)} %bitcast.1.refs_0_.refs_1_, s32[4,256]{1,0:T(4,128)} %bitcast.26, s32[4,256]{1,0:T(4,128)} %bitcast.28, s32[8,256]{1,0:T(8,128)} %bitcast.22, s32[8,256]{1,0:T(8,128)} %bitcast.24, bf16[16,8,8,128]{3,2,1,0:T(8,128)(2,1)} %bitcast.17), custom_call_target="tpu_custom_call" | custom-call | tf_op jit(solution)/shard_map/pack/pallas_call | solution.py:541
  2.9 0.0 copy-start.10
  2.9 0.0 copy-start
  2.9 0.0 copy-start.6
  3.0 0.0 copy-start.7
  3.0 0.0 copy-start.8
  3.0 0.0 copy-start.9
  3.0 7.4 %all-to-all-start = ((bf16[16,48,128]{2,1,0:T(8,128)(2,1)}), bf16[16,48,128]{2,1,0:T(8,128)(2,1)S(1)}, u32[]{:S(2)}, u32[]{:S(2)}) async-start(bf16[16,48,128]{2,1,0:T(8,128)(2,1)} %pack.1), calls=%async_computation | async-start | bytes 393216 | tf_op jit(solution)/shard_map/all_to_all | solution.py:569
  10.4 0.0 copy-start.3
  10.4 0.0 copy-done.10
  10.5 0.0 copy-done.1
  10.5 0.0 copy-done
  10.5 0.0 copy-done.6
  10.5 0.0 copy-done.7
  10.5 0.0 copy-done.8
  10.5 0.0 copy-done.9
  10.5 0.8 %copy-done.3 = bf16[512,128]{1,0:T(8,128)(2,1)S(1)} copy-done((bf16[512,128]{1,0:T(8,128)(2,1)S(1)}, bf16[512,128]{1,0:T(8,128)(2,1)}, u32[]{:S(2)}) %copy-start.3) | copy-done | bytes 131096
  11.3 0.0 copy-start.2
  11.3 1.4 %aside.1 = (s32[24,768]{1,0:T(8,128)S(1)}, f32[1024,128]{1,0:T(8,128)S(1)}, bf16[1152,128]{1,0:T(8,128)(2,1)S(1)}, bf16[1152,128]{1,0:T(8,128)(2,1)S(1)}) custom-call(s32[1]{0:T(128)} %bitcast.1.refs_0_.refs_1_, s32[4,256]{1,0:T(4,128)S(1)} %bitcast.27, s32[4,256]{1,0:T(4,128)S(1)} %bitcast.29, s32[8,256]{1,0:T(8,128)S(1)} %bitcast.23, ...), custom_call_target="tpu_custom_call" | custom-call | tf_op jit(solution)/shard_map/aside/pallas_call | solution.py:541
  12.8 3.9 %all-to-all-done.refs_0_ = bf16[16,48,128]{2,1,0:T(8,128)(2,1)S(1)} async-done(((bf16[16,48,128]{2,1,0:T(8,128)(2,1)}), bf16[16,48,128]{2,1,0:T(8,128)(2,1)S(1)}, u32[]{:S(2)}, u32[]{:S(2)}) %all-to-all-start) | async-done | bytes 196640 | tf_op jit(solution)/shard_map/all_to_all | solution.py:569
  16.6 0.0 copy-done.2
  16.6 1.9 %first.1 = (bf16[16,48,128]{2,1,0:T(8,128)(2,1)S(1)}, bf16[1024,128]{1,0:T(8,128)(2,1)S(1)}, bf16[1600,128]{1,0:T(8,128)(2,1)S(1)}) custom-call(bf16[16,48,128]{2,1,0:T(8,128)(2,1)S(1)} %all-to-all-done.refs_0_, s32[24,768]{1,0:T(8,128)S(1)} %get-tuple-element.34.refs_1_.refs_3_.refs_2_, bf16[16,8,8,128]{3,2,1,0:T(8,128)(2,1)S(1)} %bitcast.18, ...), custom_call_target="tpu_custom_call" | custom-call | tf_op jit(solution)/shard_map/first/pallas_call | solution.py:541
  18.5 0.0 copy-start.4
  18.5 10.0 %all_to_all.25.refs_0_ = bf16[16,48,128]{2,1,0:T(8,128)(2,1)S(1)} all-to-all(bf16[16,48,128]{2,1,0:T(8,128)(2,1)S(1)} %get-tuple-element.35), channel_id=1, replica_groups={{9,7,8,12,5,4,0,13,10,15,6,2,11,3,1,14},{25,23,24,28,21,20,16,29,26,31,..., dimensions={0} | all-to-all | bytes 393216 | tf_op jit(solution)/shard_map/all_to_all | solution.py:569
  28.5 2.8 %second.1 = (bf16[16,48,128]{2,1,0:T(8,128)(2,1)}, bf16[1024,128]{1,0:T(8,128)(2,1)S(1)}, bf16[1024,128]{1,0:T(8,128)(2,1)S(1)}, bf16[1600,128]{1,0:T(8,128)(2,1)S(1)}) custom-call(bf16[16,48,128]{2,1,0:T(8,128)(2,1)S(1)} %all_to_all.25.refs_0_, s32[24,768]{1,0:T(8,128)S(1)} %get-tuple-element.34.refs_1_.refs_3_.refs_2_, ...), custom_call_target="tpu_custom_call" | custom-call | tf_op jit(solution)/shard_map/second/pallas_call | solution.py:541
  31.4 0.0 copy-done.4
  31.4 4.2 %all-to-all-start.2 = ((bf16[16,48,128]{2,1,0:T(8,128)(2,1)}), bf16[16,48,128]{2,1,0:T(8,128)(2,1)S(1)}, u32[]{:S(2)}, u32[]{:S(2)}) async-start(bf16[16,48,128]{2,1,0:T(8,128)(2,1)} %get-tuple-element.39), calls=%async_computation.2 | async-start | bytes 393216 | tf_op jit(solution)/shard_map/all_to_all | solution.py:569
  35.6 0.0 copy-start.5
  35.6 1.8 %early.1 = (bf16[256,128]{1,0:T(8,128)(2,1)S(1)}, f32[416,128]{1,0:T(8,128)S(1)}, bf16[416,128]{1,0:T(8,128)(2,1)}, bf16[416,128]{1,0:T(8,128)(2,1)}, bf16[416,128]{1,0:T(8,128)(2,1)}) custom-call(s32[1]{0:T(128)} %bitcast.refs_0_, s32[1]{0:T(128)} %bitcast.1.refs_0_.refs_1_, bf16[1024,128]{1,0:T(8,128)(2,1)S(1)} %get-tuple-element.40.refs_0_.refs_2_, ...), custom_call_target="tpu_custom_call" | custom-call | tf_op jit(solution)/shard_map/early/pallas_call | solution.py:541
  37.3 0.4 collective-permute-start
  37.7 1.2 %collective-permute-start.1 = (bf16[416,128]{1,0:T(8,128)(2,1)}, bf16[416,128]{1,0:T(8,128)(2,1)}, u32[]{:S(2)}, u32[]{:S(2)}) collective-permute-start(bf16[416,128]{1,0:T(8,128)(2,1)} %get-tuple-element.53), channel_id=1, source_target_pairs={{0,16},{1,17},{2,18},{3,19},{4,20},{5,21},{6,22},{7,23},{8,24},{9,... | collective-permute-start | bytes 319496 | tf_op jit(solution)/shard_map/ppermute | solution.py:580
  38.9 0.6 collective-permute-start.2
  39.5 0.0 copy-done.5
  39.5 1.0 %again.1 = (f32[1024,128]{1,0:T(8,128)S(1)}, bf16[1280,384]{1,0:T(8,128)(2,1)S(1)}) custom-call(bf16[1600,128]{1,0:T(8,128)(2,1)S(1)} %copy-done.5, bf16[1152,128]{1,0:T(8,128)(2,1)S(1)} %copy-done), custom_call_target="tpu_custom_call" | custom-call | tf_op jit(solution)/shard_map/again/pallas_call | solution.py:541
  40.5 0.8 %inner.2.refs_4_ = f32[1024,128]{1,0:T(8,128)S(1)} custom-call(bf16[1024,128]{1,0:T(8,128)(2,1)S(1)} %get-tuple-element.40.refs_0_.refs_2_, bf16[1152,128]{1,0:T(8,128)(2,1)S(1)} %get-tuple-element.37.refs_4_.refs_1_), custom_call_target="tpu_custom_call" | custom-call | tf_op jit(solution)/shard_map/inner/pallas_call | solution.py:541
  41.4 0.4 all-to-all-done.2.refs_2_
  41.8 1.2 %slope.1 = (bf16[1024,128]{1,0:T(8,128)(2,1)S(1)}, f32[288,128]{1,0:T(8,128)S(1)}, bf16[288,128]{1,0:T(8,128)(2,1)S(1)}, bf16[288,128]{1,0:T(8,128)(2,1)S(1)}, bf16[288,128]{1,0:T(8,128)(2,1)S(1)}) custom-call(s32[1]{0:T(128)} %bitcast.refs_0_, s32[1]{0:T(128)} %bitcast.1.refs_0_.refs_1_, bf16[16,48,128]{2,1,0:T(8,128)(2,1)S(1)} %all-to-all-done.2.refs_2_, ...), custom_call_target="tpu_custom_call" | custom-call | tf_op jit(solution)/shard_map/slope/pallas_call | solution.py:541
  43.0 0.1 collective-permute-start.3
  43.1 1.2 %collective-permute-start.4 = (bf16[288,128]{1,0:T(8,128)(2,1)S(1)}, bf16[288,128]{1,0:T(8,128)(2,1)S(1)}, u32[]{:S(2)}, u32[]{:S(2)}) collective-permute-start(bf16[288,128]{1,0:T(8,128)(2,1)S(1)} %get-tuple-element.57), channel_id=1, source_target_pairs={{0,16},{1,17},{2,18},{3,19},{4,20},{5,21},{6,22},{7,23},{8,24},{9,... | collective-permute-start | bytes 221192 | tf_op jit(solution)/shard_map/ppermute | solution.py:580
  44.3 0.0 collective-permute-done.refs_1_
  44.3 0.9 %collective-permute-start.5 = (bf16[288,128]{1,0:T(8,128)(2,1)S(1)}, bf16[288,128]{1,0:T(8,128)(2,1)S(1)}, u32[]{:S(2)}, u32[]{:S(2)}) collective-permute-start(bf16[288,128]{1,0:T(8,128)(2,1)S(1)} %get-tuple-element.58), channel_id=1, source_target_pairs={{0,17},{1,16},{2,19},{3,18},{4,21},{5,20},{6,23},{7,22},{8,25},{9,... | collective-permute-start | bytes 221192 | tf_op jit(solution)/shard_map/ppermute | solution.py:580
  45.2 0.7 copy.17
  45.8 0.0 collective-permute-done.1.refs_2_
  45.9 0.0 collective-permute-done.2.refs_3_
  45.9 1.1 %gain.1.refs_1_ = f32[416,128]{1,0:T(8,128)S(1)} custom-call(f32[416,128]{1,0:T(8,128)S(1)} %get-tuple-element.51.refs_0_, bf16[416,128]{1,0:T(8,128)(2,1)} %collective-permute-done.refs_1_, bf16[416,128]{1,0:T(8,128)(2,1)} %collective-permute-done.1.refs_2_, bf16[416,128]{1,0:T(8,128)(2,1)} %collective-permute-done.2.refs_3_), custom_call_target="tpu_custom_call" | custom-call | tf_op jit(solution)/shard_map/gain/pallas_call | solution.py:541
  46.9 0.6 last.1.refs_0_
  47.6 0.8 %inner.3.refs_2_ = f32[1024,128]{1,0:T(8,128)S(1)} custom-call(bf16[1024,128]{1,0:T(8,128)(2,1)S(1)} %get-tuple-element.44.refs_0_, bf16[1152,128]{1,0:T(8,128)(2,1)S(1)} %get-tuple-element.45.refs_1_), custom_call_target="tpu_custom_call" | custom-call | tf_op jit(solution)/shard_map/inner/pallas_call | solution.py:541
  48.4 0.0 collective-permute-done.3.refs_3_
  48.4 0.0 collective-permute-done.4.refs_4_
  48.4 0.8 collective-permute-done.5.refs_5_
  49.2 0.1 join.1
  49.3 14.6 %all_to_all.26.refs_0_ = bf16[16,96,128]{2,1,0:T(8,128)(2,1)S(1)} all-to-all(bf16[16,96,128]{2,1,0:T(8,128)(2,1)S(1)} %join.1), channel_id=1, replica_groups={{9,7,8,12,5,4,0,13,10,15,6,2,11,3,1,14},{25,23,24,28,21,20,16,29,26,31,..., dimensions={0} | all-to-all | bytes 786432 | tf_op jit(solution)/shard_map/all_to_all | solution.py:569
  63.8 0.1 sum.1
  63.9 7.9 %all_to_all.27.refs_1_ = bf16[8,96,128]{2,1,0:T(8,128)(2,1)S(1)} all-to-all(bf16[8,96,128]{2,1,0:T(8,128)(2,1)S(1)} %sum.1), channel_id=1, replica_groups={{10,4,0,12,2,14,6,8},{11,5,1,13,3,15,7,9},{26,20,16,28,18,30,22,24},{27..., dimensions={0} | all-to-all | bytes 393216 | tf_op jit(solution)/shard_map/all_to_all | solution.py:569
  71.8 2.2 %collective-permute-start.6 = (bf16[8,96,128]{2,1,0:T(8,128)(2,1)S(1)}, bf16[8,96,128]{2,1,0:T(8,128)(2,1)S(1)}, u32[]{:S(2)}, u32[]{:S(2)}) collective-permute-start(bf16[8,96,128]{2,1,0:T(8,128)(2,1)S(1)} %all_to_all.27.refs_1_), channel_id=1, source_target_pairs={{0,1},{1,0},{2,3},{3,2},{4,5},{5,4},{6,7},{7,6},{8,9},{9,8},{10,11... | collective-permute-start | bytes 589832 | tf_op jit(solution)/shard_map/ppermute | solution.py:668
  74.1 1.4 %input.1 = f32[16,8,8,128]{3,2,1,0:T(8,128)} custom-call(bf16[16,96,128]{2,1,0:T(8,128)(2,1)S(1)} %all_to_all.26.refs_0_, s32[24,768]{1,0:T(8,128)S(1)} %get-tuple-element.34.refs_1_.refs_3_.refs_2_, f32[1024,128]{1,0:T(8,128)S(1)} %inner.3.refs_2_), custom_call_target="tpu_custom_call" | custom-call | tf_op jit(solution)/shard_map/input/pallas_call | solution.py:541
  75.5 0.0 collective-permute-done.6.refs_2_
  75.5 0.9 %spread.1 = (f32[576,128]{1,0:T(8,128)}, f32[576,128]{1,0:T(8,128)}, f32[256,128]{1,0:T(8,128)}) custom-call(s32[1]{0:T(128)} %bitcast.1.refs_0_.refs_1_, bf16[8,96,128]{2,1,0:T(8,128)(2,1)S(1)} %all_to_all.27.refs_1_, bf16[8,96,128]{2,1,0:T(8,128)(2,1)S(1)} %collective-permute-done.6.refs_2_), custom_call_target="tpu_custom_call" | custom-call | tf_op jit(solution)/shard_map/spread/pallas_call | solution.py:541
  (1 shorter events, 0.0 us)
Async XLA Ops:
  0.6 9.8 %copy-start.1 = (bf16[1152,128]{1,0:T(8,128)(2,1)S(1)}, bf16[1152,128]{1,0:T(8,128)(2,1)}, u32[]{:S(2)}) copy-start(bf16[1152,128]{1,0:T(8,128)(2,1)} %refs_3_.3) | copy-start | bytes 884740
  2.9 7.5 %copy-start.10 = (bf16[1,16,4,4,128]{4,3,2,1,0:T(4,128)(2,1)S(1)}, bf16[1,16,4,4,128]{4,3,2,1,0:T(4,128)(2,1)}, u32[]{:S(2)}) copy-start(bf16[1,16,4,4,128]{4,3,2,1,0:T(4,128)(2,1)} %param.10) | copy-start | bytes 196612
  2.9 7.5 %copy-start = (bf16[1152,128]{1,0:T(8,128)(2,1)S(1)}, bf16[1152,128]{1,0:T(8,128)(2,1)}, u32[]{:S(2)}) copy-start(bf16[1152,128]{1,0:T(8,128)(2,1)} %refs_1_.1) | copy-start | bytes 884740
  2.9 7.5 %copy-start.6 = (s32[256,8]{0,1:T(8,128)S(1)}, s32[256,8]{0,1:T(8,128)}, u32[]{:S(2)}) copy-start(s32[256,8]{0,1:T(8,128)} %param.16) | copy-start | bytes 24580
  3.0 7.5 %copy-start.7 = (s32[256,8]{0,1:T(8,128)S(1)}, s32[256,8]{0,1:T(8,128)}, u32[]{:S(2)}) copy-start(s32[256,8]{0,1:T(8,128)} %param.17) | copy-start | bytes 24580
  3.0 7.5 %copy-start.8 = (s32[256,4]{0,1:T(4,128)S(1)}, s32[256,4]{0,1:T(4,128)}, u32[]{:S(2)}) copy-start(s32[256,4]{0,1:T(4,128)} %param.14) | copy-start | bytes 12292
  3.0 7.5 %copy-start.9 = (s32[256,4]{0,1:T(4,128)S(1)}, s32[256,4]{0,1:T(4,128)}, u32[]{:S(2)}) copy-start(s32[256,4]{0,1:T(4,128)} %param.15) | copy-start | bytes 12292
  3.0 13.7 %all-to-all-start = ((bf16[16,48,128]{2,1,0:T(8,128)(2,1)}), bf16[16,48,128]{2,1,0:T(8,128)(2,1)S(1)}, u32[]{:S(2)}, u32[]{:S(2)}) async-start(bf16[16,48,128]{2,1,0:T(8,128)(2,1)} %pack.1), calls=%async_computation | async-start | bytes 393216 | tf_op jit(solution)/shard_map/all_to_all | solution.py:569
  10.4 0.9 %copy-start.3 = (bf16[512,128]{1,0:T(8,128)(2,1)S(1)}, bf16[512,128]{1,0:T(8,128)(2,1)}, u32[]{:S(2)}) copy-start(bf16[512,128]{1,0:T(8,128)(2,1)} %refs_5_.1) | copy-start | bytes 393220
  11.3 5.3 %copy-start.2 = (bf16[1,16,8,8,128]{4,3,2,1,0:T(8,128)(2,1)S(1)}, bf16[1,16,8,8,128]{4,3,2,1,0:T(8,128)(2,1)}, u32[]{:S(2)}) copy-start(bf16[1,16,8,8,128]{4,3,2,1,0:T(8,128)(2,1)} %param.9) | copy-start | bytes 786436
  18.5 12.8 %copy-start.4 = (bf16[1600,128]{1,0:T(8,128)(2,1)}, bf16[1600,128]{1,0:T(8,128)(2,1)S(1)}, u32[]{:S(2)}) copy-start(bf16[1600,128]{1,0:T(8,128)(2,1)S(1)} %get-tuple-element.41.refs_0_) | copy-start | bytes 1228804
  31.4 10.4 %all-to-all-start.2 = ((bf16[16,48,128]{2,1,0:T(8,128)(2,1)}), bf16[16,48,128]{2,1,0:T(8,128)(2,1)S(1)}, u32[]{:S(2)}, u32[]{:S(2)}) async-start(bf16[16,48,128]{2,1,0:T(8,128)(2,1)} %get-tuple-element.39), calls=%async_computation.2 | async-start | bytes 393216 | tf_op jit(solution)/shard_map/all_to_all | solution.py:569
  35.6 4.0 %copy-start.5 = (bf16[1600,128]{1,0:T(8,128)(2,1)S(1)}, bf16[1600,128]{1,0:T(8,128)(2,1)}, u32[]{:S(2)}) copy-start(bf16[1600,128]{1,0:T(8,128)(2,1)} %copy-done.4) | copy-start | bytes 1228804
  37.3 7.0 %collective-permute-start = (bf16[416,128]{1,0:T(8,128)(2,1)}, bf16[416,128]{1,0:T(8,128)(2,1)}, u32[]{:S(2)}, u32[]{:S(2)}) collective-permute-start(bf16[416,128]{1,0:T(8,128)(2,1)} %get-tuple-element.52), channel_id=1, source_target_pairs={{0,1},{1,0},{2,3},{3,2},{4,5},{5,4},{6,7},{7,6},{8,9},{9,8},{10,11... | collective-permute-start | bytes 319496 | tf_op jit(solution)/shard_map/ppermute | solution.py:580
  37.7 8.1 %collective-permute-start.1 = (bf16[416,128]{1,0:T(8,128)(2,1)}, bf16[416,128]{1,0:T(8,128)(2,1)}, u32[]{:S(2)}, u32[]{:S(2)}) collective-permute-start(bf16[416,128]{1,0:T(8,128)(2,1)} %get-tuple-element.53), channel_id=1, source_target_pairs={{0,16},{1,17},{2,18},{3,19},{4,20},{5,21},{6,22},{7,23},{8,24},{9,... | collective-permute-start | bytes 319496 | tf_op jit(solution)/shard_map/ppermute | solution.py:580
  38.9 6.9 %collective-permute-start.2 = (bf16[416,128]{1,0:T(8,128)(2,1)}, bf16[416,128]{1,0:T(8,128)(2,1)}, u32[]{:S(2)}, u32[]{:S(2)}) collective-permute-start(bf16[416,128]{1,0:T(8,128)(2,1)} %get-tuple-element.54), channel_id=1, source_target_pairs={{0,17},{1,16},{2,19},{3,18},{4,21},{5,20},{6,23},{7,22},{8,25},{9,... | collective-permute-start | bytes 319496 | tf_op jit(solution)/shard_map/ppermute | solution.py:580
  43.0 5.4 %collective-permute-start.3 = (bf16[288,128]{1,0:T(8,128)(2,1)S(1)}, bf16[288,128]{1,0:T(8,128)(2,1)S(1)}, u32[]{:S(2)}, u32[]{:S(2)}) collective-permute-start(bf16[288,128]{1,0:T(8,128)(2,1)S(1)} %get-tuple-element.56), channel_id=1, source_target_pairs={{0,1},{1,0},{2,3},{3,2},{4,5},{5,4},{6,7},{7,6},{8,9},{9,8},{10,11... | collective-permute-start | bytes 221192 | tf_op jit(solution)/shard_map/ppermute | solution.py:580
  43.1 5.3 %collective-permute-start.4 = (bf16[288,128]{1,0:T(8,128)(2,1)S(1)}, bf16[288,128]{1,0:T(8,128)(2,1)S(1)}, u32[]{:S(2)}, u32[]{:S(2)}) collective-permute-start(bf16[288,128]{1,0:T(8,128)(2,1)S(1)} %get-tuple-element.57), channel_id=1, source_target_pairs={{0,16},{1,17},{2,18},{3,19},{4,20},{5,21},{6,22},{7,23},{8,24},{9,... | collective-permute-start | bytes 221192 | tf_op jit(solution)/shard_map/ppermute | solution.py:580
  44.3 4.8 %collective-permute-start.5 = (bf16[288,128]{1,0:T(8,128)(2,1)S(1)}, bf16[288,128]{1,0:T(8,128)(2,1)S(1)}, u32[]{:S(2)}, u32[]{:S(2)}) collective-permute-start(bf16[288,128]{1,0:T(8,128)(2,1)S(1)} %get-tuple-element.58), channel_id=1, source_target_pairs={{0,17},{1,16},{2,19},{3,18},{4,21},{5,20},{6,23},{7,22},{8,25},{9,... | collective-permute-start | bytes 221192 | tf_op jit(solution)/shard_map/ppermute | solution.py:580
  71.8 3.6 %collective-permute-start.6 = (bf16[8,96,128]{2,1,0:T(8,128)(2,1)S(1)}, bf16[8,96,128]{2,1,0:T(8,128)(2,1)S(1)}, u32[]{:S(2)}, u32[]{:S(2)}) collective-permute-start(bf16[8,96,128]{2,1,0:T(8,128)(2,1)S(1)} %all_to_all.27.refs_1_), channel_id=1, source_target_pairs={{0,1},{1,0},{2,3},{3,2},{4,5},{5,4},{6,7},{7,6},{8,9},{9,8},{10,11... | collective-permute-start | bytes 589832 | tf_op jit(solution)/shard_map/ppermute | solution.py:668

commit v7 on v6

--- a/solution.py
+++ b/solution.py
@@ -463,9 +463,12 @@
         chunks = [by_core[device % 2][z.ring.index(device // 2)] for device in z.order]
         halves.append(jnp.concatenate(chunks, axis=0))
     one_ref[...] = jnp.concatenate([half[z.early : z.early + z.late] for half in halves], axis=0)
+    push(one_ref)
     early = jnp.concatenate([half[: z.early] for half in halves], axis=0)
     two_ref[...] = early[: z.tap_rows]
+    push(two_ref)
     low_ref[...] = early[z.tap_rows :]
+    push(low_ref)
 
 
 def vmem(*shape, dtype=F32):
@@ -668,7 +671,7 @@
     other = lax.ppermute(mine, "tile", [(t, t ^ 1) for t in range(z.devices)])
     grad_first, grad_second, grad_down = call(
         bind(spread_kernel, z),
-        [array(z.tap_rows, chan), array(z.tap_rows, chan), array(z.down_rows, chan)],
+        [far(z.tap_rows, chan), far(z.tap_rows, chan), far(z.down_rows, chan)],
         scalars=1,
         name="spread",
     )(me, mine, other)

time: 76.9 us -> 76.9 us (level)
  no operation moved by 1% of the time
where the time goes in v7:
time: 76.9 us; the launch traced here: 76.4 us
  blocking collectives  32.5 us (42%)
  starting transfers between devices  18.3 us (24%)
  Pallas kernels  18.1 us (24%)
  waiting for transfers between devices  5.09 us (7%)
  local copies, waits for them, and re-layouts  1.53 us (2%)
  between operations  0.93 us (1%)
    all_to_all x3, blocking collectives, exchange(): lax.all_to_all(x, 'tile', split_axis=0, concat_axis=0, tiled=True, axis_i...  32.5 us
    pallas_call x15, Pallas kernels, run(): pl.pallas_call(kernel, out_shape=[pltpu.HBM(out[0], out[1]) if is_far els...  18.1 us
    all_to_all x2, starting transfers between devices, exchange(): lax.all_to_all(x, 'tile', split_axis=0, concat_axis=0, tiled=True, axis_i...  11.6 us
    ppermute x6, starting transfers between devices, deal(): got.append(lax.ppermute(others[k], ('dp', 'tile'), pairs))  4.41 us
    all_to_all x2, waiting for transfers between devices, exchange(): lax.all_to_all(x, 'tile', split_axis=0, concat_axis=0, tiled=True, axis_i...  4.31 us
    ppermute x1, starting transfers between devices, local(): other = lax.ppermute(mine, 'tile', [(t, t ^ 1) for t in range(z.devices)])  2.24 us
  transfers between devices with their start and end apart: 9, of which 3 were waited for; matrix products, arithmetic and copies ran while one was open for 1% of the time, Pallas kernels for 13%

profile of v7, /device:TPU:1, one launch (start us, length us, event | category | flops | bytes accessed | tf_op | source)
XLA Modules:
  0.0 76.4 jit_solution(2900494963042443265)
XLA Ops:
  0.6 0.0 copy-start.1
  0.6 2.3 %pack.1 = bf16[16,48,128]{2,1,0:T(8,128)(2,1)} custom-call(s32[1]{0:T(128)} %bitcast.1.refs_0_.refs_1_, s32[4,256]{1,0:T(4,128)} %bitcast.26, s32[4,256]{1,0:T(4,128)} %bitcast.28, s32[8,256]{1,0:T(8,128)} %bitcast.22, s32[8,256]{1,0:T(8,128)} %bitcast.24, bf16[16,8,8,128]{3,2,1,0:T(8,128)(2,1)} %bitcast.17), custom_call_target="tpu_custom_call" | custom-call | tf_op jit(solution)/shard_map/pack/pallas_call | solution.py:544
  2.9 0.0 copy-start.10
  2.9 0.0 copy-start
  2.9 0.0 copy-start.6
  3.0 0.0 copy-start.7
  3.0 0.0 copy-start.8
  3.0 0.0 copy-start.9
  3.0 7.4 %all-to-all-start = ((bf16[16,48,128]{2,1,0:T(8,128)(2,1)}), bf16[16,48,128]{2,1,0:T(8,128)(2,1)S(1)}, u32[]{:S(2)}, u32[]{:S(2)}) async-start(bf16[16,48,128]{2,1,0:T(8,128)(2,1)} %pack.1), calls=%async_computation | async-start | bytes 393216 | tf_op jit(solution)/shard_map/all_to_all | solution.py:572
  10.4 0.0 copy-start.3
  10.4 0.0 copy-done.10
  10.5 0.0 copy-done.1
  10.5 0.0 copy-done
  10.5 0.0 copy-done.6
  10.5 0.0 copy-done.7
  10.5 0.0 copy-done.8
  10.5 0.0 copy-done.9
  10.5 0.8 %copy-done.3 = bf16[512,128]{1,0:T(8,128)(2,1)S(1)} copy-done((bf16[512,128]{1,0:T(8,128)(2,1)S(1)}, bf16[512,128]{1,0:T(8,128)(2,1)}, u32[]{:S(2)}) %copy-start.3) | copy-done | bytes 131096
  11.3 0.0 copy-start.2
  11.3 1.4 %aside.1 = (s32[24,768]{1,0:T(8,128)S(1)}, f32[1024,128]{1,0:T(8,128)S(1)}, bf16[1152,128]{1,0:T(8,128)(2,1)S(1)}, bf16[1152,128]{1,0:T(8,128)(2,1)S(1)}) custom-call(s32[1]{0:T(128)} %bitcast.1.refs_0_.refs_1_, s32[4,256]{1,0:T(4,128)S(1)} %bitcast.27, s32[4,256]{1,0:T(4,128)S(1)} %bitcast.29, s32[8,256]{1,0:T(8,128)S(1)} %bitcast.23, ...), custom_call_target="tpu_custom_call" | custom-call | tf_op jit(solution)/shard_map/aside/pallas_call | solution.py:544
  12.8 3.9 %all-to-all-done.refs_0_ = bf16[16,48,128]{2,1,0:T(8,128)(2,1)S(1)} async-done(((bf16[16,48,128]{2,1,0:T(8,128)(2,1)}), bf16[16,48,128]{2,1,0:T(8,128)(2,1)S(1)}, u32[]{:S(2)}, u32[]{:S(2)}) %all-to-all-start) | async-done | bytes 196640 | tf_op jit(solution)/shard_map/all_to_all | solution.py:572
  16.6 0.0 copy-done.2
  16.6 1.9 %first.1 = (bf16[16,48,128]{2,1,0:T(8,128)(2,1)S(1)}, bf16[1024,128]{1,0:T(8,128)(2,1)S(1)}, bf16[1600,128]{1,0:T(8,128)(2,1)S(1)}) custom-call(bf16[16,48,128]{2,1,0:T(8,128)(2,1)S(1)} %all-to-all-done.refs_0_, s32[24,768]{1,0:T(8,128)S(1)} %get-tuple-element.34.refs_1_.refs_3_.refs_2_, bf16[16,8,8,128]{3,2,1,0:T(8,128)(2,1)S(1)} %bitcast.18, ...), custom_call_target="tpu_custom_call" | custom-call | tf_op jit(solution)/shard_map/first/pallas_call | solution.py:544
  18.5 0.0 copy-start.4
  18.5 10.0 %all_to_all.25.refs_0_ = bf16[16,48,128]{2,1,0:T(8,128)(2,1)S(1)} all-to-all(bf16[16,48,128]{2,1,0:T(8,128)(2,1)S(1)} %get-tuple-element.35), channel_id=1, replica_groups={{9,7,8,12,5,4,0,13,10,15,6,2,11,3,1,14},{25,23,24,28,21,20,16,29,26,31,..., dimensions={0} | all-to-all | bytes 393216 | tf_op jit(solution)/shard_map/all_to_all | solution.py:572
  28.5 2.8 %second.1 = (bf16[16,48,128]{2,1,0:T(8,128)(2,1)}, bf16[1024,128]{1,0:T(8,128)(2,1)S(1)}, bf16[1024,128]{1,0:T(8,128)(2,1)S(1)}, bf16[1600,128]{1,0:T(8,128)(2,1)S(1)}) custom-call(bf16[16,48,128]{2,1,0:T(8,128)(2,1)S(1)} %all_to_all.25.refs_0_, s32[24,768]{1,0:T(8,128)S(1)} %get-tuple-element.34.refs_1_.refs_3_.refs_2_, ...), custom_call_target="tpu_custom_call" | custom-call | tf_op jit(solution)/shard_map/second/pallas_call | solution.py:544
  31.4 0.0 copy-done.4
  31.4 4.2 %all-to-all-start.2 = ((bf16[16,48,128]{2,1,0:T(8,128)(2,1)}), bf16[16,48,128]{2,1,0:T(8,128)(2,1)S(1)}, u32[]{:S(2)}, u32[]{:S(2)}) async-start(bf16[16,48,128]{2,1,0:T(8,128)(2,1)} %get-tuple-element.39), calls=%async_computation.2 | async-start | bytes 393216 | tf_op jit(solution)/shard_map/all_to_all | solution.py:572
  35.6 0.0 copy-start.5
  35.6 1.8 %early.1 = (bf16[256,128]{1,0:T(8,128)(2,1)S(1)}, f32[416,128]{1,0:T(8,128)S(1)}, bf16[416,128]{1,0:T(8,128)(2,1)}, bf16[416,128]{1,0:T(8,128)(2,1)}, bf16[416,128]{1,0:T(8,128)(2,1)}) custom-call(s32[1]{0:T(128)} %bitcast.refs_0_, s32[1]{0:T(128)} %bitcast.1.refs_0_.refs_1_, bf16[1024,128]{1,0:T(8,128)(2,1)S(1)} %get-tuple-element.40.refs_0_.refs_2_, ...), custom_call_target="tpu_custom_call" | custom-call | tf_op jit(solution)/shard_map/early/pallas_call | solution.py:544
  37.3 0.4 collective-permute-start
  37.7 1.2 %collective-permute-start.1 = (bf16[416,128]{1,0:T(8,128)(2,1)}, bf16[416,128]{1,0:T(8,128)(2,1)}, u32[]{:S(2)}, u32[]{:S(2)}) collective-permute-start(bf16[416,128]{1,0:T(8,128)(2,1)} %get-tuple-element.53), channel_id=1, source_target_pairs={{0,16},{1,17},{2,18},{3,19},{4,20},{5,21},{6,22},{7,23},{8,24},{9,... | collective-permute-start | bytes 319496 | tf_op jit(solution)/shard_map/ppermute | solution.py:583
  38.9 0.6 collective-permute-start.2
  39.5 0.0 copy-done.5
  39.5 1.0 %again.1 = (f32[1024,128]{1,0:T(8,128)S(1)}, bf16[1280,384]{1,0:T(8,128)(2,1)S(1)}) custom-call(bf16[1600,128]{1,0:T(8,128)(2,1)S(1)} %copy-done.5, bf16[1152,128]{1,0:T(8,128)(2,1)S(1)} %copy-done), custom_call_target="tpu_custom_call" | custom-call | tf_op jit(solution)/shard_map/again/pallas_call | solution.py:544
  40.5 0.8 %inner.2.refs_4_ = f32[1024,128]{1,0:T(8,128)S(1)} custom-call(bf16[1024,128]{1,0:T(8,128)(2,1)S(1)} %get-tuple-element.40.refs_0_.refs_2_, bf16[1152,128]{1,0:T(8,128)(2,1)S(1)} %get-tuple-element.37.refs_4_.refs_1_), custom_call_target="tpu_custom_call" | custom-call | tf_op jit(solution)/shard_map/inner/pallas_call | solution.py:544
  41.4 0.4 all-to-all-done.2.refs_2_
  41.8 1.2 %slope.1 = (bf16[1024,128]{1,0:T(8,128)(2,1)S(1)}, f32[288,128]{1,0:T(8,128)S(1)}, bf16[288,128]{1,0:T(8,128)(2,1)S(1)}, bf16[288,128]{1,0:T(8,128)(2,1)S(1)}, bf16[288,128]{1,0:T(8,128)(2,1)S(1)}) custom-call(s32[1]{0:T(128)} %bitcast.refs_0_, s32[1]{0:T(128)} %bitcast.1.refs_0_.refs_1_, bf16[16,48,128]{2,1,0:T(8,128)(2,1)S(1)} %all-to-all-done.2.refs_2_, ...), custom_call_target="tpu_custom_call" | custom-call | tf_op jit(solution)/shard_map/slope/pallas_call | solution.py:544
  43.0 0.1 collective-permute-start.3
  43.1 1.2 %collective-permute-start.4 = (bf16[288,128]{1,0:T(8,128)(2,1)S(1)}, bf16[288,128]{1,0:T(8,128)(2,1)S(1)}, u32[]{:S(2)}, u32[]{:S(2)}) collective-permute-start(bf16[288,128]{1,0:T(8,128)(2,1)S(1)} %get-tuple-element.57), channel_id=1, source_target_pairs={{0,16},{1,17},{2,18},{3,19},{4,20},{5,21},{6,22},{7,23},{8,24},{9,... | collective-permute-start | bytes 221192 | tf_op jit(solution)/shard_map/ppermute | solution.py:583
  44.3 0.0 collective-permute-done.refs_1_
  44.3 0.9 %collective-permute-start.5 = (bf16[288,128]{1,0:T(8,128)(2,1)S(1)}, bf16[288,128]{1,0:T(8,128)(2,1)S(1)}, u32[]{:S(2)}, u32[]{:S(2)}) collective-permute-start(bf16[288,128]{1,0:T(8,128)(2,1)S(1)} %get-tuple-element.58), channel_id=1, source_target_pairs={{0,17},{1,16},{2,19},{3,18},{4,21},{5,20},{6,23},{7,22},{8,25},{9,... | collective-permute-start | bytes 221192 | tf_op jit(solution)/shard_map/ppermute | solution.py:583
  45.2 0.7 copy.17
  45.8 0.0 collective-permute-done.1.refs_2_
  45.9 0.0 collective-permute-done.2.refs_3_
  45.9 1.1 %gain.1.refs_1_ = f32[416,128]{1,0:T(8,128)S(1)} custom-call(f32[416,128]{1,0:T(8,128)S(1)} %get-tuple-element.51.refs_0_, bf16[416,128]{1,0:T(8,128)(2,1)} %collective-permute-done.refs_1_, bf16[416,128]{1,0:T(8,128)(2,1)} %collective-permute-done.1.refs_2_, bf16[416,128]{1,0:T(8,128)(2,1)} %collective-permute-done.2.refs_3_), custom_call_target="tpu_custom_call" | custom-call | tf_op jit(solution)/shard_map/gain/pallas_call | solution.py:544
  46.9 0.6 last.1.refs_0_
  47.6 0.8 %inner.3.refs_2_ = f32[1024,128]{1,0:T(8,128)S(1)} custom-call(bf16[1024,128]{1,0:T(8,128)(2,1)S(1)} %get-tuple-element.44.refs_0_, bf16[1152,128]{1,0:T(8,128)(2,1)S(1)} %get-tuple-element.45.refs_1_), custom_call_target="tpu_custom_call" | custom-call | tf_op jit(solution)/shard_map/inner/pallas_call | solution.py:544
  48.4 0.0 collective-permute-done.3.refs_3_
  48.4 0.0 collective-permute-done.4.refs_4_
  48.4 0.8 collective-permute-done.5.refs_5_
  49.2 0.1 join.1
  49.3 14.6 %all_to_all.26.refs_0_ = bf16[16,96,128]{2,1,0:T(8,128)(2,1)S(1)} all-to-all(bf16[16,96,128]{2,1,0:T(8,128)(2,1)S(1)} %join.1), channel_id=1, replica_groups={{9,7,8,12,5,4,0,13,10,15,6,2,11,3,1,14},{25,23,24,28,21,20,16,29,26,31,..., dimensions={0} | all-to-all | bytes 786432 | tf_op jit(solution)/shard_map/all_to_all | solution.py:572
  63.8 0.1 sum.1
  63.9 7.9 %all_to_all.27.refs_1_ = bf16[8,96,128]{2,1,0:T(8,128)(2,1)S(1)} all-to-all(bf16[8,96,128]{2,1,0:T(8,128)(2,1)S(1)} %sum.1), channel_id=1, replica_groups={{10,4,0,12,2,14,6,8},{11,5,1,13,3,15,7,9},{26,20,16,28,18,30,22,24},{27..., dimensions={0} | all-to-all | bytes 393216 | tf_op jit(solution)/shard_map/all_to_all | solution.py:572
  71.8 2.2 %collective-permute-start.6 = (bf16[8,96,128]{2,1,0:T(8,128)(2,1)S(1)}, bf16[8,96,128]{2,1,0:T(8,128)(2,1)S(1)}, u32[]{:S(2)}, u32[]{:S(2)}) collective-permute-start(bf16[8,96,128]{2,1,0:T(8,128)(2,1)S(1)} %all_to_all.27.refs_1_), channel_id=1, source_target_pairs={{0,1},{1,0},{2,3},{3,2},{4,5},{5,4},{6,7},{7,6},{8,9},{9,8},{10,11... | collective-permute-start | bytes 589832 | tf_op jit(solution)/shard_map/ppermute | solution.py:671
  74.1 1.4 %input.1 = f32[16,8,8,128]{3,2,1,0:T(8,128)} custom-call(bf16[16,96,128]{2,1,0:T(8,128)(2,1)S(1)} %all_to_all.26.refs_0_, s32[24,768]{1,0:T(8,128)S(1)} %get-tuple-element.34.refs_1_.refs_3_.refs_2_, f32[1024,128]{1,0:T(8,128)S(1)} %inner.3.refs_2_), custom_call_target="tpu_custom_call" | custom-call | tf_op jit(solution)/shard_map/input/pallas_call | solution.py:544
  75.5 0.0 collective-permute-done.6.refs_2_
  75.5 0.9 %spread.1 = (f32[576,128]{1,0:T(8,128)}, f32[576,128]{1,0:T(8,128)}, f32[256,128]{1,0:T(8,128)}) custom-call(s32[1]{0:T(128)} %bitcast.1.refs_0_.refs_1_, bf16[8,96,128]{2,1,0:T(8,128)(2,1)S(1)} %all_to_all.27.refs_1_, bf16[8,96,128]{2,1,0:T(8,128)(2,1)S(1)} %collective-permute-done.6.refs_2_), custom_call_target="tpu_custom_call" | custom-call | tf_op jit(solution)/shard_map/spread/pallas_call | solution.py:544
  (1 shorter events, 0.0 us)
Async XLA Ops:
  0.6 9.8 %copy-start.1 = (bf16[1152,128]{1,0:T(8,128)(2,1)S(1)}, bf16[1152,128]{1,0:T(8,128)(2,1)}, u32[]{:S(2)}) copy-start(bf16[1152,128]{1,0:T(8,128)(2,1)} %refs_3_.3) | copy-start | bytes 884740
  2.9 7.5 %copy-start.10 = (bf16[1,16,4,4,128]{4,3,2,1,0:T(4,128)(2,1)S(1)}, bf16[1,16,4,4,128]{4,3,2,1,0:T(4,128)(2,1)}, u32[]{:S(2)}) copy-start(bf16[1,16,4,4,128]{4,3,2,1,0:T(4,128)(2,1)} %param.10) | copy-start | bytes 196612
  2.9 7.5 %copy-start = (bf16[1152,128]{1,0:T(8,128)(2,1)S(1)}, bf16[1152,128]{1,0:T(8,128)(2,1)}, u32[]{:S(2)}) copy-start(bf16[1152,128]{1,0:T(8,128)(2,1)} %refs_1_.1) | copy-start | bytes 884740
  2.9 7.5 %copy-start.6 = (s32[256,8]{0,1:T(8,128)S(1)}, s32[256,8]{0,1:T(8,128)}, u32[]{:S(2)}) copy-start(s32[256,8]{0,1:T(8,128)} %param.16) | copy-start | bytes 24580
  3.0 7.5 %copy-start.7 = (s32[256,8]{0,1:T(8,128)S(1)}, s32[256,8]{0,1:T(8,128)}, u32[]{:S(2)}) copy-start(s32[256,8]{0,1:T(8,128)} %param.17) | copy-start | bytes 24580
  3.0 7.5 %copy-start.8 = (s32[256,4]{0,1:T(4,128)S(1)}, s32[256,4]{0,1:T(4,128)}, u32[]{:S(2)}) copy-start(s32[256,4]{0,1:T(4,128)} %param.14) | copy-start | bytes 12292
  3.0 7.5 %copy-start.9 = (s32[256,4]{0,1:T(4,128)S(1)}, s32[256,4]{0,1:T(4,128)}, u32[]{:S(2)}) copy-start(s32[256,4]{0,1:T(4,128)} %param.15) | copy-start | bytes 12292
  3.0 13.7 %all-to-all-start = ((bf16[16,48,128]{2,1,0:T(8,128)(2,1)}), bf16[16,48,128]{2,1,0:T(8,128)(2,1)S(1)}, u32[]{:S(2)}, u32[]{:S(2)}) async-start(bf16[16,48,128]{2,1,0:T(8,128)(2,1)} %pack.1), calls=%async_computation | async-start | bytes 393216 | tf_op jit(solution)/shard_map/all_to_all | solution.py:572
  10.4 0.9 %copy-start.3 = (bf16[512,128]{1,0:T(8,128)(2,1)S(1)}, bf16[512,128]{1,0:T(8,128)(2,1)}, u32[]{:S(2)}) copy-start(bf16[512,128]{1,0:T(8,128)(2,1)} %refs_5_.1) | copy-start | bytes 393220
  11.3 5.3 %copy-start.2 = (bf16[1,16,8,8,128]{4,3,2,1,0:T(8,128)(2,1)S(1)}, bf16[1,16,8,8,128]{4,3,2,1,0:T(8,128)(2,1)}, u32[]{:S(2)}) copy-start(bf16[1,16,8,8,128]{4,3,2,1,0:T(8,128)(2,1)} %param.9) | copy-start | bytes 786436
  18.5 12.8 %copy-start.4 = (bf16[1600,128]{1,0:T(8,128)(2,1)}, bf16[1600,128]{1,0:T(8,128)(2,1)S(1)}, u32[]{:S(2)}) copy-start(bf16[1600,128]{1,0:T(8,128)(2,1)S(1)} %get-tuple-element.41.refs_0_) | copy-start | bytes 1228804
  31.4 10.4 %all-to-all-start.2 = ((bf16[16,48,128]{2,1,0:T(8,128)(2,1)}), bf16[16,48,128]{2,1,0:T(8,128)(2,1)S(1)}, u32[]{:S(2)}, u32[]{:S(2)}) async-start(bf16[16,48,128]{2,1,0:T(8,128)(2,1)} %get-tuple-element.39), calls=%async_computation.2 | async-start | bytes 393216 | tf_op jit(solution)/shard_map/all_to_all | solution.py:572
  35.6 4.0 %copy-start.5 = (bf16[1600,128]{1,0:T(8,128)(2,1)S(1)}, bf16[1600,128]{1,0:T(8,128)(2,1)}, u32[]{:S(2)}) copy-start(bf16[1600,128]{1,0:T(8,128)(2,1)} %copy-done.4) | copy-start | bytes 1228804
  37.3 7.0 %collective-permute-start = (bf16[416,128]{1,0:T(8,128)(2,1)}, bf16[416,128]{1,0:T(8,128)(2,1)}, u32[]{:S(2)}, u32[]{:S(2)}) collective-permute-start(bf16[416,128]{1,0:T(8,128)(2,1)} %get-tuple-element.52), channel_id=1, source_target_pairs={{0,1},{1,0},{2,3},{3,2},{4,5},{5,4},{6,7},{7,6},{8,9},{9,8},{10,11... | collective-permute-start | bytes 319496 | tf_op jit(solution)/shard_map/ppermute | solution.py:583
  37.7 8.1 %collective-permute-start.1 = (bf16[416,128]{1,0:T(8,128)(2,1)}, bf16[416,128]{1,0:T(8,128)(2,1)}, u32[]{:S(2)}, u32[]{:S(2)}) collective-permute-start(bf16[416,128]{1,0:T(8,128)(2,1)} %get-tuple-element.53), channel_id=1, source_target_pairs={{0,16},{1,17},{2,18},{3,19},{4,20},{5,21},{6,22},{7,23},{8,24},{9,... | collective-permute-start | bytes 319496 | tf_op jit(solution)/shard_map/ppermute | solution.py:583
  38.9 6.9 %collective-permute-start.2 = (bf16[416,128]{1,0:T(8,128)(2,1)}, bf16[416,128]{1,0:T(8,128)(2,1)}, u32[]{:S(2)}, u32[]{:S(2)}) collective-permute-start(bf16[416,128]{1,0:T(8,128)(2,1)} %get-tuple-element.54), channel_id=1, source_target_pairs={{0,17},{1,16},{2,19},{3,18},{4,21},{5,20},{6,23},{7,22},{8,25},{9,... | collective-permute-start | bytes 319496 | tf_op jit(solution)/shard_map/ppermute | solution.py:583
  43.0 5.4 %collective-permute-start.3 = (bf16[288,128]{1,0:T(8,128)(2,1)S(1)}, bf16[288,128]{1,0:T(8,128)(2,1)S(1)}, u32[]{:S(2)}, u32[]{:S(2)}) collective-permute-start(bf16[288,128]{1,0:T(8,128)(2,1)S(1)} %get-tuple-element.56), channel_id=1, source_target_pairs={{0,1},{1,0},{2,3},{3,2},{4,5},{5,4},{6,7},{7,6},{8,9},{9,8},{10,11... | collective-permute-start | bytes 221192 | tf_op jit(solution)/shard_map/ppermute | solution.py:583
  43.1 5.3 %collective-permute-start.4 = (bf16[288,128]{1,0:T(8,128)(2,1)S(1)}, bf16[288,128]{1,0:T(8,128)(2,1)S(1)}, u32[]{:S(2)}, u32[]{:S(2)}) collective-permute-start(bf16[288,128]{1,0:T(8,128)(2,1)S(1)} %get-tuple-element.57), channel_id=1, source_target_pairs={{0,16},{1,17},{2,18},{3,19},{4,20},{5,21},{6,22},{7,23},{8,24},{9,... | collective-permute-start | bytes 221192 | tf_op jit(solution)/shard_map/ppermute | solution.py:583
  44.3 4.8 %collective-permute-start.5 = (bf16[288,128]{1,0:T(8,128)(2,1)S(1)}, bf16[288,128]{1,0:T(8,128)(2,1)S(1)}, u32[]{:S(2)}, u32[]{:S(2)}) collective-permute-start(bf16[288,128]{1,0:T(8,128)(2,1)S(1)} %get-tuple-element.58), channel_id=1, source_target_pairs={{0,17},{1,16},{2,19},{3,18},{4,21},{5,20},{6,23},{7,22},{8,25},{9,... | collective-permute-start | bytes 221192 | tf_op jit(solution)/shard_map/ppermute | solution.py:583
  71.8 3.6 %collective-permute-start.6 = (bf16[8,96,128]{2,1,0:T(8,128)(2,1)S(1)}, bf16[8,96,128]{2,1,0:T(8,128)(2,1)S(1)}, u32[]{:S(2)}, u32[]{:S(2)}) collective-permute-start(bf16[8,96,128]{2,1,0:T(8,128)(2,1)S(1)} %all_to_all.27.refs_1_), channel_id=1, source_target_pairs={{0,1},{1,0},{2,3},{3,2},{4,5},{5,4},{6,7},{7,6},{8,9},{9,8},{10,11... | collective-permute-start | bytes 589832 | tf_op jit(solution)/shard_map/ppermute | solution.py:671
